TPU v7x, 256 devices: a whole 4x4x8 slice. The times are simulated.
256 devices in a mesh: lat: 16 (over z_lo, x, core), src: 16 (over y, z_hi).
Axes of the slice: x: 4, y: 4, z: 8 (z_hi: 4, z_lo: 2; z = z_hi * 2 + z_lo), core: 2. Of those that a mesh axis runs over, the one named last changes fastest.
Arguments:
- fine_residual: bfloat16 [32, 32, 256, 2048], P('lat', 'src'), may hold values from -6 to 6
- basis: bfloat16 [32, 32, 2048, 128], P('lat', 'src'), may hold values from -0.25 to 0.25
- diag_inverse: bfloat16 [32, 32, 128, 128], P('lat', 'src'), may hold values from -0.32 to 1.7, as said below
- hoppings: bfloat16 [32, 32, 8, 128, 128], P('lat', 'src'), may hold values from -0.125 to 0.125
- neighbours: int32 [32, 6], replicated, may hold values from 0 to 31, as said below
- aggregation: int32 [32, 32], P('lat', 'src'), may hold values from 0 to 31, as said below
Outputs:
- correction: bfloat16 [32, 32, 256, 2048], P('lat', 'src')
Inputs may be any that keep to these rules, and one draw needn't show every extreme that they name: `diag_inverse`: a site's diagonal inverse is one on the diagonal within a fifth (two fifths in some draws) plus independent off-diagonal entries. The spatial sites form a periodic grid of 16 by 1 by 2 sites, site (x, y, z) having index (x * 1 + y) * 2 + z; columns 2k and 2k+1 hold the two periodic neighbours along grid direction k, one step up and one step down, in an order drawn for each k. `aggregation`: in each row, every aligned block of 2 entries is a permutation of that block's own column indices.
All inputs are finite; a program needn't handle non-finite values.
Results may differ from a plain program's by a relative error of at most 0.0075.
Values may be sent and summed in bfloat16 or wider, within the bound.
No kernel may reach another device: no remote copies, remote signals or barrier semaphores. Data moves between devices by JAX's collectives and lax.ppermute only.
A program may use at most 128 MiB of HBM per device.

v0:
```python
import jax
import jax.numpy as jnp
from jax import lax
from jax.sharding import PartitionSpec as P

SWEEPS = 3


damping = 0.8


def with_halo(cells, sides, width):
    for axis, dim in sides:
        count = lax.axis_size(axis)
        head = lax.slice_in_dim(cells, 0, width, axis=dim)
        tail = lax.slice_in_dim(cells, cells.shape[dim] - width, cells.shape[dim], axis=dim)
        cells = jnp.concatenate(
            [
                lax.ppermute(tail, axis, [(i, (i + 1) % count) for i in range(count)]),
                cells,
                lax.ppermute(head, axis, [((i + 1) % count, i) for i in range(count)]),
            ],
            axis=dim,
        )
    return cells


def hop_terms(source, neighbour_rows, padded, hops):
    spatial = jnp.take(source, neighbour_rows, axis=1)
    upper_time = padded[2:][:, :, None]
    lower_time = padded[:-2][:, :, None]
    stacked = jnp.concatenate([spatial, upper_time, lower_time], axis=2)
    return jnp.einsum("tsknc,tskcd->tsnd", stacked, hops, preferred_element_type=jnp.float32)


def first_sweep(coarse_rhs, inverse_blocks):
    applied = jnp.einsum(
        "tsnc,tscd->tsnd", coarse_rhs, inverse_blocks, preferred_element_type=jnp.float32
    )
    return (damping * applied).astype(jnp.bfloat16)


def later_sweep(coarse_rhs, iterate, hop_sum, inverse_blocks):
    difference = (coarse_rhs.astype(jnp.float32) - hop_sum).astype(jnp.bfloat16)
    applied = jnp.einsum(
        "tsnc,tscd->tsnd", difference, inverse_blocks, preferred_element_type=jnp.float32
    )
    return ((1.0 - damping) * iterate.astype(jnp.float32) + damping * applied).astype(jnp.bfloat16)


def body(fine_residual, basis, diag_inverse, hoppings, neighbours, aggregation):
    slab_width = basis.shape[1]
    restricted = jnp.einsum(
        "tsnr,tsrc->tsnc", fine_residual, basis, preferred_element_type=jnp.float32
    ).astype(jnp.bfloat16)
    within = aggregation - lax.axis_index("src") * slab_width
    inverse = jnp.argsort(within, axis=1)
    coarse_rhs = jnp.take_along_axis(restricted, inverse[:, :, None, None], axis=1)
    operator_inverse, operator_hops = (
        lax.all_gather(diag_inverse, "src", axis=1, tiled=True),
        lax.all_gather(hoppings, "src", axis=1, tiled=True),
    )
    source_rhs = lax.all_to_all(coarse_rhs, "src", split_axis=2, concat_axis=1, tiled=True)
    iterate = first_sweep(source_rhs, operator_inverse)
    for sweep_index in range(SWEEPS - 1):
        padded = with_halo(iterate, (("lat", 0),), 1)
        hop_sum = hop_terms(iterate, neighbours, padded, operator_hops)
        iterate = later_sweep(source_rhs, iterate, hop_sum, operator_inverse)
    solved = lax.all_to_all(iterate, "src", split_axis=1, concat_axis=2, tiled=True)
    gathered = jnp.take_along_axis(solved, within[:, :, None, None], axis=1)
    return jnp.einsum(
        "tsnc,tsrc->tsnr", gathered, basis, preferred_element_type=jnp.float32
    ).astype(jnp.bfloat16)


def solution(mesh):
    return jax.shard_map(
        body,
        mesh=mesh,
        in_specs=(
            P("lat", "src", None, None),
            P("lat", "src", None, None),
            P("lat", "src", None, None),
            P("lat", "src", None, None, None),
            P(),
            P("lat", "src"),
        ),
        out_specs=P("lat", "src", None, None),
        check_vma=False,
    )
```

profile of v0, /device:TPU:32, one launch (start us, length us, event | category | flops | bytes accessed | tf_op | source)
XLA Modules:
  0.0 339.0 jit_solution(17021212386013432402)
XLA Ops:
  6.5 0.0 copy-start
  6.5 0.0 all-gather.3.cloned.1.call-start
  6.5 0.7 all-gather.3.cloned.1.call-update
  7.3 0.0 all-gather.5.cloned.1.call-start
  7.3 0.7 all-gather.5.cloned.1.call-update
  8.0 0.8 copy.43
  8.8 0.6 sort.17
  9.4 0.1 copy.45
  9.5 0.1 reshape.67
  9.6 0.0 copy-done
  9.6 0.0 copy-start.1
  9.6 3.4 %convolution_convert_fusion.1 = bf16[2,2,256,128]{3,2,1,0:T(8,128)(2,1)S(1)} fusion(bf16[2,2,256,2048]{3,2,1,0:T(8,128)(2,1)} %param.10, bf16[2,2,2048,128]{3,2,1,0:T(8,128)(2,1)S(1)} %copy-done), kind=kOutput, calls=%fused_computation.34 | convolution fusion | flops 537001984 | bytes 6553600 | tf_op jit(solution)/shard_map/tsnr,tsrc->tsnc/dot_general | solution.py:53
  13.0 0.6 gather_fusion
  13.6 1.0 broadcast_select_fusion
  14.7 10.3 %all-to-all-start = ((bf16[2,2,256,128]{3,1,0,2:T(2,128)(2,1)}), bf16[2,2,256,128]{3,1,0,2:T(2,128)(2,1)S(1)}, u32[]{:S(2)}, u32[]{:S(2)}) async-start(bf16[2,2,256,128]{3,1,0,2:T(2,128)(2,1)} %broadcast_select_fusion), calls=%async_computation | async-start | bytes 524288 | tf_op jit(solution)/shard_map/all_to_all | solution.py:63
  25.0 0.0 copy-done.1
  25.0 0.1 copy.49
  25.1 0.1 reshape.71
  25.2 0.1 copy.48
  25.3 13.8 %all-to-all-done = bf16[2,2,256,128]{3,1,0,2:T(2,128)(2,1)S(1)} async-done(((bf16[2,2,256,128]{3,1,0,2:T(2,128)(2,1)}), bf16[2,2,256,128]{3,1,0,2:T(2,128)(2,1)S(1)}, u32[]{:S(2)}, u32[]{:S(2)}) %all-to-all-start) | async-done | bytes 262176 | tf_op jit(solution)/shard_map/all_to_all | solution.py:63
  39.2 35.3 %all-gather.3.cloned.1.call-done = bf16[2,32,128,128]{3,2,1,0:T(8,128)(2,1)} async-done(((bf16[2,2,128,128]{3,2,1,0:T(8,128)(2,1)}), bf16[2,32,128,128]{3,2,1,0:T(8,128)(2,1)}) %all-gather.3.cloned.1.call-update) | async-done | bytes 2097168 | tf_op jit(solution)/shard_map/all_gather | solution.py:60
  74.5 2.2 fusion.36
  76.7 3.0 collective-permute-start
  79.7 0.0 collective-permute-start.1
  79.7 2.0 gather_fusion.1
  81.7 2.8 fusion.13
  84.6 0.0 collective-permute-done
  84.6 1.7 collective-permute-done.1
  86.3 1.0 fusion.46
  87.3 189.4 %all-gather.5.cloned.1.call-done = bf16[2,32,8,128,128]{4,3,2,1,0:T(8,128)(2,1)} async-done(((bf16[2,2,8,128,128]{4,3,2,1,0:T(8,128)(2,1)}), bf16[2,32,8,128,128]{4,3,2,1,0:T(8,128)(2,1)}) %all-gather.5.cloned.1.call-update) | async-done | bytes 16777232 | tf_op jit(solution)/shard_map/all_gather | solution.py:61
  276.7 10.0 %fusion.34 = bf16[2,32,16,128]{3,2,1,0:T(8,128)(2,1)S(1)} fusion(bf16[2,32,128,128]{3,2,1,0:T(8,128)(2,1)} %all-gather.3.cloned.1.call-done, bf16[2,32,8,128,128]{4,3,2,1,0:T(8,128)(2,1)} %all-gather.5.cloned.1.call-done, bf16[2,32,1,16,128]{4,3,2,1,0:T(8,128)(2,1)S(1)} %get-tuple-element.14, bf16[2,32,1,16,128]{4,3,2,1,0:T(8,128)(2,1)S(1)} %get-tuple-element.13, ...), kind=kOutput, calls=%fused_computation.32 | convolution fusion | flops 305135616 | bytes 21757952 | tf_op jit(solution)/shard_map/tsnc,tscd->tsnd/dot_general | solution.py:45
  286.7 2.0 gather_fusion.2
  288.8 0.1 collective-permute-start.2
  288.9 0.5 collective-permute-start.3
  289.4 2.8 fusion.12
  292.2 0.0 collective-permute-done.2
  292.2 3.4 %collective-permute-done.3 = bf16[1,32,16,128]{3,2,1,0:T(8,128)(2,1)S(1)} collective-permute-done((bf16[1,32,16,128]{3,2,1,0:T(8,128)(2,1)S(1)}, bf16[1,32,16,128]{3,2,1,0:T(8,128)(2,1)S(1)}, u32[]{:S(2)}, u32[]{:S(2)}) %collective-permute-start.3) | collective-permute-done | bytes 131104 | tf_op jit(solution)/shard_map/ppermute | solution.py:19
  295.7 10.0 %fusion.35 = bf16[2,32,16,128]{3,2,1,0:T(8,128)(2,1)S(1)} fusion(bf16[2,32,128,128]{3,2,1,0:T(8,128)(2,1)} %all-gather.3.cloned.1.call-done, bf16[2,32,8,128,128]{4,3,2,1,0:T(8,128)(2,1)} %all-gather.5.cloned.1.call-done, bf16[2,32,1,16,128]{4,3,2,1,0:T(8,128)(2,1)S(1)} %get-tuple-element.10, bf16[2,32,1,16,128]{4,3,2,1,0:T(8,128)(2,1)S(1)} %get-tuple-element.9, ...), kind=kOutput, calls=%fused_computation.33 | convolution fusion | flops 305135616 | bytes 21757952 | tf_op jit(solution)/shard_map/tsnc,tscd->tsnd/dot_general | solution.py:45
  305.7 0.7 copy.58
  306.4 10.0 %all-to-all-start.1 = ((bf16[2,32,16,128]{3,2,0,1:T(8,128)(2,1)}), bf16[2,32,16,128]{3,2,0,1:T(8,128)(2,1)S(1)}, u32[]{:S(2)}, u32[]{:S(2)}) async-start(bf16[2,32,16,128]{3,2,0,1:T(8,128)(2,1)} %copy.58), calls=%async_computation.1 | async-start | bytes 524288 | tf_op jit(solution)/shard_map/all_to_all | solution.py:69
  316.4 0.1 copy.44
  316.5 0.1 reshape.80
  316.6 11.6 %all-to-all-done.1 = bf16[2,32,16,128]{3,2,0,1:T(8,128)(2,1)S(1)} async-done(((bf16[2,32,16,128]{3,2,0,1:T(8,128)(2,1)}), bf16[2,32,16,128]{3,2,0,1:T(8,128)(2,1)S(1)}, u32[]{:S(2)}, u32[]{:S(2)}) %all-to-all-start.1) | async-done | bytes 262176 | tf_op jit(solution)/shard_map/all_to_all | solution.py:69
  328.2 0.6 gather_fusion.3
  328.8 3.3 convolution_convert_fusion
  (14 shorter events, 0.2 us)
Async XLA Ops:
  6.5 3.0 copy-start
  6.5 67.9 %all-gather.3.cloned.1.call-start = ((), (), s32[]{:S(2)}) async-start(), calls=%async_computation.2 | async-start | bytes 2228224 | tf_op jit(solution)/shard_map/all_gather | solution.py:60
  7.3 269.4 %all-gather.5.cloned.1.call-start = ((), (), s32[]{:S(2)}) async-start(), calls=%async_computation.3 | async-start | bytes 17825792 | tf_op jit(solution)/shard_map/all_gather | solution.py:61
  9.6 15.4 %copy-start.1 = (s32[32,6]{0,1:T(8,128)S(1)}, s32[32,6]{0,1:T(8,128)}, u32[]{:S(2)}) copy-start(s32[32,6]{0,1:T(8,128)} %param.14) | copy-start | bytes 2308
  14.7 24.4 %all-to-all-start = ((bf16[2,2,256,128]{3,1,0,2:T(2,128)(2,1)}), bf16[2,2,256,128]{3,1,0,2:T(2,128)(2,1)S(1)}, u32[]{:S(2)}, u32[]{:S(2)}) async-start(bf16[2,2,256,128]{3,1,0,2:T(2,128)(2,1)} %broadcast_select_fusion), calls=%async_computation | async-start | bytes 524288 | tf_op jit(solution)/shard_map/all_to_all | solution.py:63
  76.7 7.9 %collective-permute-start = (bf16[1,32,16,128]{3,2,1,0:T(8,128)(2,1)S(1)}, bf16[1,32,16,128]{3,2,1,0:T(8,128)(2,1)S(1)}, u32[]{:S(2)}, u32[]{:S(2)}) collective-permute-start(bf16[1,32,16,128]{3,2,1,0:T(8,128)(2,1)S(1)} %get-tuple-element.15), channel_id=1, source_target_pairs={{16,0},{32,16},{48,32},{64,48},{80,64},{96,80},{112,96},{128,112},... | collective-permute-start | bytes 393224 | tf_op jit(solution)/shard_map/ppermute | solution.py:21
  79.7 6.6 %collective-permute-start.1 = (bf16[1,32,16,128]{3,2,1,0:T(8,128)(2,1)S(1)}, bf16[1,32,16,128]{3,2,1,0:T(8,128)(2,1)}, u32[]{:S(2)}, u32[]{:S(2)}) collective-permute-start(bf16[1,32,16,128]{3,2,1,0:T(8,128)(2,1)S(1)} %get-tuple-element.16), channel_id=1, source_target_pairs={{0,16},{16,32},{32,48},{48,64},{64,80},{80,96},{96,112},{112,128},... | collective-permute-start | bytes 393224 | tf_op jit(solution)/shard_map/ppermute | solution.py:19
  288.8 3.4 %collective-permute-start.2 = (bf16[1,32,16,128]{3,2,1,0:T(8,128)(2,1)S(1)}, bf16[1,32,16,128]{3,2,1,0:T(8,128)(2,1)S(1)}, u32[]{:S(2)}, u32[]{:S(2)}) collective-permute-start(bf16[1,32,16,128]{3,2,1,0:T(8,128)(2,1)S(1)} %get-tuple-element.11), channel_id=1, source_target_pairs={{16,0},{32,16},{48,32},{64,48},{80,64},{96,80},{112,96},{128,112},... | collective-permute-start | bytes 393224 | tf_op jit(solution)/shard_map/ppermute | solution.py:21
  288.9 6.8 %collective-permute-start.3 = (bf16[1,32,16,128]{3,2,1,0:T(8,128)(2,1)S(1)}, bf16[1,32,16,128]{3,2,1,0:T(8,128)(2,1)S(1)}, u32[]{:S(2)}, u32[]{:S(2)}) collective-permute-start(bf16[1,32,16,128]{3,2,1,0:T(8,128)(2,1)S(1)} %get-tuple-element.12), channel_id=1, source_target_pairs={{0,16},{16,32},{32,48},{48,64},{64,80},{80,96},{96,112},{112,128},... | collective-permute-start | bytes 393224 | tf_op jit(solution)/shard_map/ppermute | solution.py:19
  306.4 21.8 %all-to-all-start.1 = ((bf16[2,32,16,128]{3,2,0,1:T(8,128)(2,1)}), bf16[2,32,16,128]{3,2,0,1:T(8,128)(2,1)S(1)}, u32[]{:S(2)}, u32[]{:S(2)}) async-start(bf16[2,32,16,128]{3,2,0,1:T(8,128)(2,1)} %copy.58), calls=%async_computation.1 | async-start | bytes 524288 | tf_op jit(solution)/shard_map/all_to_all | solution.py:69
Sparse Core Ops, SparseCore 0:
  9.8 64.5 all-gather.2
  76.9 199.7 all-gather.4
where the time goes:
time: 339 us
  waiting for transfers between devices  257 us (76%)
  matrix products  29 us (9%)
  starting transfers between devices  23.9 us (7%)
  between operations  13.5 us (4%)
  other arithmetic  8.38 us (2%)
  local copies, waits for them, and re-layouts  7.54 us (2%)
    all_gather x1, waiting for transfers between devices, body(): lax.all_gather(hoppings, 'src', axis=1, tiled=True)  189 us
    all_gather x1, waiting for transfers between devices, body(): lax.all_gather(diag_inverse, 'src', axis=1, tiled=True)  35.3 us
    dot_general x2, matrix products, later_sweep(): jnp.einsum('tsnc,tscd->tsnd', difference, inverse_blocks, preferred_eleme...  20 us
    all_to_all x1, waiting for transfers between devices, body(): lax.all_to_all(coarse_rhs, 'src', split_axis=2, concat_axis=1, tiled=True)  13.8 us
    all_to_all x1, waiting for transfers between devices, body(): lax.all_to_all(iterate, 'src', split_axis=1, concat_axis=2, tiled=True)  11.6 us
    all_to_all x1, starting transfers between devices, body(): lax.all_to_all(coarse_rhs, 'src', split_axis=2, concat_axis=1, tiled=True)  10.3 us
    all_to_all x1, starting transfers between devices, body(): lax.all_to_all(iterate, 'src', split_axis=1, concat_axis=2, tiled=True)  9.99 us
  transfers between devices with their start and end apart: 8, of which 6 were waited for; matrix products, arithmetic and copies ran while one was open for 5% of the time, Pallas kernels for 0%

commit v1 on v0

v1 whole, which is shorter than its diff:
```python
import jax
import jax.numpy as jnp
from jax import lax
from jax.experimental import pallas as pl
from jax.experimental.pallas import tpu as pltpu
from jax.sharding import PartitionSpec as P

CHUNKS = 2
DAMPING = 0.8
KEEP = 1.0 - DAMPING
BF16 = jnp.bfloat16
F32 = jnp.float32


def dot(a, b):
    return jnp.dot(a, b, preferred_element_type=F32)


def params():
    return pltpu.CompilerParams(
        dimension_semantics=("arbitrary", "arbitrary"), vmem_limit_bytes=24 * 1024 * 1024
    )


def full(shape):
    return pl.BlockSpec(shape, lambda *_: (0,) * len(shape))


def put_iterate(t, c, value, whole, first, last):
    whole[t, c] = value

    @pl.when(t == 0)
    def _():
        first[c] = value

    @pl.when(t == whole.shape[0] - 1)
    def _():
        last[c] = value


def restrict_kernel(agg, fine, basis, dinv, rhs, e, first, last):
    t, s = pl.program_id(0), pl.program_id(1)
    c = agg[t, s] & 1
    r = dot(fine[0, 0], basis[0, 0]).astype(BF16)
    rhs[t, c] = r
    put_iterate(t, c, (DAMPING * dot(r, dinv[0, 0])).astype(BF16), e, first, last)


def restrict(j, n, agg, fine, basis, dinv):
    nt, ns, _, nf = fine.shape
    nc = basis.shape[3]
    whole = (nt, ns, n, nc)
    edge = (ns, n, nc)
    return pl.pallas_call(
        restrict_kernel,
        grid_spec=pltpu.PrefetchScalarGridSpec(
            num_scalar_prefetch=1,
            grid=(nt, ns),
            in_specs=[
                pl.BlockSpec((1, 1, n, nf), lambda t, s, a: (t, s, j, 0)),
                pl.BlockSpec((1, 1, nf, nc), lambda t, s, a: (t, s, 0, 0)),
                pl.BlockSpec((1, 1, nc, nc), lambda t, s, a: (t, a[t, s] & 1, 0, 0)),
            ],
            out_specs=[full(whole), full(whole), full(edge), full(edge)],
        ),
        out_shape=[
            jax.ShapeDtypeStruct(whole, BF16),
            jax.ShapeDtypeStruct(whole, BF16),
            jax.ShapeDtypeStruct(edge, BF16),
            jax.ShapeDtypeStruct(edge, BF16),
        ],
        compiler_params=params(),
        cost_estimate=pl.CostEstimate(
            flops=2 * nt * ns * n * nc * (nf + nc),
            bytes_accessed=2 * nt * ns * (n * nf + nf * nc),
            transcendentals=0,
        ),
        name="restrict",
    )(agg, fine, basis, dinv)


def next_iterate(agg, nbr, t, c, rhs, e, up, dn, lup, ldn, hops, dinv):
    nt = e.shape[0]
    site = (agg[0, 0] & -2) + c
    upward = nbr[site, 0] == (site + 2) % nbr.shape[0]
    own, other = e[t, c], e[t, 1 - c]
    above, below = up[0, 0], dn[0, 0]
    later = jnp.where(t == nt - 1, lup[c], e[jnp.minimum(t + 1, nt - 1), c])
    earlier = jnp.where(t == 0, ldn[c], e[jnp.maximum(t - 1, 0), c])
    stacked = jnp.concatenate(
        [
            jnp.where(upward, above, below),
            jnp.where(upward, below, above),
            own,
            own,
            other,
            other,
            later,
            earlier,
        ],
        axis=1,
    )
    nc = own.shape[1]
    hop = dot(stacked, hops[0, 0].reshape(8 * nc, nc))
    difference = (rhs[0, 0].astype(F32) - hop).astype(BF16)
    return (KEEP * own.astype(F32) + DAMPING * dot(difference, dinv[0, 0])).astype(BF16)


def sweep_kernel(agg, nbr, rhs, e, up, dn, lup, ldn, hops, dinv, out, first, last):
    t, c = pl.program_id(0), pl.program_id(1)
    value = next_iterate(agg, nbr, t, c, rhs, e, up, dn, lup, ldn, hops, dinv)
    put_iterate(t, c, value, out, first, last)


def sweep(agg, nbr, rhs, e, halo, hops, dinv):
    nt, ns, n, nc = e.shape
    edge = (ns, n, nc)
    block = pl.BlockSpec((1, 1, n, nc), lambda t, c, a, b: (t, c, 0, 0))
    return pl.pallas_call(
        sweep_kernel,
        grid_spec=pltpu.PrefetchScalarGridSpec(
            num_scalar_prefetch=2,
            grid=(nt, ns),
            in_specs=[
                block,
                full(e.shape),
                block,
                block,
                full(edge),
                full(edge),
                pl.BlockSpec((1, 1, 8, nc, nc), lambda t, c, a, b: (t, c, 0, 0, 0)),
                pl.BlockSpec((1, 1, nc, nc), lambda t, c, a, b: (t, c, 0, 0)),
            ],
            out_specs=[full(e.shape), full(edge), full(edge)],
        ),
        out_shape=[
            jax.ShapeDtypeStruct(e.shape, BF16),
            jax.ShapeDtypeStruct(edge, BF16),
            jax.ShapeDtypeStruct(edge, BF16),
        ],
        compiler_params=params(),
        cost_estimate=pl.CostEstimate(
            flops=2 * nt * ns * n * nc * 9 * nc,
            bytes_accessed=2 * nt * ns * (9 * nc * nc + 5 * n * nc),
            transcendentals=0,
        ),
        name="sweep",
    )(agg, nbr, rhs, e, *halo, hops, dinv)


def prolong_kernel(agg, nbr, rhs, e, up, dn, lup, ldn, hops, dinv, basis, *rest):
    out = rest[-1]
    t, s = pl.program_id(0), pl.program_id(1)
    c = agg[t, s] & 1
    value = next_iterate(agg, nbr, t, c, rhs, e, up, dn, lup, ldn, hops, dinv)
    out[0, 0] = lax.dot_general(
        value, basis[0, 0], (((1,), (1,)), ((), ())), preferred_element_type=F32
    ).astype(BF16)


def prolong(j, shape, agg, nbr, rhs, e, halo, hops, dinv, basis, previous):
    nt, ns, n, nc = e.shape
    nf = basis.shape[2]
    edge = (ns, n, nc)
    at_site = lambda t, s, a, b: (t, a[t, s] & 1, 0, 0)
    block = pl.BlockSpec((1, 1, n, nc), at_site)
    in_specs = [
        block,
        full(e.shape),
        block,
        block,
        full(edge),
        full(edge),
        pl.BlockSpec((1, 1, 8, nc, nc), lambda t, s, a, b: (t, a[t, s] & 1, 0, 0, 0)),
        pl.BlockSpec((1, 1, nc, nc), at_site),
        pl.BlockSpec((1, 1, nf, nc), lambda t, s, a, b: (t, s, 0, 0)),
    ]
    operands = [agg, nbr, rhs, e, *halo, hops, dinv, basis]
    aliases = {}
    if previous is not None:
        aliases = {len(operands): 0}
        in_specs.append(pl.BlockSpec(memory_space=pl.ANY))
        operands.append(previous)
    return pl.pallas_call(
        prolong_kernel,
        grid_spec=pltpu.PrefetchScalarGridSpec(
            num_scalar_prefetch=2,
            grid=(nt, ns),
            in_specs=in_specs,
            out_specs=pl.BlockSpec((1, 1, n, nf), lambda t, s, a, b: (t, s, j, 0)),
        ),
        out_shape=jax.ShapeDtypeStruct(shape, BF16),
        input_output_aliases=aliases,
        compiler_params=params(),
        cost_estimate=pl.CostEstimate(
            flops=2 * nt * ns * n * nc * (9 * nc + nf),
            bytes_accessed=2 * nt * ns * (9 * nc * nc + 5 * n * nc + nf * nc + n * nf),
            transcendentals=0,
        ),
        name="prolong",
    )(*operands)


def exchange(e, first, last):
    def from_next(x, axis):
        count = lax.axis_size(axis)
        return lax.ppermute(x, axis, [((i + 1) % count, i) for i in range(count)])

    def from_previous(x, axis):
        count = lax.axis_size(axis)
        return lax.ppermute(x, axis, [(i, (i + 1) % count) for i in range(count)])

    return (
        from_next(e, "src"),
        from_previous(e, "src"),
        from_next(first, "lat"),
        from_previous(last, "lat"),
    )


def body(fine, basis, dinv, hops, nbr, agg):
    n = fine.shape[2] // CHUNKS
    state = []
    for j in range(CHUNKS):
        rhs, e, first, last = restrict(j, n, agg, fine, basis, dinv)
        state.append((rhs, e, exchange(e, first, last)))
    for j in range(CHUNKS):
        rhs, e, halo = state[j]
        e, first, last = sweep(agg, nbr, rhs, e, halo, hops, dinv)
        state[j] = (rhs, e, exchange(e, first, last))
    out = None
    for j in range(CHUNKS):
        rhs, e, halo = state[j]
        out = prolong(j, fine.shape, agg, nbr, rhs, e, halo, hops, dinv, basis, out)
    return out


def solution(mesh):
    return jax.shard_map(
        body,
        mesh=mesh,
        in_specs=(
            P("lat", "src", None, None),
            P("lat", "src", None, None),
            P("lat", "src", None, None),
            P("lat", "src", None, None, None),
            P(),
            P("lat", "src"),
        ),
        out_specs=P("lat", "src", None, None),
        check_vma=False,
    )
```

time: 339 us -> 75 us (0.22)
  waiting for transfers between devices: 257 us -> 2.2 us
  matrix products: 29 us -> 0 us
  Pallas kernels: 0 us -> 21.7 us
  starting transfers between devices: 23.9 us -> 38.6 us
  between operations: 13.5 us -> 0.11 us
  other arithmetic: 8.38 us -> 0 us
  local copies, waits for them, and re-layouts: 7.54 us -> 11.3 us
    all_gather x2 -> x0, waiting for transfers between devices: 225 us -> none  [the longest x1 189 us: body(): lax.all_gather(hoppings, 'src', axis=1, tiled=True)]
    ppermute x4 -> x16, starting transfers between devices: 3.54 us -> 38.6 us  [the longest x8 35.1 us: from_next(): return lax.ppermute(x, axis, [((i + 1) % count, i) for i in range(count)])]
    dot_general x5 -> x0, matrix products: 29 us -> none  [the longest x2 20 us: later_sweep(): jnp.einsum('tsnc,tscd->tsnd', difference, inverse_blocks, preferred_eleme...]
    all_to_all x2 -> x0, waiting for transfers between devices: 25.4 us -> none  [the longest x1 13.8 us: body(): lax.all_to_all(coarse_rhs, 'src', split_axis=2, concat_axis=1, tiled=True)]
    pallas_call x0 -> x6, Pallas kernels: none -> 21.7 us  [the longest x2 8.55 us: prolong(): pl.pallas_call(prolong_kernel, grid_spec=pltpu.PrefetchScalarGridSpec(num...]
    all_to_all x2 -> x0, starting transfers between devices: 20.3 us -> none  [the longest x1 10.3 us: body(): lax.all_to_all(coarse_rhs, 'src', split_axis=2, concat_axis=1, tiled=True)]
    unnamed x5 -> x29, local copies, waits for them, and re-layouts: 0.77 us -> 11.3 us
    select_n x4 -> x0, other arithmetic: 6.74 us -> none  [the longest x3 5.7 us: hop_terms(): spatial = jnp.take(source, neighbour_rows, axis=1)]
  transfers between devices with their start and end apart: 8 -> 16, of which waited for: 6 -> 2; matrix products, arithmetic and copies ran while one was open for 5% -> 1% of each run, Pallas kernels for 0% -> 20%
where the time goes in v1:
time: 75 us; the launch traced here: 73.8 us
  starting transfers between devices  38.6 us (51%)
  Pallas kernels  21.7 us (29%)
  local copies, waits for them, and re-layouts  11.3 us (15%)
  waiting for transfers between devices  2.2 us (3%)
    ppermute x8, starting transfers between devices, from_next(): return lax.ppermute(x, axis, [((i + 1) % count, i) for i in range(count)])  35.1 us
    unnamed x29, local copies, waits for them, and re-layouts  11.3 us
    pallas_call x2, Pallas kernels, prolong(): pl.pallas_call(prolong_kernel, grid_spec=pltpu.PrefetchScalarGridSpec(num...  8.55 us
    pallas_call x2, Pallas kernels, sweep(): pl.pallas_call(sweep_kernel, grid_spec=pltpu.PrefetchScalarGridSpec(num_s...  7.33 us
    pallas_call x2, Pallas kernels, restrict(): pl.pallas_call(restrict_kernel, grid_spec=pltpu.PrefetchScalarGridSpec(nu...  5.81 us
    ppermute x8, starting transfers between devices, from_previous(): return lax.ppermute(x, axis, [(i, (i + 1) % count) for i in range(count)])  3.45 us
    ppermute x8, waiting for transfers between devices, from_previous(): return lax.ppermute(x, axis, [(i, (i + 1) % count) for i in range(count)])  1.52 us
  transfers between devices with their start and end apart: 16, of which 2 were waited for; matrix products, arithmetic and copies ran while one was open for 1% of the time, Pallas kernels for 20%

profile of v1, /device:TPU:32, one launch (start us, length us, event | category | flops | bytes accessed | tf_op | source)
XLA Modules:
  0.0 73.8 jit_solution(17526278339450267507)
XLA Ops:
  0.0 0.0 copy-start
  0.0 1.6 %copy-done = bf16[2,2,2048,128]{3,2,1,0:T(8,128)(2,1)S(1)} copy-done((bf16[2,2,2048,128]{3,2,1,0:T(8,128)(2,1)S(1)}, bf16[2,2,2048,128]{3,2,1,0:T(8,128)(2,1)}, u32[]{:S(2)}) %copy-start) | copy-done | bytes 2097176
  1.6 0.0 copy-start.3
  1.6 2.2 %copy-done.3 = bf16[2,2,256,2048]{3,2,1,0:T(8,128)(2,1)S(1)} copy-done((bf16[2,2,256,2048]{3,2,1,0:T(8,128)(2,1)S(1)}, bf16[2,2,256,2048]{3,2,1,0:T(8,128)(2,1)}, u32[]{:S(2)}) %copy-start.3) | copy-done | bytes 4194328
  3.8 0.0 copy-start.4
  3.8 0.9 %copy-done.4 = bf16[2,2,128,128]{3,2,1,0:T(8,128)(2,1)S(1)} copy-done((bf16[2,2,128,128]{3,2,1,0:T(8,128)(2,1)S(1)}, bf16[2,2,128,128]{3,2,1,0:T(8,128)(2,1)}, u32[]{:S(2)}) %copy-start.4) | copy-done | bytes 131096
  4.7 0.0 copy-start.12
  4.7 0.7 copy-done.12
  5.4 2.9 %restrict.3 = (bf16[2,2,128,128]{3,2,1,0:T(8,128)(2,1)S(1)}, bf16[2,2,128,128]{3,2,1,0:T(8,128)(2,1)}, bf16[2,128,128]{2,1,0:T(8,128)(2,1)S(1)}, bf16[2,128,128]{2,1,0:T(8,128)(2,1)S(1)}) custom-call(s32[2,2]{1,0:T(2,128)S(1)} %copy-done.12, bf16[2,2,256,2048]{3,2,1,0:T(8,128)(2,1)S(1)} %copy-done.3, bf16[2,2,2048,128]{3,2,1,0:T(8,128)(2,1)S(1)} %copy-done, ...), custom_call_target="tpu_custom_call" | custom-call | flops 285212672 | bytes 4194304 | tf_op jit(solution)/shard_map/restrict/pallas_call | solution.py:54
  8.2 0.0 copy-start.2
  8.2 0.0 copy-start.5
  8.2 3.3 %collective-permute-start.9 = (bf16[2,2,128,128]{3,2,1,0:T(8,128)(2,1)}, bf16[2,2,128,128]{3,2,1,0:T(8,128)(2,1)S(1)}, u32[]{:S(2)}, u32[]{:S(2)}) collective-permute-start(bf16[2,2,128,128]{3,2,1,0:T(8,128)(2,1)} %get-tuple-element.27.e), channel_id=1, source_target_pairs={{0,1},{1,2},{2,3},{3,4},{4,5},{5,6},{6,7},{7,8},{8,9},{9,10},{10,1... | collective-permute-start | bytes 393224 | tf_op jit(solution)/shard_map/ppermute | solution.py:211
  11.5 4.6 %collective-permute-start.8 = (bf16[2,2,128,128]{3,2,1,0:T(8,128)(2,1)}, bf16[2,2,128,128]{3,2,1,0:T(8,128)(2,1)}, u32[]{:S(2)}, u32[]{:S(2)}) collective-permute-start(bf16[2,2,128,128]{3,2,1,0:T(8,128)(2,1)} %get-tuple-element.27.e), channel_id=1, source_target_pairs={{1,0},{2,1},{3,2},{4,3},{5,4},{6,5},{7,6},{8,7},{9,8},{10,9},{11,1... | collective-permute-start | bytes 393224 | tf_op jit(solution)/shard_map/ppermute | solution.py:207
  16.1 2.4 %collective-permute-start.10 = (bf16[2,128,128]{2,1,0:T(8,128)(2,1)S(1)}, bf16[2,128,128]{2,1,0:T(8,128)(2,1)S(1)}, u32[]{:S(2)}, u32[]{:S(2)}) collective-permute-start(bf16[2,128,128]{2,1,0:T(8,128)(2,1)S(1)} %get-tuple-element.28), channel_id=1, source_target_pairs={{16,0},{32,16},{48,32},{64,48},{80,64},{96,80},{112,96},{128,112},... | collective-permute-start | bytes 196616 | tf_op jit(solution)/shard_map/ppermute | solution.py:207
  18.5 0.0 copy-start.1
  18.5 0.0 collective-permute-start.11
  18.5 2.9 %restrict.2 = (bf16[2,2,128,128]{3,2,1,0:T(8,128)(2,1)S(1)}, bf16[2,2,128,128]{3,2,1,0:T(8,128)(2,1)}, bf16[2,128,128]{2,1,0:T(8,128)(2,1)}, bf16[2,128,128]{2,1,0:T(8,128)(2,1)}) custom-call(s32[2,2]{1,0:T(2,128)S(1)} %copy-done.12, bf16[2,2,256,2048]{3,2,1,0:T(8,128)(2,1)S(1)} %copy-done.3, bf16[2,2,2048,128]{3,2,1,0:T(8,128)(2,1)S(1)} %copy-done, ...), custom_call_target="tpu_custom_call" | custom-call | flops 285212672 | bytes 4194304 | tf_op jit(solution)/shard_map/restrict/pallas_call | solution.py:54
  21.4 0.0 collective-permute-start.1
  21.4 0.7 collective-permute-done.10.lup
  22.1 0.6 copy-done.8
  22.7 5.6 %collective-permute-start = (bf16[2,2,128,128]{3,2,1,0:T(8,128)(2,1)}, bf16[2,2,128,128]{3,2,1,0:T(8,128)(2,1)}, u32[]{:S(2)}, u32[]{:S(2)}) collective-permute-start(bf16[2,2,128,128]{3,2,1,0:T(8,128)(2,1)} %get-tuple-element.20.e), channel_id=1, source_target_pairs={{1,0},{2,1},{3,2},{4,3},{5,4},{6,5},{7,6},{8,7},{9,8},{10,9},{11,1... | collective-permute-start | bytes 393224 | tf_op jit(solution)/shard_map/ppermute | solution.py:207
  28.3 0.0 collective-permute-done.11.ldn
  28.3 0.0 copy-start.10
  28.3 0.6 copy-done.10
  28.9 3.3 %collective-permute-start.2 = (bf16[2,128,128]{2,1,0:T(8,128)(2,1)}, bf16[2,128,128]{2,1,0:T(8,128)(2,1)}, u32[]{:S(2)}, u32[]{:S(2)}) collective-permute-start(bf16[2,128,128]{2,1,0:T(8,128)(2,1)} %get-tuple-element.21), channel_id=1, source_target_pairs={{16,0},{32,16},{48,32},{64,48},{80,64},{96,80},{112,96},{128,112},... | collective-permute-start | bytes 196616 | tf_op jit(solution)/shard_map/ppermute | solution.py:207
  32.2 0.0 collective-permute-done.9.dn
  32.2 0.0 copy-start.6
  32.2 0.6 copy-done.6
  32.8 0.0 collective-permute-start.3
  32.8 0.8 %copy.11.nbr = s32[32,6]{1,0:T(8,128)S(1)} copy(s32[32,6]{0,1:T(8,128)} %param.10) | data formatting | bytes 1536 | tf_op args[4]
  33.6 0.0 collective-permute-done.8.up
  33.6 0.0 copy-done.2
  33.6 0.0 copy-done.5
  33.6 0.0 copy-start.7
  33.6 0.9 %copy-done.7 = bf16[2,2,128,128]{3,2,1,0:T(8,128)(2,1)S(1)} copy-done((bf16[2,2,128,128]{3,2,1,0:T(8,128)(2,1)S(1)}, bf16[2,2,128,128]{3,2,1,0:T(8,128)(2,1)}, u32[]{:S(2)}) %copy-start.7) | copy-done | bytes 131096
  34.5 0.0 copy-start.9
  34.5 0.8 %copy-done.9 = bf16[2,128,128]{2,1,0:T(8,128)(2,1)S(1)} copy-done((bf16[2,128,128]{2,1,0:T(8,128)(2,1)S(1)}, bf16[2,128,128]{2,1,0:T(8,128)(2,1)}, u32[]{:S(2)}) %copy-start.9) | copy-done | bytes 65560
  35.4 0.8 %copy-done.11 = bf16[2,128,128]{2,1,0:T(8,128)(2,1)S(1)} copy-done((bf16[2,128,128]{2,1,0:T(8,128)(2,1)S(1)}, bf16[2,128,128]{2,1,0:T(8,128)(2,1)}, u32[]{:S(2)}) %copy-start.11) | copy-done | bytes 65560
  36.2 0.7 copy-done.13
  36.9 3.6 %sweep.3 = (bf16[2,2,128,128]{3,2,1,0:T(8,128)(2,1)S(1)}, bf16[2,128,128]{2,1,0:T(8,128)(2,1)S(1)}, bf16[2,128,128]{2,1,0:T(8,128)(2,1)S(1)}) custom-call(s32[2,2]{1,0:T(2,128)S(1)} %copy-done.13, s32[32,6]{1,0:T(8,128)S(1)} %copy.11.nbr, bf16[2,2,128,128]{3,2,1,0:T(8,128)(2,1)S(1)} %get-tuple-element.26.rhs, bf16[2,2,128,128]{3,2,1,0:T(8,128)(2,1)} %get-tuple-element.27.e, ...), custom_call_target="tpu_custom_call" | custom-call | flops 150994944 | bytes 1835008 | tf_op jit(solution)/shard_map/sweep/pallas_call | solution.py:119
  40.5 0.1 collective-permute-start.13
  40.6 0.0 collective-permute-done.2.lup
  40.6 3.9 %collective-permute-start.14 = (bf16[2,128,128]{2,1,0:T(8,128)(2,1)S(1)}, bf16[2,128,128]{2,1,0:T(8,128)(2,1)S(1)}, u32[]{:S(2)}, u32[]{:S(2)}) collective-permute-start(bf16[2,128,128]{2,1,0:T(8,128)(2,1)S(1)} %get-tuple-element.31), channel_id=1, source_target_pairs={{16,0},{32,16},{48,32},{64,48},{80,64},{96,80},{112,96},{128,112},... | collective-permute-start | bytes 196616 | tf_op jit(solution)/shard_map/ppermute | solution.py:207
  44.5 0.0 collective-permute-done.3.ldn
  44.6 5.9 %collective-permute-start.12 = (bf16[2,2,128,128]{3,2,1,0:T(8,128)(2,1)S(1)}, bf16[2,2,128,128]{3,2,1,0:T(8,128)(2,1)S(1)}, u32[]{:S(2)}, u32[]{:S(2)}) collective-permute-start(bf16[2,2,128,128]{3,2,1,0:T(8,128)(2,1)S(1)} %get-tuple-element.30.e), channel_id=1, source_target_pairs={{1,0},{2,1},{3,2},{4,3},{5,4},{6,5},{7,6},{8,7},{9,8},{10,9},{11,1... | collective-permute-start | bytes 393224 | tf_op jit(solution)/shard_map/ppermute | solution.py:207
  50.4 0.0 collective-permute-done.1.dn
  50.4 0.0 collective-permute-start.15
  50.4 0.0 collective-permute-done.up
  50.4 3.7 %sweep.2 = (bf16[2,2,128,128]{3,2,1,0:T(8,128)(2,1)S(1)}, bf16[2,128,128]{2,1,0:T(8,128)(2,1)S(1)}, bf16[2,128,128]{2,1,0:T(8,128)(2,1)S(1)}) custom-call(s32[2,2]{1,0:T(2,128)S(1)} %copy-done.13, s32[32,6]{1,0:T(8,128)S(1)} %copy.11.nbr, bf16[2,2,128,128]{3,2,1,0:T(8,128)(2,1)S(1)} %get-tuple-element.19.rhs, bf16[2,2,128,128]{3,2,1,0:T(8,128)(2,1)} %get-tuple-element.20.e, ...), custom_call_target="tpu_custom_call" | custom-call | flops 150994944 | bytes 1835008 | tf_op jit(solution)/shard_map/sweep/pallas_call | solution.py:119
  54.2 0.1 collective-permute-start.5
  54.2 0.0 collective-permute-done.14.lup
  54.3 6.2 %collective-permute-start.4 = (bf16[2,2,128,128]{3,2,1,0:T(8,128)(2,1)S(1)}, bf16[2,2,128,128]{3,2,1,0:T(8,128)(2,1)S(1)}, u32[]{:S(2)}, u32[]{:S(2)}) collective-permute-start(bf16[2,2,128,128]{3,2,1,0:T(8,128)(2,1)S(1)} %get-tuple-element.23.e), channel_id=1, source_target_pairs={{1,0},{2,1},{3,2},{4,3},{5,4},{6,5},{7,6},{8,7},{9,8},{10,9},{11,1... | collective-permute-start | bytes 393224 | tf_op jit(solution)/shard_map/ppermute | solution.py:207
  60.5 0.0 collective-permute-done.15.ldn
  60.5 3.3 %collective-permute-start.6 = (bf16[2,128,128]{2,1,0:T(8,128)(2,1)S(1)}, bf16[2,128,128]{2,1,0:T(8,128)(2,1)S(1)}, u32[]{:S(2)}, u32[]{:S(2)}) collective-permute-start(bf16[2,128,128]{2,1,0:T(8,128)(2,1)S(1)} %get-tuple-element.24), channel_id=1, source_target_pairs={{16,0},{32,16},{48,32},{64,48},{80,64},{96,80},{112,96},{128,112},... | collective-permute-start | bytes 196616 | tf_op jit(solution)/shard_map/ppermute | solution.py:207
  63.8 0.0 collective-permute-done.13.dn
  63.8 0.0 collective-permute-start.7
  63.8 0.0 collective-permute-done.12.up
  63.8 0.0 copy-done.1
  63.8 4.3 %prolong.2.rest_0_ = bf16[2,2,256,2048]{3,2,1,0:T(8,128)(2,1)} custom-call(s32[2,2]{1,0:T(2,128)S(1)} %copy-done.13, s32[32,6]{1,0:T(8,128)S(1)} %copy.11.nbr, bf16[2,2,128,128]{3,2,1,0:T(8,128)(2,1)S(1)} %get-tuple-element.26.rhs, bf16[2,2,128,128]{3,2,1,0:T(8,128)(2,1)S(1)} %get-tuple-element.30.e, ...), custom_call_target="tpu_custom_call" | custom-call | flops 419430400 | bytes 6029312 | tf_op jit(solution)/shard_map/prolong/pallas_call | solution.py:184
  68.1 0.0 collective-permute-done.6.lup
  68.1 1.5 %collective-permute-done.7.ldn = bf16[2,128,128]{2,1,0:T(8,128)(2,1)S(1)} collective-permute-done((bf16[2,128,128]{2,1,0:T(8,128)(2,1)S(1)}, bf16[2,128,128]{2,1,0:T(8,128)(2,1)S(1)}, u32[]{:S(2)}, u32[]{:S(2)}) %collective-permute-start.7) | collective-permute-done | bytes 65568 | tf_op jit(solution)/shard_map/ppermute | solution.py:211
  69.6 0.0 collective-permute-done.5.dn
  69.6 0.0 collective-permute-done.4.up
  69.6 4.3 %prolong.3 = bf16[2,2,256,2048]{3,2,1,0:T(8,128)(2,1)} custom-call(s32[2,2]{1,0:T(2,128)S(1)} %copy-done.13, s32[32,6]{1,0:T(8,128)S(1)} %copy.11.nbr, bf16[2,2,128,128]{3,2,1,0:T(8,128)(2,1)S(1)} %get-tuple-element.19.rhs, bf16[2,2,128,128]{3,2,1,0:T(8,128)(2,1)S(1)} %get-tuple-element.23.e, ...), custom_call_target="tpu_custom_call", output_to_operand_aliasing={{}: (11, {})} | custom-call | flops 419430400 | bytes 6029312 | tf_op jit(solution)/shard_map/prolong/pallas_call | solution.py:184
  (3 shorter events, 0.0 us)
Async XLA Ops:
  0.0 1.6 %copy-start = (bf16[2,2,2048,128]{3,2,1,0:T(8,128)(2,1)S(1)}, bf16[2,2,2048,128]{3,2,1,0:T(8,128)(2,1)}, u32[]{:S(2)}) copy-start(bf16[2,2,2048,128]{3,2,1,0:T(8,128)(2,1)} %basis.7) | copy-start | bytes 6291460
  1.6 2.2 %copy-start.3 = (bf16[2,2,256,2048]{3,2,1,0:T(8,128)(2,1)S(1)}, bf16[2,2,256,2048]{3,2,1,0:T(8,128)(2,1)}, u32[]{:S(2)}) copy-start(bf16[2,2,256,2048]{3,2,1,0:T(8,128)(2,1)} %fine.3) | copy-start | bytes 12582916
  3.8 0.9 %copy-start.4 = (bf16[2,2,128,128]{3,2,1,0:T(8,128)(2,1)S(1)}, bf16[2,2,128,128]{3,2,1,0:T(8,128)(2,1)}, u32[]{:S(2)}) copy-start(bf16[2,2,128,128]{3,2,1,0:T(8,128)(2,1)} %dinv.11) | copy-start | bytes 393220
  4.7 0.7 copy-start.12
  8.2 25.4 %copy-start.2 = (bf16[2,2,8,128,128]{4,3,2,1,0:T(8,128)(2,1)S(1)}, bf16[2,2,8,128,128]{4,3,2,1,0:T(8,128)(2,1)}, u32[]{:S(2)}) copy-start(bf16[2,2,8,128,128]{4,3,2,1,0:T(8,128)(2,1)} %hops.7) | copy-start | bytes 3145732
  8.2 25.4 %copy-start.5 = (bf16[2,2,128,128]{3,2,1,0:T(8,128)(2,1)S(1)}, bf16[2,2,128,128]{3,2,1,0:T(8,128)(2,1)}, u32[]{:S(2)}) copy-start(bf16[2,2,128,128]{3,2,1,0:T(8,128)(2,1)} %dinv.11) | copy-start | bytes 393220
  8.2 23.9 %collective-permute-start.9 = (bf16[2,2,128,128]{3,2,1,0:T(8,128)(2,1)}, bf16[2,2,128,128]{3,2,1,0:T(8,128)(2,1)S(1)}, u32[]{:S(2)}, u32[]{:S(2)}) collective-permute-start(bf16[2,2,128,128]{3,2,1,0:T(8,128)(2,1)} %get-tuple-element.27.e), channel_id=1, source_target_pairs={{0,1},{1,2},{2,3},{3,4},{4,5},{5,6},{6,7},{7,8},{8,9},{9,10},{10,1... | collective-permute-start | bytes 393224 | tf_op jit(solution)/shard_map/ppermute | solution.py:211
  11.5 22.1 %collective-permute-start.8 = (bf16[2,2,128,128]{3,2,1,0:T(8,128)(2,1)}, bf16[2,2,128,128]{3,2,1,0:T(8,128)(2,1)}, u32[]{:S(2)}, u32[]{:S(2)}) collective-permute-start(bf16[2,2,128,128]{3,2,1,0:T(8,128)(2,1)} %get-tuple-element.27.e), channel_id=1, source_target_pairs={{1,0},{2,1},{3,2},{4,3},{5,4},{6,5},{7,6},{8,7},{9,8},{10,9},{11,1... | collective-permute-start | bytes 393224 | tf_op jit(solution)/shard_map/ppermute | solution.py:207
  16.1 6.0 %collective-permute-start.10 = (bf16[2,128,128]{2,1,0:T(8,128)(2,1)S(1)}, bf16[2,128,128]{2,1,0:T(8,128)(2,1)S(1)}, u32[]{:S(2)}, u32[]{:S(2)}) collective-permute-start(bf16[2,128,128]{2,1,0:T(8,128)(2,1)S(1)} %get-tuple-element.28), channel_id=1, source_target_pairs={{16,0},{32,16},{48,32},{64,48},{80,64},{96,80},{112,96},{128,112},... | collective-permute-start | bytes 196616 | tf_op jit(solution)/shard_map/ppermute | solution.py:207
  18.5 45.3 %copy-start.1 = (bf16[2,2,2048,128]{3,2,1,0:T(8,128)(2,1)S(1)}, bf16[2,2,2048,128]{3,2,1,0:T(8,128)(2,1)}, u32[]{:S(2)}) copy-start(bf16[2,2,2048,128]{3,2,1,0:T(8,128)(2,1)} %basis.7) | copy-start | bytes 6291460
  18.5 9.8 %collective-permute-start.11 = (bf16[2,128,128]{2,1,0:T(8,128)(2,1)S(1)}, bf16[2,128,128]{2,1,0:T(8,128)(2,1)S(1)}, u32[]{:S(2)}, u32[]{:S(2)}) collective-permute-start(bf16[2,128,128]{2,1,0:T(8,128)(2,1)S(1)} %get-tuple-element.29), channel_id=1, source_target_pairs={{0,16},{16,32},{32,48},{48,64},{64,80},{80,96},{96,112},{112,128},... | collective-permute-start | bytes 196616 | tf_op jit(solution)/shard_map/ppermute | solution.py:211
  21.4 29.0 %collective-permute-start.1 = (bf16[2,2,128,128]{3,2,1,0:T(8,128)(2,1)}, bf16[2,2,128,128]{3,2,1,0:T(8,128)(2,1)}, u32[]{:S(2)}, u32[]{:S(2)}) collective-permute-start(bf16[2,2,128,128]{3,2,1,0:T(8,128)(2,1)} %get-tuple-element.20.e), channel_id=1, source_target_pairs={{0,1},{1,2},{2,3},{3,4},{4,5},{5,6},{6,7},{7,8},{8,9},{9,10},{10,1... | collective-permute-start | bytes 393224 | tf_op jit(solution)/shard_map/ppermute | solution.py:211
  22.1 0.6 copy-start.8
  22.7 27.7 %collective-permute-start = (bf16[2,2,128,128]{3,2,1,0:T(8,128)(2,1)}, bf16[2,2,128,128]{3,2,1,0:T(8,128)(2,1)}, u32[]{:S(2)}, u32[]{:S(2)}) collective-permute-start(bf16[2,2,128,128]{3,2,1,0:T(8,128)(2,1)} %get-tuple-element.20.e), channel_id=1, source_target_pairs={{1,0},{2,1},{3,2},{4,3},{5,4},{6,5},{7,6},{8,7},{9,8},{10,9},{11,1... | collective-permute-start | bytes 393224 | tf_op jit(solution)/shard_map/ppermute | solution.py:207
  28.3 0.6 copy-start.10
  28.9 11.7 %collective-permute-start.2 = (bf16[2,128,128]{2,1,0:T(8,128)(2,1)}, bf16[2,128,128]{2,1,0:T(8,128)(2,1)}, u32[]{:S(2)}, u32[]{:S(2)}) collective-permute-start(bf16[2,128,128]{2,1,0:T(8,128)(2,1)} %get-tuple-element.21), channel_id=1, source_target_pairs={{16,0},{32,16},{48,32},{64,48},{80,64},{96,80},{112,96},{128,112},... | collective-permute-start | bytes 196616 | tf_op jit(solution)/shard_map/ppermute | solution.py:207
  32.2 0.6 copy-start.6
  32.8 11.7 %collective-permute-start.3 = (bf16[2,128,128]{2,1,0:T(8,128)(2,1)}, bf16[2,128,128]{2,1,0:T(8,128)(2,1)}, u32[]{:S(2)}, u32[]{:S(2)}) collective-permute-start(bf16[2,128,128]{2,1,0:T(8,128)(2,1)} %get-tuple-element.22), channel_id=1, source_target_pairs={{0,16},{16,32},{32,48},{48,64},{64,80},{80,96},{96,112},{112,128},... | collective-permute-start | bytes 196616 | tf_op jit(solution)/shard_map/ppermute | solution.py:211
  33.6 0.9 %copy-start.7 = (bf16[2,2,128,128]{3,2,1,0:T(8,128)(2,1)S(1)}, bf16[2,2,128,128]{3,2,1,0:T(8,128)(2,1)}, u32[]{:S(2)}) copy-start(bf16[2,2,128,128]{3,2,1,0:T(8,128)(2,1)} %copy-done.6) | copy-start | bytes 393220
  34.5 0.8 %copy-start.9 = (bf16[2,128,128]{2,1,0:T(8,128)(2,1)S(1)}, bf16[2,128,128]{2,1,0:T(8,128)(2,1)}, u32[]{:S(2)}) copy-start(bf16[2,128,128]{2,1,0:T(8,128)(2,1)} %copy-done.8) | copy-start | bytes 196612
  35.4 0.8 %copy-start.11 = (bf16[2,128,128]{2,1,0:T(8,128)(2,1)S(1)}, bf16[2,128,128]{2,1,0:T(8,128)(2,1)}, u32[]{:S(2)}) copy-start(bf16[2,128,128]{2,1,0:T(8,128)(2,1)} %copy-done.10) | copy-start | bytes 196612
  36.2 0.7 copy-start.13
  40.5 23.3 %collective-permute-start.13 = (bf16[2,2,128,128]{3,2,1,0:T(8,128)(2,1)S(1)}, bf16[2,2,128,128]{3,2,1,0:T(8,128)(2,1)S(1)}, u32[]{:S(2)}, u32[]{:S(2)}) collective-permute-start(bf16[2,2,128,128]{3,2,1,0:T(8,128)(2,1)S(1)} %get-tuple-element.30.e), channel_id=1, source_target_pairs={{0,1},{1,2},{2,3},{3,4},{4,5},{5,6},{6,7},{7,8},{8,9},{9,10},{10,1... | collective-permute-start | bytes 393224 | tf_op jit(solution)/shard_map/ppermute | solution.py:211
  40.6 13.6 %collective-permute-start.14 = (bf16[2,128,128]{2,1,0:T(8,128)(2,1)S(1)}, bf16[2,128,128]{2,1,0:T(8,128)(2,1)S(1)}, u32[]{:S(2)}, u32[]{:S(2)}) collective-permute-start(bf16[2,128,128]{2,1,0:T(8,128)(2,1)S(1)} %get-tuple-element.31), channel_id=1, source_target_pairs={{16,0},{32,16},{48,32},{64,48},{80,64},{96,80},{112,96},{128,112},... | collective-permute-start | bytes 196616 | tf_op jit(solution)/shard_map/ppermute | solution.py:207
  44.6 19.2 %collective-permute-start.12 = (bf16[2,2,128,128]{3,2,1,0:T(8,128)(2,1)S(1)}, bf16[2,2,128,128]{3,2,1,0:T(8,128)(2,1)S(1)}, u32[]{:S(2)}, u32[]{:S(2)}) collective-permute-start(bf16[2,2,128,128]{3,2,1,0:T(8,128)(2,1)S(1)} %get-tuple-element.30.e), channel_id=1, source_target_pairs={{1,0},{2,1},{3,2},{4,3},{5,4},{6,5},{7,6},{8,7},{9,8},{10,9},{11,1... | collective-permute-start | bytes 393224 | tf_op jit(solution)/shard_map/ppermute | solution.py:207
  50.4 10.1 %collective-permute-start.15 = (bf16[2,128,128]{2,1,0:T(8,128)(2,1)S(1)}, bf16[2,128,128]{2,1,0:T(8,128)(2,1)S(1)}, u32[]{:S(2)}, u32[]{:S(2)}) collective-permute-start(bf16[2,128,128]{2,1,0:T(8,128)(2,1)S(1)} %get-tuple-element.32), channel_id=1, source_target_pairs={{0,16},{16,32},{32,48},{48,64},{64,80},{80,96},{96,112},{112,128},... | collective-permute-start | bytes 196616 | tf_op jit(solution)/shard_map/ppermute | solution.py:211
  54.2 15.4 %collective-permute-start.5 = (bf16[2,2,128,128]{3,2,1,0:T(8,128)(2,1)S(1)}, bf16[2,2,128,128]{3,2,1,0:T(8,128)(2,1)S(1)}, u32[]{:S(2)}, u32[]{:S(2)}) collective-permute-start(bf16[2,2,128,128]{3,2,1,0:T(8,128)(2,1)S(1)} %get-tuple-element.23.e), channel_id=1, source_target_pairs={{0,1},{1,2},{2,3},{3,4},{4,5},{5,6},{6,7},{7,8},{8,9},{9,10},{10,1... | collective-permute-start | bytes 393224 | tf_op jit(solution)/shard_map/ppermute | solution.py:211
  54.3 15.3 %collective-permute-start.4 = (bf16[2,2,128,128]{3,2,1,0:T(8,128)(2,1)S(1)}, bf16[2,2,128,128]{3,2,1,0:T(8,128)(2,1)S(1)}, u32[]{:S(2)}, u32[]{:S(2)}) collective-permute-start(bf16[2,2,128,128]{3,2,1,0:T(8,128)(2,1)S(1)} %get-tuple-element.23.e), channel_id=1, source_target_pairs={{1,0},{2,1},{3,2},{4,3},{5,4},{6,5},{7,6},{8,7},{9,8},{10,9},{11,1... | collective-permute-start | bytes 393224 | tf_op jit(solution)/shard_map/ppermute | solution.py:207
  60.5 7.6 %collective-permute-start.6 = (bf16[2,128,128]{2,1,0:T(8,128)(2,1)S(1)}, bf16[2,128,128]{2,1,0:T(8,128)(2,1)S(1)}, u32[]{:S(2)}, u32[]{:S(2)}) collective-permute-start(bf16[2,128,128]{2,1,0:T(8,128)(2,1)S(1)} %get-tuple-element.24), channel_id=1, source_target_pairs={{16,0},{32,16},{48,32},{64,48},{80,64},{96,80},{112,96},{128,112},... | collective-permute-start | bytes 196616 | tf_op jit(solution)/shard_map/ppermute | solution.py:207
  63.8 5.8 %collective-permute-start.7 = (bf16[2,128,128]{2,1,0:T(8,128)(2,1)S(1)}, bf16[2,128,128]{2,1,0:T(8,128)(2,1)S(1)}, u32[]{:S(2)}, u32[]{:S(2)}) collective-permute-start(bf16[2,128,128]{2,1,0:T(8,128)(2,1)S(1)} %get-tuple-element.25), channel_id=1, source_target_pairs={{0,16},{16,32},{32,48},{48,64},{64,80},{80,96},{96,112},{112,128},... | collective-permute-start | bytes 196616 | tf_op jit(solution)/shard_map/ppermute | solution.py:211

commit v2 on v0

v2 whole, which is shorter than its diff:
```python
import functools

import jax
import jax.numpy as jnp
from jax import lax
from jax.experimental import pallas as pl
from jax.experimental.pallas import tpu as pltpu
from jax.sharding import PartitionSpec as P

DAMPING = 0.8
KEEP = 1.0 - DAMPING
BF16 = jnp.bfloat16
F32 = jnp.float32
PIECES = 4
HBM = pl.BlockSpec(memory_space=pltpu.HBM)
VMEM = pl.BlockSpec(memory_space=pltpu.VMEM)
PARAMS = pltpu.CompilerParams(vmem_limit_bytes=32 * 1024 * 1024)


def in_hbm(x):
    return pltpu.with_memory_space_constraint(x, pltpu.HBM)


def in_vmem(x):
    return pltpu.with_memory_space_constraint(x, pltpu.VMEM)


def dot(a, b):
    return jnp.dot(a, b, preferred_element_type=F32)


class Copies:
    def __init__(self, sems):
        self.sems = sems
        self.count = 0

    def start(self, src, dst):
        copy = pltpu.make_async_copy(src, dst, self.sems.at[self.count])
        self.count += 1
        copy.start()
        return copy


def restrict_kernel(
    t, agg, fine, basis, dinv, rhs, e, agg_s, fine_v, basis_v, dinv_v, sems
):
    ns, n = fine_v.shape[0], fine_v.shape[1]
    rows = n // PIECES
    copies = Copies(sems)
    agg_in = copies.start(agg, agg_s)
    basis_in, fine_in = [], []
    for s in range(ns):
        basis_in.append(copies.start(basis.at[t, s], basis_v.at[s]))
        for p in range(PIECES):
            part = pl.ds(p * rows, rows)
            fine_in.append(copies.start(fine.at[t, s, part], fine_v.at[s, part]))
    dinv_in = copies.start(dinv.at[t], dinv_v)
    agg_in.wait()
    for s in range(ns):
        c = agg_s[t, s] & 1
        basis_in[s].wait()
        if s == 0:
            dinv_in.wait()
        for p in range(PIECES):
            part = pl.ds(p * rows, rows)
            fine_in[s * PIECES + p].wait()
            r = dot(fine_v[s, part], basis_v[s]).astype(BF16)
            rhs[c, part] = r
            e[c, part] = (DAMPING * dot(r, dinv_v[c])).astype(BF16)


def restrict(t, agg, fine, basis, dinv):
    _, ns, n, nf = fine.shape
    nc = basis.shape[3]
    part = pltpu.VMEM((ns, n, nc), BF16)
    return pl.pallas_call(
        functools.partial(restrict_kernel, t),
        in_specs=[HBM] * 4,
        out_specs=[VMEM] * 2,
        out_shape=[part, part],
        scratch_shapes=[
            pltpu.SMEM(agg.shape, jnp.int32),
            pltpu.VMEM((ns, n, nf), BF16),
            pltpu.VMEM((ns, nf, nc), BF16),
            pltpu.VMEM((ns, nc, nc), BF16),
            pltpu.SemaphoreType.DMA((2 + ns * (PIECES + 1),)),
        ],
        compiler_params=PARAMS,
        cost_estimate=pl.CostEstimate(
            flops=2 * ns * n * nc * (nf + nc),
            bytes_accessed=2 * ns * (n * nf + nf * nc),
            transcendentals=0,
        ),
        name="restrict",
    )(*map(in_hbm, (agg, fine, basis, dinv)))


def next_iterate(c, upward, rhs, e, later, earlier, up, dn, hops, dinv):
    ns, _, nc = e.shape
    own, other = e[c], e[ns - 1 - c]
    above, below = up[c], dn[c]
    stacked = jnp.concatenate(
        [
            jnp.where(upward, above, below),
            jnp.where(upward, below, above),
            own,
            own,
            other,
            other,
            later[c],
            earlier[c],
        ],
        axis=1,
    )
    hop = dot(stacked, hops[c].reshape(8 * nc, nc))
    difference = (rhs[c].astype(F32) - hop).astype(BF16)
    return (KEEP * own.astype(F32) + DAMPING * dot(difference, dinv[c])).astype(BF16)


def is_upward(c, agg_s, nbr_s):
    spatial = nbr_s.shape[1]
    site = (agg_s[0, 0] & -2) + c
    return nbr_s[0, site] == lax.rem(site + 2, spatial)


def fetch_sweep(copies, t, agg, nbr, hops, dinv, agg_s, nbr_s, hops_v, dinv_v):
    return [
        copies.start(agg, agg_s),
        copies.start(nbr, nbr_s),
        copies.start(hops.at[t], hops_v),
        copies.start(dinv.at[t], dinv_v),
    ]


def sweep_kernel(t, *refs):
    agg, nbr = refs[:2]
    coarse = refs[2:8]
    hops, dinv, out, agg_s, nbr_s, hops_v, dinv_v, sems = refs[8:]
    for wait in fetch_sweep(
        Copies(sems), t, agg, nbr, hops, dinv, agg_s, nbr_s, hops_v, dinv_v
    ):
        wait.wait()
    for c in range(out.shape[0]):
        out[c] = next_iterate(c, is_upward(c, agg_s, nbr_s), *coarse, hops_v, dinv_v)


def sweep_scratch(agg, nbr, shape):
    ns, _, nc = shape
    return [
        pltpu.SMEM(agg.shape, jnp.int32),
        pltpu.SMEM(nbr.shape, jnp.int32),
        pltpu.VMEM((ns, 8, nc, nc), BF16),
        pltpu.VMEM((ns, nc, nc), BF16),
    ]


def sweep(t, agg, nbr, coarse, hops, dinv):
    shape = coarse[0].shape
    ns, n, nc = shape
    return pl.pallas_call(
        functools.partial(sweep_kernel, t),
        in_specs=[HBM] * 2 + [VMEM] * 6 + [HBM] * 2,
        out_specs=VMEM,
        out_shape=pltpu.VMEM(shape, BF16),
        scratch_shapes=[
            *sweep_scratch(agg, nbr, shape),
            pltpu.SemaphoreType.DMA((4,)),
        ],
        compiler_params=PARAMS,
        cost_estimate=pl.CostEstimate(
            flops=2 * ns * n * nc * 9 * nc,
            bytes_accessed=2 * ns * (9 * nc * nc + 7 * n * nc),
            transcendentals=0,
        ),
        name="sweep",
    )(in_hbm(agg), in_hbm(nbr), *map(in_vmem, coarse), in_hbm(hops), in_hbm(dinv))


def prolong_kernel(t, *refs):
    agg, nbr = refs[:2]
    coarse = refs[2:8]
    hops, dinv, basis = refs[8:11]
    out, agg_s, nbr_s, hops_v, dinv_v, basis_v, out_v, sems = refs[len(refs) - 8 :]
    ns, n, nf = out_v.shape
    rows = n // PIECES
    copies = Copies(sems)
    waits = fetch_sweep(copies, t, agg, nbr, hops, dinv, agg_s, nbr_s, hops_v, dinv_v)
    basis_in = [copies.start(basis.at[t, s], basis_v.at[s]) for s in range(ns)]
    for wait in waits:
        wait.wait()
    outs = []
    for s in range(ns):
        c = agg_s[t, s] & 1
        value = next_iterate(c, is_upward(c, agg_s, nbr_s), *coarse, hops_v, dinv_v)
        basis_in[s].wait()
        for p in range(PIECES):
            part = pl.ds(p * rows, rows)
            out_v[s, part] = lax.dot_general(
                value[p * rows : (p + 1) * rows],
                basis_v[s],
                (((1,), (1,)), ((), ())),
                preferred_element_type=F32,
            ).astype(BF16)
            outs.append(copies.start(out_v.at[s, part], out.at[t, s, part]))
    for wait in outs:
        wait.wait()


def prolong(t, shape, agg, nbr, coarse, hops, dinv, basis, previous):
    part = coarse[0].shape
    ns, n, nc = part
    nf = basis.shape[2]
    operands = [in_hbm(agg), in_hbm(nbr), *map(in_vmem, coarse)]
    operands += map(in_hbm, (hops, dinv, basis))
    in_specs = [HBM] * 2 + [VMEM] * 6 + [HBM] * 3
    aliases = {}
    if previous is not None:
        aliases = {len(operands): 0}
        operands.append(in_hbm(previous))
        in_specs.append(HBM)
    return pl.pallas_call(
        functools.partial(prolong_kernel, t),
        in_specs=in_specs,
        out_specs=HBM,
        out_shape=pltpu.HBM(shape, BF16),
        input_output_aliases=aliases,
        scratch_shapes=[
            *sweep_scratch(agg, nbr, part),
            pltpu.VMEM((ns, nf, nc), BF16),
            pltpu.VMEM((ns, n, nf), BF16),
            pltpu.SemaphoreType.DMA((4 + ns * (PIECES + 1),)),
        ],
        compiler_params=PARAMS,
        cost_estimate=pl.CostEstimate(
            flops=2 * ns * n * nc * (9 * nc + nf),
            bytes_accessed=2 * ns * (9 * nc * nc + 6 * n * nc + nf * nc + n * nf),
            transcendentals=0,
        ),
        name="prolong",
    )(*operands)


def from_next(x, axis):
    count = lax.axis_size(axis)
    return lax.ppermute(x, axis, [((i + 1) % count, i) for i in range(count)])


def from_previous(x, axis):
    count = lax.axis_size(axis)
    return lax.ppermute(x, axis, [(i, (i + 1) % count) for i in range(count)])


def halos(e):
    first, last = e[0], e[-1]
    beyond = from_next(first, "lat")
    before = from_previous(last, "lat")
    spatial = [(from_next(x, "src"), from_previous(x, "src")) for x in e]
    later = [*e[1:], beyond]
    earlier = [before, *e[:-1]]
    return [(e[t], later[t], earlier[t], *spatial[t]) for t in range(len(e))]


def body(fine, basis, dinv, hops, nbr, agg):
    nbr = nbr.T
    slices = range(fine.shape[0])
    pairs = [restrict(t, agg, fine, basis, dinv) for t in slices]
    rhs = [p[0] for p in pairs]
    e = [p[1] for p in pairs]
    around = halos(e)
    e = [sweep(t, agg, nbr, (rhs[t], *around[t]), hops, dinv) for t in slices]
    around = halos(e)
    out = None
    for t in slices:
        out = prolong(t, fine.shape, agg, nbr, (rhs[t], *around[t]), hops, dinv, basis, out)
    return out


def solution(mesh):
    return jax.shard_map(
        body,
        mesh=mesh,
        in_specs=(
            P("lat", "src", None, None),
            P("lat", "src", None, None),
            P("lat", "src", None, None),
            P("lat", "src", None, None, None),
            P(),
            P("lat", "src"),
        ),
        out_specs=P("lat", "src", None, None),
        check_vma=False,
    )
```

time: 339 us -> 57 us (0.17)
  waiting for transfers between devices: 257 us -> 0.67 us
  matrix products: 29 us -> 0 us
  Pallas kernels: 0 us -> 21.3 us
  between operations: 13.5 us -> 0.25 us
  starting transfers between devices: 23.9 us -> 34.7 us
  other arithmetic: 8.38 us -> 0 us
  local copies, waits for them, and re-layouts: 7.54 us -> 0 us
    all_gather x2 -> x0, waiting for transfers between devices: 225 us -> none  [the longest x1 189 us: body(): lax.all_gather(hoppings, 'src', axis=1, tiled=True)]
    ppermute x4 -> x12, starting transfers between devices: 3.54 us -> 34.7 us  [the longest x6 30.5 us: from_next(): return lax.ppermute(x, axis, [((i + 1) % count, i) for i in range(count)])]
    dot_general x5 -> x0, matrix products: 29 us -> none  [the longest x2 20 us: later_sweep(): jnp.einsum('tsnc,tscd->tsnd', difference, inverse_blocks, preferred_eleme...]
    all_to_all x2 -> x0, waiting for transfers between devices: 25.4 us -> none  [the longest x1 13.8 us: body(): lax.all_to_all(coarse_rhs, 'src', split_axis=2, concat_axis=1, tiled=True)]
    pallas_call x0 -> x6, Pallas kernels: none -> 21.3 us  [the longest x2 9.3 us: restrict(): pl.pallas_call(functools.partial(restrict_kernel, t), in_specs=[HBM] * 4,...]
    all_to_all x2 -> x0, starting transfers between devices: 20.3 us -> none  [the longest x1 10.3 us: body(): lax.all_to_all(coarse_rhs, 'src', split_axis=2, concat_axis=1, tiled=True)]
    select_n x4 -> x0, other arithmetic: 6.74 us -> none  [the longest x3 5.7 us: hop_terms(): spatial = jnp.take(source, neighbour_rows, axis=1)]
    gather x6 -> x0, local copies, waits for them, and re-layouts: 5.46 us -> none  [the longest x2 4.09 us: hop_terms(): spatial = jnp.take(source, neighbour_rows, axis=1)]
  transfers between devices with their start and end apart: 8 -> 12, of which waited for: 6 -> 1; matrix products, arithmetic and copies ran while one was open for 5% -> 0% of each run, Pallas kernels for 0% -> 22%
where the time goes in v2:
time: 57 us; the launch traced here: 56.9 us
  starting transfers between devices  34.7 us (61%)
  Pallas kernels  21.3 us (37%)
  waiting for transfers between devices  0.67 us (1%)
    ppermute x6, starting transfers between devices, from_next(): return lax.ppermute(x, axis, [((i + 1) % count, i) for i in range(count)])  30.5 us
    pallas_call x2, Pallas kernels, restrict(): pl.pallas_call(functools.partial(restrict_kernel, t), in_specs=[HBM] * 4,...  9.3 us
    pallas_call x2, Pallas kernels, prolong(): pl.pallas_call(functools.partial(prolong_kernel, t), in_specs=in_specs, o...  8.49 us
    ppermute x6, starting transfers between devices, from_previous(): return lax.ppermute(x, axis, [(i, (i + 1) % count) for i in range(count)])  4.14 us
    pallas_call x2, Pallas kernels, sweep(): pl.pallas_call(functools.partial(sweep_kernel, t), in_specs=[HBM] * 2 + [...  3.49 us
  transfers between devices with their start and end apart: 12, of which 1 were waited for; matrix products, arithmetic and copies ran while one was open for 0% of the time, Pallas kernels for 22%

profile of v2, /device:TPU:32, one launch (start us, length us, event | category | flops | bytes accessed | tf_op | source)
XLA Modules:
  0.0 56.9 jit_solution(9199658210828893713)
XLA Ops:
  0.0 4.6 %restrict.3 = (bf16[2,256,128]{2,1,0:T(8,128)(2,1)S(1)}, bf16[2,256,128]{2,1,0:T(8,128)(2,1)S(1)}) custom-call(s32[2,2]{1,0:T(2,128)} %refs_0_.7, bf16[2,2,256,2048]{3,2,1,0:T(8,128)(2,1)} %fine.3, bf16[2,2,2048,128]{3,2,1,0:T(8,128)(2,1)} %refs_10_.3, bf16[2,2,128,128]{3,2,1,0:T(8,128)(2,1)} %refs_9_.7), custom_call_target="tpu_custom_call" | custom-call | flops 285212672 | bytes 3145728 | tf_op jit(solution)/shard_map/restrict/pallas_call | solution.py:76
  4.7 3.4 %collective-permute-start.5 = (bf16[2,256,128]{2,1,0:T(8,128)(2,1)S(1)}, bf16[2,256,128]{2,1,0:T(8,128)(2,1)S(1)}, u32[]{:S(2)}, u32[]{:S(2)}) collective-permute-start(bf16[2,256,128]{2,1,0:T(8,128)(2,1)S(1)} %get-tuple-element.11.refs_5_.refs_3_), channel_id=1, source_target_pairs={{0,1},{1,2},{2,3},{3,4},{4,5},{5,6},{6,7},{7,8},{8,9},{9,10},{10,1... | collective-permute-start | bytes 393224 | tf_op jit(solution)/shard_map/ppermute | solution.py:250
  8.0 4.7 %collective-permute-start.4 = (bf16[2,256,128]{2,1,0:T(8,128)(2,1)S(1)}, bf16[2,256,128]{2,1,0:T(8,128)(2,1)S(1)}, u32[]{:S(2)}, u32[]{:S(2)}) collective-permute-start(bf16[2,256,128]{2,1,0:T(8,128)(2,1)S(1)} %get-tuple-element.11.refs_5_.refs_3_), channel_id=1, source_target_pairs={{1,0},{2,1},{3,2},{4,3},{5,4},{6,5},{7,6},{8,7},{9,8},{10,9},{11,1... | collective-permute-start | bytes 393224 | tf_op jit(solution)/shard_map/ppermute | solution.py:245
  12.7 4.6 %restrict.2 = (bf16[2,256,128]{2,1,0:T(8,128)(2,1)S(1)}, bf16[2,256,128]{2,1,0:T(8,128)(2,1)S(1)}) custom-call(s32[2,2]{1,0:T(2,128)} %refs_0_.7, bf16[2,2,256,2048]{3,2,1,0:T(8,128)(2,1)} %fine.3, bf16[2,2,2048,128]{3,2,1,0:T(8,128)(2,1)} %refs_10_.3, bf16[2,2,128,128]{3,2,1,0:T(8,128)(2,1)} %refs_9_.7), custom_call_target="tpu_custom_call" | custom-call | flops 285212672 | bytes 3145728 | tf_op jit(solution)/shard_map/restrict/pallas_call | solution.py:76
  17.3 0.1 collective-permute-start.3
  17.4 3.8 %collective-permute-start = (bf16[2,256,128]{2,1,0:T(8,128)(2,1)S(1)}, bf16[2,256,128]{2,1,0:T(8,128)(2,1)S(1)}, u32[]{:S(2)}, u32[]{:S(2)}) collective-permute-start(bf16[2,256,128]{2,1,0:T(8,128)(2,1)S(1)} %get-tuple-element.11.refs_5_.refs_3_), channel_id=1, source_target_pairs={{16,0},{32,16},{48,32},{64,48},{80,64},{96,80},{112,96},{128,112},... | collective-permute-start | bytes 393224 | tf_op jit(solution)/shard_map/ppermute | solution.py:245
  21.3 0.0 collective-permute-start.2
  21.3 0.0 collective-permute-done.5.refs_7_
  21.3 6.2 %collective-permute-start.1 = (bf16[2,256,128]{2,1,0:T(8,128)(2,1)S(1)}, bf16[2,256,128]{2,1,0:T(8,128)(2,1)S(1)}, u32[]{:S(2)}, u32[]{:S(2)}) collective-permute-start(bf16[2,256,128]{2,1,0:T(8,128)(2,1)S(1)} %get-tuple-element.10.refs_3_.refs_4_), channel_id=1, source_target_pairs={{1,0},{2,1},{3,2},{4,3},{5,4},{6,5},{7,6},{8,7},{9,8},{10,9},{11,1... | collective-permute-start | bytes 393224 | tf_op jit(solution)/shard_map/ppermute | solution.py:245
  27.5 0.0 collective-permute-done.4.refs_6_
  27.5 0.0 collective-permute-done.3.refs_5_
  27.5 1.7 %sweep.3.refs_3_.refs_5_ = bf16[2,256,128]{2,1,0:T(8,128)(2,1)S(1)} custom-call(s32[2,2]{1,0:T(2,128)} %refs_0_.7, s32[6,32]{1,0:T(8,128)} %bitcast.1, bf16[2,256,128]{2,1,0:T(8,128)(2,1)S(1)} %get-tuple-element.12.refs_2_, bf16[2,256,128]{2,1,0:T(8,128)(2,1)S(1)} %get-tuple-element.11.refs_5_.refs_3_, ...), custom_call_target="tpu_custom_call" | custom-call | flops 150994944 | bytes 1507328 | tf_op jit(solution)/shard_map/sweep/pallas_call | solution.py:160
  29.3 0.1 collective-permute-start.11
  29.4 6.2 %collective-permute-start.10 = (bf16[2,256,128]{2,1,0:T(8,128)(2,1)S(1)}, bf16[2,256,128]{2,1,0:T(8,128)(2,1)S(1)}, u32[]{:S(2)}, u32[]{:S(2)}) collective-permute-start(bf16[2,256,128]{2,1,0:T(8,128)(2,1)S(1)} %sweep.3.refs_3_.refs_5_), channel_id=1, source_target_pairs={{1,0},{2,1},{3,2},{4,3},{5,4},{6,5},{7,6},{8,7},{9,8},{10,9},{11,1... | collective-permute-start | bytes 393224 | tf_op jit(solution)/shard_map/ppermute | solution.py:245
  35.6 0.0 collective-permute-done.refs_4_
  35.6 0.0 collective-permute-done.2.refs_7_
  35.6 0.0 collective-permute-done.1.refs_6_
  35.6 1.7 %sweep.2.refs_4_.refs_3_ = bf16[2,256,128]{2,1,0:T(8,128)(2,1)S(1)} custom-call(s32[2,2]{1,0:T(2,128)} %refs_0_.7, s32[6,32]{1,0:T(8,128)} %bitcast.2, bf16[2,256,128]{2,1,0:T(8,128)(2,1)S(1)} %get-tuple-element.9.refs_2_, bf16[2,256,128]{2,1,0:T(8,128)(2,1)S(1)} %get-tuple-element.10.refs_3_.refs_4_, bf16[2,256,128]{2,1,0:T(8,128)(2,1)S(1)} %collective-permute-done.refs_4_, ...), custom_call_target="tpu_custom_call" | custom-call | flops 150994944 | bytes 1507328 | tf_op jit(solution)/shard_map/sweep/pallas_call | solution.py:160
  37.4 0.1 collective-permute-start.9
  37.5 3.8 %collective-permute-start.6 = (bf16[2,256,128]{2,1,0:T(8,128)(2,1)S(1)}, bf16[2,256,128]{2,1,0:T(8,128)(2,1)S(1)}, u32[]{:S(2)}, u32[]{:S(2)}) collective-permute-start(bf16[2,256,128]{2,1,0:T(8,128)(2,1)S(1)} %sweep.3.refs_3_.refs_5_), channel_id=1, source_target_pairs={{16,0},{32,16},{48,32},{64,48},{80,64},{96,80},{112,96},{128,112},... | collective-permute-start | bytes 393224 | tf_op jit(solution)/shard_map/ppermute | solution.py:245
  41.3 0.5 collective-permute-start.8
  41.8 0.0 collective-permute-done.11.refs_7_
  41.8 5.7 %collective-permute-start.7 = (bf16[2,256,128]{2,1,0:T(8,128)(2,1)S(1)}, bf16[2,256,128]{2,1,0:T(8,128)(2,1)S(1)}, u32[]{:S(2)}, u32[]{:S(2)}) collective-permute-start(bf16[2,256,128]{2,1,0:T(8,128)(2,1)S(1)} %sweep.2.refs_4_.refs_3_), channel_id=1, source_target_pairs={{1,0},{2,1},{3,2},{4,3},{5,4},{6,5},{7,6},{8,7},{9,8},{10,9},{11,1... | collective-permute-start | bytes 393224 | tf_op jit(solution)/shard_map/ppermute | solution.py:245
  47.5 0.0 collective-permute-done.10.refs_6_
  47.6 0.0 collective-permute-done.9.refs_5_
  47.6 4.2 %prolong.2.refs_11_ = bf16[2,2,256,2048]{3,2,1,0:T(8,128)(2,1)} custom-call(s32[2,2]{1,0:T(2,128)} %refs_0_.7, s32[6,32]{1,0:T(8,128)} %bitcast.3, bf16[2,256,128]{2,1,0:T(8,128)(2,1)S(1)} %get-tuple-element.12.refs_2_, bf16[2,256,128]{2,1,0:T(8,128)(2,1)S(1)} %sweep.3.refs_3_.refs_5_, bf16[2,256,128]{2,1,0:T(8,128)(2,1)S(1)} %sweep.2.refs_4_.refs_3_, ...), custom_call_target="tpu_custom_call" | custom-call | flops 419430400 | bytes 4521984 | tf_op jit(solution)/shard_map/prolong/pallas_call | solution.py:221
  51.8 0.0 collective-permute-done.6.refs_4_
  51.8 0.6 %collective-permute-done.8.refs_7_ = bf16[2,256,128]{2,1,0:T(8,128)(2,1)S(1)} collective-permute-done((bf16[2,256,128]{2,1,0:T(8,128)(2,1)S(1)}, bf16[2,256,128]{2,1,0:T(8,128)(2,1)S(1)}, u32[]{:S(2)}, u32[]{:S(2)}) %collective-permute-start.8) | collective-permute-done | bytes 131104 | tf_op jit(solution)/shard_map/ppermute | solution.py:250
  52.5 0.0 collective-permute-done.7.refs_6_
  52.5 4.2 %prolong.3 = bf16[2,2,256,2048]{3,2,1,0:T(8,128)(2,1)} custom-call(s32[2,2]{1,0:T(2,128)} %refs_0_.7, s32[6,32]{1,0:T(8,128)} %bitcast.4, bf16[2,256,128]{2,1,0:T(8,128)(2,1)S(1)} %get-tuple-element.9.refs_2_, bf16[2,256,128]{2,1,0:T(8,128)(2,1)S(1)} %sweep.2.refs_4_.refs_3_, ...), custom_call_target="tpu_custom_call", output_to_operand_aliasing={{}: (11, {})} | custom-call | flops 419430400 | bytes 4521984 | tf_op jit(solution)/shard_map/prolong/pallas_call | solution.py:221
Async XLA Ops:
  4.7 16.6 %collective-permute-start.5 = (bf16[2,256,128]{2,1,0:T(8,128)(2,1)S(1)}, bf16[2,256,128]{2,1,0:T(8,128)(2,1)S(1)}, u32[]{:S(2)}, u32[]{:S(2)}) collective-permute-start(bf16[2,256,128]{2,1,0:T(8,128)(2,1)S(1)} %get-tuple-element.11.refs_5_.refs_3_), channel_id=1, source_target_pairs={{0,1},{1,2},{2,3},{3,4},{4,5},{5,6},{6,7},{7,8},{8,9},{9,10},{10,1... | collective-permute-start | bytes 393224 | tf_op jit(solution)/shard_map/ppermute | solution.py:250
  8.0 19.5 %collective-permute-start.4 = (bf16[2,256,128]{2,1,0:T(8,128)(2,1)S(1)}, bf16[2,256,128]{2,1,0:T(8,128)(2,1)S(1)}, u32[]{:S(2)}, u32[]{:S(2)}) collective-permute-start(bf16[2,256,128]{2,1,0:T(8,128)(2,1)S(1)} %get-tuple-element.11.refs_5_.refs_3_), channel_id=1, source_target_pairs={{1,0},{2,1},{3,2},{4,3},{5,4},{6,5},{7,6},{8,7},{9,8},{10,9},{11,1... | collective-permute-start | bytes 393224 | tf_op jit(solution)/shard_map/ppermute | solution.py:245
  17.3 10.2 %collective-permute-start.3 = (bf16[2,256,128]{2,1,0:T(8,128)(2,1)S(1)}, bf16[2,256,128]{2,1,0:T(8,128)(2,1)S(1)}, u32[]{:S(2)}, u32[]{:S(2)}) collective-permute-start(bf16[2,256,128]{2,1,0:T(8,128)(2,1)S(1)} %get-tuple-element.10.refs_3_.refs_4_), channel_id=1, source_target_pairs={{0,16},{16,32},{32,48},{48,64},{64,80},{80,96},{96,112},{112,128},... | collective-permute-start | bytes 393224 | tf_op jit(solution)/shard_map/ppermute | solution.py:250
  17.4 18.2 %collective-permute-start = (bf16[2,256,128]{2,1,0:T(8,128)(2,1)S(1)}, bf16[2,256,128]{2,1,0:T(8,128)(2,1)S(1)}, u32[]{:S(2)}, u32[]{:S(2)}) collective-permute-start(bf16[2,256,128]{2,1,0:T(8,128)(2,1)S(1)} %get-tuple-element.11.refs_5_.refs_3_), channel_id=1, source_target_pairs={{16,0},{32,16},{48,32},{64,48},{80,64},{96,80},{112,96},{128,112},... | collective-permute-start | bytes 393224 | tf_op jit(solution)/shard_map/ppermute | solution.py:245
  21.3 14.3 %collective-permute-start.2 = (bf16[2,256,128]{2,1,0:T(8,128)(2,1)S(1)}, bf16[2,256,128]{2,1,0:T(8,128)(2,1)S(1)}, u32[]{:S(2)}, u32[]{:S(2)}) collective-permute-start(bf16[2,256,128]{2,1,0:T(8,128)(2,1)S(1)} %get-tuple-element.10.refs_3_.refs_4_), channel_id=1, source_target_pairs={{0,1},{1,2},{2,3},{3,4},{4,5},{5,6},{6,7},{7,8},{8,9},{9,10},{10,1... | collective-permute-start | bytes 393224 | tf_op jit(solution)/shard_map/ppermute | solution.py:250
  21.3 14.3 %collective-permute-start.1 = (bf16[2,256,128]{2,1,0:T(8,128)(2,1)S(1)}, bf16[2,256,128]{2,1,0:T(8,128)(2,1)S(1)}, u32[]{:S(2)}, u32[]{:S(2)}) collective-permute-start(bf16[2,256,128]{2,1,0:T(8,128)(2,1)S(1)} %get-tuple-element.10.refs_3_.refs_4_), channel_id=1, source_target_pairs={{1,0},{2,1},{3,2},{4,3},{5,4},{6,5},{7,6},{8,7},{9,8},{10,9},{11,1... | collective-permute-start | bytes 393224 | tf_op jit(solution)/shard_map/ppermute | solution.py:245
  29.3 12.6 %collective-permute-start.11 = (bf16[2,256,128]{2,1,0:T(8,128)(2,1)S(1)}, bf16[2,256,128]{2,1,0:T(8,128)(2,1)S(1)}, u32[]{:S(2)}, u32[]{:S(2)}) collective-permute-start(bf16[2,256,128]{2,1,0:T(8,128)(2,1)S(1)} %sweep.3.refs_3_.refs_5_), channel_id=1, source_target_pairs={{0,1},{1,2},{2,3},{3,4},{4,5},{5,6},{6,7},{7,8},{8,9},{9,10},{10,1... | collective-permute-start | bytes 393224 | tf_op jit(solution)/shard_map/ppermute | solution.py:250
  29.4 18.2 %collective-permute-start.10 = (bf16[2,256,128]{2,1,0:T(8,128)(2,1)S(1)}, bf16[2,256,128]{2,1,0:T(8,128)(2,1)S(1)}, u32[]{:S(2)}, u32[]{:S(2)}) collective-permute-start(bf16[2,256,128]{2,1,0:T(8,128)(2,1)S(1)} %sweep.3.refs_3_.refs_5_), channel_id=1, source_target_pairs={{1,0},{2,1},{3,2},{4,3},{5,4},{6,5},{7,6},{8,7},{9,8},{10,9},{11,1... | collective-permute-start | bytes 393224 | tf_op jit(solution)/shard_map/ppermute | solution.py:245
  37.4 10.2 %collective-permute-start.9 = (bf16[2,256,128]{2,1,0:T(8,128)(2,1)S(1)}, bf16[2,256,128]{2,1,0:T(8,128)(2,1)S(1)}, u32[]{:S(2)}, u32[]{:S(2)}) collective-permute-start(bf16[2,256,128]{2,1,0:T(8,128)(2,1)S(1)} %sweep.2.refs_4_.refs_3_), channel_id=1, source_target_pairs={{0,16},{16,32},{32,48},{48,64},{64,80},{80,96},{96,112},{112,128},... | collective-permute-start | bytes 393224 | tf_op jit(solution)/shard_map/ppermute | solution.py:250
  37.5 14.4 %collective-permute-start.6 = (bf16[2,256,128]{2,1,0:T(8,128)(2,1)S(1)}, bf16[2,256,128]{2,1,0:T(8,128)(2,1)S(1)}, u32[]{:S(2)}, u32[]{:S(2)}) collective-permute-start(bf16[2,256,128]{2,1,0:T(8,128)(2,1)S(1)} %sweep.3.refs_3_.refs_5_), channel_id=1, source_target_pairs={{16,0},{32,16},{48,32},{64,48},{80,64},{96,80},{112,96},{128,112},... | collective-permute-start | bytes 393224 | tf_op jit(solution)/shard_map/ppermute | solution.py:245
  41.3 11.2 %collective-permute-start.8 = (bf16[2,256,128]{2,1,0:T(8,128)(2,1)S(1)}, bf16[2,256,128]{2,1,0:T(8,128)(2,1)S(1)}, u32[]{:S(2)}, u32[]{:S(2)}) collective-permute-start(bf16[2,256,128]{2,1,0:T(8,128)(2,1)S(1)} %sweep.2.refs_4_.refs_3_), channel_id=1, source_target_pairs={{0,1},{1,2},{2,3},{3,4},{4,5},{5,6},{6,7},{7,8},{8,9},{9,10},{10,1... | collective-permute-start | bytes 393224 | tf_op jit(solution)/shard_map/ppermute | solution.py:250
  41.8 10.6 %collective-permute-start.7 = (bf16[2,256,128]{2,1,0:T(8,128)(2,1)S(1)}, bf16[2,256,128]{2,1,0:T(8,128)(2,1)S(1)}, u32[]{:S(2)}, u32[]{:S(2)}) collective-permute-start(bf16[2,256,128]{2,1,0:T(8,128)(2,1)S(1)} %sweep.2.refs_4_.refs_3_), channel_id=1, source_target_pairs={{1,0},{2,1},{3,2},{4,3},{5,4},{6,5},{7,6},{8,7},{9,8},{10,9},{11,1... | collective-permute-start | bytes 393224 | tf_op jit(solution)/shard_map/ppermute | solution.py:245

commit v3 on v2

v3 whole, which is shorter than its diff:
```python
import functools

import jax
import jax.numpy as jnp
from jax import lax
from jax.experimental import pallas as pl
from jax.experimental.pallas import tpu as pltpu
from jax.sharding import PartitionSpec as P

DAMPING = 0.8
KEEP = 1.0 - DAMPING
BF16 = jnp.bfloat16
F32 = jnp.float32
PIECES = 2
HBM = pl.BlockSpec(memory_space=pltpu.HBM)
VMEM = pl.BlockSpec(memory_space=pltpu.VMEM)
PARAMS = pltpu.CompilerParams(vmem_limit_bytes=32 * 1024 * 1024)


def in_hbm(x):
    return pltpu.with_memory_space_constraint(x, pltpu.HBM)


def in_vmem(x):
    return pltpu.with_memory_space_constraint(x, pltpu.VMEM)


def dot(a, b):
    return jnp.dot(a, b, preferred_element_type=F32)


class Copies:
    def __init__(self, sems):
        self.sems = sems
        self.count = 0

    def start(self, src, dst):
        copy = pltpu.make_async_copy(src, dst, self.sems.at[self.count])
        self.count += 1
        copy.start()
        return copy


def restrict_kernel(agg, nbr, fine, basis, dinv, hops, *refs):
    nt, ns, _, nf = fine.shape
    rhs, e = refs[:nt], refs[nt : 2 * nt]
    basis_v, dinv_v = refs[2 * nt : 2 * nt + 2]
    hops_v = refs[2 * nt + 2 : 3 * nt + 2]
    agg_s, nbr_s, fine_v, sems = refs[3 * nt + 2 :]
    depth = nf // PIECES
    copies = Copies(sems)
    agg_in = copies.start(agg, agg_s)
    nbr_in = copies.start(nbr, nbr_s)
    loads = {}
    for t in range(nt):
        for s in range(ns):
            pieces = PIECES if (t, s) == (0, 0) else 1
            depth = nf // pieces
            for p in range(pieces):
                part = pl.ds(p * depth, depth)
                loads[t, s, p] = (
                    copies.start(basis.at[t, s, part], basis_v.at[t, s, part]),
                    copies.start(fine.at[t, s, :, part], fine_v.at[t, s, :, part]),
                )
    dinv_in = copies.start(dinv, dinv_v)
    agg_in.wait()
    nbr_in.wait()
    hops_in = []
    for t in range(nt):
        for c in range(ns):
            spatial = nbr_s.shape[1]
            site = (agg_s[0, 0] & -2) + c
            upward = (nbr_s[0, site] == lax.rem(site + 2, spatial)).astype(jnp.int32)
            hops_in.append(copies.start(hops.at[t, c, 1 - upward], hops_v[t].at[c, 0]))
            hops_in.append(copies.start(hops.at[t, c, upward], hops_v[t].at[c, 1]))
            rest = pl.ds(2, 6)
            hops_in.append(copies.start(hops.at[t, c, rest], hops_v[t].at[c, rest]))
    for t in range(nt):
        for s in range(ns):
            c = agg_s[t, s] & 1
            pieces = PIECES if (t, s) == (0, 0) else 1
            depth = nf // pieces
            total = None
            for p in range(pieces):
                for load in loads[t, s, p]:
                    load.wait()
                part = pl.ds(p * depth, depth)
                term = dot(fine_v[t, s, :, part], basis_v[t, s, part])
                total = term if total is None else total + term
            r = total.astype(BF16)
            if (t, s) == (0, 0):
                dinv_in.wait()
            rhs[t][c] = r
            e[t][c] = (DAMPING * dot(r, dinv_v[t, c])).astype(BF16)
    for load in hops_in:
        load.wait()


def restrict(agg, nbr, fine, basis, dinv, hops):
    nt, ns, n, nf = fine.shape
    nc = basis.shape[3]
    part = pltpu.VMEM((ns, n, nc), BF16)
    out_shape = [
        *[part] * (2 * nt),
        pltpu.VMEM(basis.shape, BF16),
        pltpu.VMEM(dinv.shape, BF16),
        *[pltpu.VMEM(hops.shape[1:], BF16)] * nt,
    ]
    out = pl.pallas_call(
        restrict_kernel,
        in_specs=[HBM] * 6,
        out_specs=[VMEM] * len(out_shape),
        out_shape=out_shape,
        scratch_shapes=[
            pltpu.SMEM(agg.shape, jnp.int32),
            pltpu.SMEM(nbr.shape, jnp.int32),
            pltpu.VMEM(fine.shape, BF16),
            pltpu.SemaphoreType.DMA((3 + 2 * (nt * ns + PIECES - 1) + 3 * nt * ns,)),
        ],
        compiler_params=PARAMS,
        cost_estimate=pl.CostEstimate(
            flops=2 * nt * ns * n * nc * (nf + nc),
            bytes_accessed=2 * nt * ns * (n * nf + nf * nc + 9 * nc * nc),
            transcendentals=0,
        ),
        name="restrict",
    )(*map(in_hbm, (agg, nbr, fine, basis, dinv, hops)))
    return out[:nt], out[nt : 2 * nt], out[2 * nt], out[2 * nt + 1], out[2 * nt + 2 :]


def next_iterate(c, rhs, e, later, earlier, up, dn, hops, dinv):
    ns, _, nc = e.shape
    own, other = e[c], e[ns - 1 - c]
    stacked = jnp.concatenate(
        [up[c], dn[c], own, own, other, other, later[c], earlier[c]], axis=1
    )
    hop = dot(stacked, hops[c].reshape(8 * nc, nc))
    difference = (rhs[c].astype(F32) - hop).astype(BF16)
    return (KEEP * own.astype(F32) + DAMPING * dot(difference, dinv[c])).astype(BF16)


def sweep_kernel(t, *refs):
    hops, dinv, out = refs[6:]
    for c in range(out.shape[0]):
        out[c] = next_iterate(c, *refs[:6], hops, dinv.at[t])


def sweep(t, coarse, hops, dinv):
    shape = coarse[0].shape
    ns, n, nc = shape
    return pl.pallas_call(
        functools.partial(sweep_kernel, t),
        in_specs=[VMEM] * 8,
        out_specs=VMEM,
        out_shape=pltpu.VMEM(shape, BF16),
        compiler_params=PARAMS,
        cost_estimate=pl.CostEstimate(
            flops=2 * ns * n * nc * 9 * nc,
            bytes_accessed=2 * ns * (9 * nc * nc + 7 * n * nc),
            transcendentals=0,
        ),
        name="sweep",
    )(*map(in_vmem, (*coarse, hops, dinv)))


def prolong_kernel(t, *refs):
    hops, dinv, basis, agg = refs[6:10]
    out, agg_s, value_v, out_v, sems = refs[len(refs) - 5 :]
    ns, n, nf = out_v.shape
    width = nf // PIECES
    copies = Copies(sems)
    agg_in = copies.start(agg, agg_s)
    for c in range(ns):
        value_v[c] = next_iterate(c, *refs[:6], hops, dinv.at[t])
    agg_in.wait()
    outs = []
    for s in range(ns):
        value = value_v[agg_s[t, s] & 1]
        for p in range(PIECES):
            part = pl.ds(p * width, width)
            out_v[s, :, part] = lax.dot_general(
                value, basis[t, s, part], (((1,), (1,)), ((), ())), preferred_element_type=F32
            ).astype(BF16)
            outs.append(copies.start(out_v.at[s, :, part], out.at[t, s, :, part]))
    for wait in outs:
        wait.wait()


def prolong(t, shape, agg, coarse, hops, dinv, basis, previous):
    part = coarse[0].shape
    ns, n, nc = part
    nf = basis.shape[2]
    operands = [*map(in_vmem, (*coarse, hops, dinv, basis)), in_hbm(agg)]
    in_specs = [VMEM] * 9 + [HBM]
    aliases = {}
    if previous is not None:
        aliases = {len(operands): 0}
        operands.append(in_hbm(previous))
        in_specs.append(HBM)
    return pl.pallas_call(
        functools.partial(prolong_kernel, t),
        in_specs=in_specs,
        out_specs=HBM,
        out_shape=pltpu.HBM(shape, BF16),
        input_output_aliases=aliases,
        scratch_shapes=[
            pltpu.SMEM(agg.shape, jnp.int32),
            pltpu.VMEM(part, BF16),
            pltpu.VMEM((ns, n, nf), BF16),
            pltpu.SemaphoreType.DMA((1 + ns * PIECES,)),
        ],
        compiler_params=PARAMS,
        cost_estimate=pl.CostEstimate(
            flops=2 * ns * n * nc * (9 * nc + nf),
            bytes_accessed=2 * ns * (9 * nc * nc + 6 * n * nc + nf * nc + n * nf),
            transcendentals=0,
        ),
        name="prolong",
    )(*operands)


def from_next(x, axis):
    count = lax.axis_size(axis)
    return lax.ppermute(x, axis, [((i + 1) % count, i) for i in range(count)])


def from_previous(x, axis):
    count = lax.axis_size(axis)
    return lax.ppermute(x, axis, [(i, (i + 1) % count) for i in range(count)])


def halos(e):
    first, last = e[0], e[-1]
    beyond = from_next(first, "lat")
    before = from_previous(last, "lat")
    spatial = [(from_next(x, "src"), from_previous(x, "src")) for x in e]
    later = [*e[1:], beyond]
    earlier = [before, *e[:-1]]
    return [(e[t], later[t], earlier[t], *spatial[t]) for t in range(len(e))]


def body(fine, basis, dinv, hops, nbr, agg):
    slices = range(fine.shape[0])
    rhs, e, basis, dinv, hops = restrict(agg, nbr.T, fine, basis, dinv, hops)
    around = halos(e)
    e = [sweep(t, (rhs[t], *around[t]), hops[t], dinv) for t in slices]
    around = halos(e)
    out = None
    for t in slices:
        out = prolong(t, fine.shape, agg, (rhs[t], *around[t]), hops[t], dinv, basis, out)
    return out


def solution(mesh):
    return jax.shard_map(
        body,
        mesh=mesh,
        in_specs=(
            P("lat", "src", None, None),
            P("lat", "src", None, None),
            P("lat", "src", None, None),
            P("lat", "src", None, None, None),
            P(),
            P("lat", "src"),
        ),
        out_specs=P("lat", "src", None, None),
        check_vma=False,
    )
```

time: 57 us -> 46.8 us (0.82)
  the two profiles are of different devices: /device:TPU:32 before, /device:TPU:3 now
where the time goes in v3:
time: 46.8 us; the launch traced here: 46.6 us
  starting transfers between devices  26.5 us (57%)
  Pallas kernels  10.8 us (23%)
  waiting for transfers between devices  9.23 us (20%)
    ppermute x6, starting transfers between devices, from_next(): return lax.ppermute(x, axis, [((i + 1) % count, i) for i in range(count)])  16.9 us
    ppermute x6, starting transfers between devices, from_previous(): return lax.ppermute(x, axis, [(i, (i + 1) % count) for i in range(count)])  9.68 us
    ppermute x6, waiting for transfers between devices, from_previous(): return lax.ppermute(x, axis, [(i, (i + 1) % count) for i in range(count)])  6.56 us
    pallas_call x1, Pallas kernels, restrict(): pl.pallas_call(restrict_kernel, in_specs=[HBM] * 6, out_specs=[VMEM] * le...  4.82 us
    pallas_call x2, Pallas kernels, prolong(): pl.pallas_call(functools.partial(prolong_kernel, t), in_specs=in_specs, o...  4.67 us
    ppermute x6, waiting for transfers between devices, from_next(): return lax.ppermute(x, axis, [((i + 1) % count, i) for i in range(count)])  2.67 us
    pallas_call x2, Pallas kernels, sweep(): pl.pallas_call(functools.partial(sweep_kernel, t), in_specs=[VMEM] * 8, o...  1.32 us
  transfers between devices with their start and end apart: 12, of which 3 were waited for; matrix products, arithmetic and copies ran while one was open for 0% of the time, Pallas kernels for 8%

profile of v3, /device:TPU:3, one launch (start us, length us, event | category | flops | bytes accessed | tf_op | source)
XLA Modules:
  0.0 46.6 jit_solution(12985710955287059222)
XLA Ops:
  0.0 4.8 %restrict.1 = (bf16[2,256,128]{2,1,0:T(8,128)(2,1)S(1)}, bf16[2,256,128]{2,1,0:T(8,128)(2,1)S(1)}, bf16[2,256,128]{2,1,0:T(8,128)(2,1)S(1)}, bf16[2,256,128]{2,1...) custom-call(s32[2,2]{1,0:T(2,128)} %refs_9_.3, ...), custom_call_target="tpu_custom_call" | custom-call | flops 570425344 | bytes 7471104 | tf_op jit(solution)/shard_map/restrict/pallas_call | solution.py:109
  4.8 1.8 %collective-permute-start.3 = (bf16[2,256,128]{2,1,0:T(8,128)(2,1)S(1)}, bf16[2,256,128]{2,1,0:T(8,128)(2,1)S(1)}, u32[]{:S(2)}, u32[]{:S(2)}) collective-permute-start(bf16[2,256,128]{2,1,0:T(8,128)(2,1)S(1)} %get-tuple-element.14.refs_1_.refs_2_), channel_id=1, source_target_pairs={{0,16},{16,32},{32,48},{48,64},{64,80},{80,96},{96,112},{112,128},... | collective-permute-start | bytes 393224 | tf_op jit(solution)/shard_map/ppermute | solution.py:229
  6.7 3.0 %collective-permute-start.5 = (bf16[2,256,128]{2,1,0:T(8,128)(2,1)S(1)}, bf16[2,256,128]{2,1,0:T(8,128)(2,1)S(1)}, u32[]{:S(2)}, u32[]{:S(2)}) collective-permute-start(bf16[2,256,128]{2,1,0:T(8,128)(2,1)S(1)} %get-tuple-element.15.refs_3_.refs_1_), channel_id=1, source_target_pairs={{0,1},{1,2},{2,3},{3,4},{4,5},{5,6},{6,7},{7,8},{8,9},{9,10},{10,1... | collective-permute-start | bytes 393224 | tf_op jit(solution)/shard_map/ppermute | solution.py:229
  9.7 5.5 %collective-permute-start.4 = (bf16[2,256,128]{2,1,0:T(8,128)(2,1)S(1)}, bf16[2,256,128]{2,1,0:T(8,128)(2,1)S(1)}, u32[]{:S(2)}, u32[]{:S(2)}) collective-permute-start(bf16[2,256,128]{2,1,0:T(8,128)(2,1)S(1)} %get-tuple-element.15.refs_3_.refs_1_), channel_id=1, source_target_pairs={{1,0},{2,1},{3,2},{4,3},{5,4},{6,5},{7,6},{8,7},{9,8},{10,9},{11,1... | collective-permute-start | bytes 393224 | tf_op jit(solution)/shard_map/ppermute | solution.py:224
  15.2 0.0 collective-permute-start.2
  15.2 5.7 %collective-permute-start.1 = (bf16[2,256,128]{2,1,0:T(8,128)(2,1)S(1)}, bf16[2,256,128]{2,1,0:T(8,128)(2,1)S(1)}, u32[]{:S(2)}, u32[]{:S(2)}) collective-permute-start(bf16[2,256,128]{2,1,0:T(8,128)(2,1)S(1)} %get-tuple-element.14.refs_1_.refs_2_), channel_id=1, source_target_pairs={{1,0},{2,1},{3,2},{4,3},{5,4},{6,5},{7,6},{8,7},{9,8},{10,9},{11,1... | collective-permute-start | bytes 393224 | tf_op jit(solution)/shard_map/ppermute | solution.py:224
  20.8 0.0 collective-permute-done.3.refs_3_
  20.8 0.0 collective-permute-start
  20.8 0.0 collective-permute-done.5.refs_5_
  20.8 2.7 %collective-permute-done.4.refs_4_ = bf16[2,256,128]{2,1,0:T(8,128)(2,1)S(1)} collective-permute-done((bf16[2,256,128]{2,1,0:T(8,128)(2,1)S(1)}, bf16[2,256,128]{2,1,0:T(8,128)(2,1)S(1)}, u32[]{:S(2)}, u32[]{:S(2)}) %collective-permute-start.4) | collective-permute-done | bytes 131104 | tf_op jit(solution)/shard_map/ppermute | solution.py:224
  23.5 0.7 %sweep.3.refs_1_.refs_3_ = bf16[2,256,128]{2,1,0:T(8,128)(2,1)S(1)} custom-call(bf16[2,256,128]{2,1,0:T(8,128)(2,1)S(1)} %get-tuple-element.18.refs_0_, bf16[2,256,128]{2,1,0:T(8,128)(2,1)S(1)} %get-tuple-element.15.refs_3_.refs_1_, bf16[2,256,128]{2,1,0:T(8,128)(2,1)S(1)} %get-tuple-element.14.refs_1_.refs_2_, ...), custom_call_target="tpu_custom_call" | custom-call | flops 150994944 | bytes 1507328 | tf_op jit(solution)/shard_map/sweep/pallas_call | solution.py:151
  24.2 3.0 %collective-permute-start.11 = (bf16[2,256,128]{2,1,0:T(8,128)(2,1)S(1)}, bf16[2,256,128]{2,1,0:T(8,128)(2,1)S(1)}, u32[]{:S(2)}, u32[]{:S(2)}) collective-permute-start(bf16[2,256,128]{2,1,0:T(8,128)(2,1)S(1)} %sweep.3.refs_1_.refs_3_), channel_id=1, source_target_pairs={{0,1},{1,2},{2,3},{3,4},{4,5},{5,6},{6,7},{7,8},{8,9},{9,10},{10,1... | collective-permute-start | bytes 393224 | tf_op jit(solution)/shard_map/ppermute | solution.py:229
  27.2 2.7 %collective-permute-start.10 = (bf16[2,256,128]{2,1,0:T(8,128)(2,1)S(1)}, bf16[2,256,128]{2,1,0:T(8,128)(2,1)S(1)}, u32[]{:S(2)}, u32[]{:S(2)}) collective-permute-start(bf16[2,256,128]{2,1,0:T(8,128)(2,1)S(1)} %sweep.3.refs_1_.refs_3_), channel_id=1, source_target_pairs={{1,0},{2,1},{3,2},{4,3},{5,4},{6,5},{7,6},{8,7},{9,8},{10,9},{11,1... | collective-permute-start | bytes 393224 | tf_op jit(solution)/shard_map/ppermute | solution.py:224
  29.9 0.0 collective-permute-done.2.refs_5_
  29.9 0.0 collective-permute-done.1.refs_4_
  29.9 0.0 collective-permute-done.refs_2_
  29.9 0.7 %sweep.2.refs_2_.refs_1_ = bf16[2,256,128]{2,1,0:T(8,128)(2,1)S(1)} custom-call(bf16[2,256,128]{2,1,0:T(8,128)(2,1)S(1)} %get-tuple-element.13.refs_0_, bf16[2,256,128]{2,1,0:T(8,128)(2,1)S(1)} %get-tuple-element.14.refs_1_.refs_2_, bf16[2,256,128]{2,1,0:T(8,128)(2,1)S(1)} %collective-permute-done.refs_2_, ...), custom_call_target="tpu_custom_call" | custom-call | flops 150994944 | bytes 1507328 | tf_op jit(solution)/shard_map/sweep/pallas_call | solution.py:151
  30.6 1.4 %collective-permute-start.9 = (bf16[2,256,128]{2,1,0:T(8,128)(2,1)S(1)}, bf16[2,256,128]{2,1,0:T(8,128)(2,1)S(1)}, u32[]{:S(2)}, u32[]{:S(2)}) collective-permute-start(bf16[2,256,128]{2,1,0:T(8,128)(2,1)S(1)} %sweep.2.refs_2_.refs_1_), channel_id=1, source_target_pairs={{0,16},{16,32},{32,48},{48,64},{64,80},{80,96},{96,112},{112,128},... | collective-permute-start | bytes 393224 | tf_op jit(solution)/shard_map/ppermute | solution.py:229
  32.0 0.0 collective-permute-start.6
  32.0 0.4 collective-permute-start.8
  32.4 2.3 %collective-permute-done.11.refs_5_ = bf16[2,256,128]{2,1,0:T(8,128)(2,1)S(1)} collective-permute-done((bf16[2,256,128]{2,1,0:T(8,128)(2,1)S(1)}, bf16[2,256,128]{2,1,0:T(8,128)(2,1)S(1)}, u32[]{:S(2)}, u32[]{:S(2)}) %collective-permute-start.11) | collective-permute-done | bytes 131104 | tf_op jit(solution)/shard_map/ppermute | solution.py:229
  34.8 3.0 %collective-permute-start.7 = (bf16[2,256,128]{2,1,0:T(8,128)(2,1)S(1)}, bf16[2,256,128]{2,1,0:T(8,128)(2,1)S(1)}, u32[]{:S(2)}, u32[]{:S(2)}) collective-permute-start(bf16[2,256,128]{2,1,0:T(8,128)(2,1)S(1)} %sweep.2.refs_2_.refs_1_), channel_id=1, source_target_pairs={{1,0},{2,1},{3,2},{4,3},{5,4},{6,5},{7,6},{8,7},{9,8},{10,9},{11,1... | collective-permute-start | bytes 393224 | tf_op jit(solution)/shard_map/ppermute | solution.py:224
  37.7 0.0 collective-permute-done.10.refs_4_
  37.7 0.0 collective-permute-done.9.refs_3_
  37.7 2.3 %prolong.2.refs_10_ = bf16[2,2,256,2048]{3,2,1,0:T(8,128)(2,1)} custom-call(bf16[2,256,128]{2,1,0:T(8,128)(2,1)S(1)} %get-tuple-element.18.refs_0_, bf16[2,256,128]{2,1,0:T(8,128)(2,1)S(1)} %sweep.3.refs_1_.refs_3_, bf16[2,256,128]{2,1,0:T(8,128)(2,1)S(1)} %sweep.2.refs_2_.refs_1_, bf16[2,256,128]{2,1,0:T(8,128)(2,1)S(1)} %collective-permute-done.9.refs_3_, ...), custom_call_target="tpu_custom_call" | custom-call | flops 419430400 | bytes 4521984 | tf_op jit(solution)/shard_map/prolong/pallas_call | solution.py:200
  40.1 0.0 collective-permute-done.6.refs_2_
  40.1 4.2 %collective-permute-done.8.refs_5_ = bf16[2,256,128]{2,1,0:T(8,128)(2,1)S(1)} collective-permute-done((bf16[2,256,128]{2,1,0:T(8,128)(2,1)S(1)}, bf16[2,256,128]{2,1,0:T(8,128)(2,1)S(1)}, u32[]{:S(2)}, u32[]{:S(2)}) %collective-permute-start.8) | collective-permute-done | bytes 131104 | tf_op jit(solution)/shard_map/ppermute | solution.py:229
  44.3 0.0 collective-permute-done.7.refs_4_
  44.3 2.3 %prolong.3 = bf16[2,2,256,2048]{3,2,1,0:T(8,128)(2,1)} custom-call(bf16[2,256,128]{2,1,0:T(8,128)(2,1)S(1)} %get-tuple-element.13.refs_0_, bf16[2,256,128]{2,1,0:T(8,128)(2,1)S(1)} %sweep.2.refs_2_.refs_1_, bf16[2,256,128]{2,1,0:T(8,128)(2,1)S(1)} %collective-permute-done.6.refs_2_, ...), custom_call_target="tpu_custom_call", output_to_operand_aliasing={{}: (10, {})} | custom-call | flops 419430400 | bytes 4521984 | tf_op jit(solution)/shard_map/prolong/pallas_call | solution.py:200
Async XLA Ops:
  4.8 16.0 %collective-permute-start.3 = (bf16[2,256,128]{2,1,0:T(8,128)(2,1)S(1)}, bf16[2,256,128]{2,1,0:T(8,128)(2,1)S(1)}, u32[]{:S(2)}, u32[]{:S(2)}) collective-permute-start(bf16[2,256,128]{2,1,0:T(8,128)(2,1)S(1)} %get-tuple-element.14.refs_1_.refs_2_), channel_id=1, source_target_pairs={{0,16},{16,32},{32,48},{48,64},{64,80},{80,96},{96,112},{112,128},... | collective-permute-start | bytes 393224 | tf_op jit(solution)/shard_map/ppermute | solution.py:229
  6.7 14.2 %collective-permute-start.5 = (bf16[2,256,128]{2,1,0:T(8,128)(2,1)S(1)}, bf16[2,256,128]{2,1,0:T(8,128)(2,1)S(1)}, u32[]{:S(2)}, u32[]{:S(2)}) collective-permute-start(bf16[2,256,128]{2,1,0:T(8,128)(2,1)S(1)} %get-tuple-element.15.refs_3_.refs_1_), channel_id=1, source_target_pairs={{0,1},{1,2},{2,3},{3,4},{4,5},{5,6},{6,7},{7,8},{8,9},{9,10},{10,1... | collective-permute-start | bytes 393224 | tf_op jit(solution)/shard_map/ppermute | solution.py:229
  9.7 13.8 %collective-permute-start.4 = (bf16[2,256,128]{2,1,0:T(8,128)(2,1)S(1)}, bf16[2,256,128]{2,1,0:T(8,128)(2,1)S(1)}, u32[]{:S(2)}, u32[]{:S(2)}) collective-permute-start(bf16[2,256,128]{2,1,0:T(8,128)(2,1)S(1)} %get-tuple-element.15.refs_3_.refs_1_), channel_id=1, source_target_pairs={{1,0},{2,1},{3,2},{4,3},{5,4},{6,5},{7,6},{8,7},{9,8},{10,9},{11,1... | collective-permute-start | bytes 393224 | tf_op jit(solution)/shard_map/ppermute | solution.py:224
  15.2 14.8 %collective-permute-start.2 = (bf16[2,256,128]{2,1,0:T(8,128)(2,1)S(1)}, bf16[2,256,128]{2,1,0:T(8,128)(2,1)S(1)}, u32[]{:S(2)}, u32[]{:S(2)}) collective-permute-start(bf16[2,256,128]{2,1,0:T(8,128)(2,1)S(1)} %get-tuple-element.14.refs_1_.refs_2_), channel_id=1, source_target_pairs={{0,1},{1,2},{2,3},{3,4},{4,5},{5,6},{6,7},{7,8},{8,9},{9,10},{10,1... | collective-permute-start | bytes 393224 | tf_op jit(solution)/shard_map/ppermute | solution.py:229
  15.2 14.8 %collective-permute-start.1 = (bf16[2,256,128]{2,1,0:T(8,128)(2,1)S(1)}, bf16[2,256,128]{2,1,0:T(8,128)(2,1)S(1)}, u32[]{:S(2)}, u32[]{:S(2)}) collective-permute-start(bf16[2,256,128]{2,1,0:T(8,128)(2,1)S(1)} %get-tuple-element.14.refs_1_.refs_2_), channel_id=1, source_target_pairs={{1,0},{2,1},{3,2},{4,3},{5,4},{6,5},{7,6},{8,7},{9,8},{10,9},{11,1... | collective-permute-start | bytes 393224 | tf_op jit(solution)/shard_map/ppermute | solution.py:224
  20.8 9.1 %collective-permute-start = (bf16[2,256,128]{2,1,0:T(8,128)(2,1)S(1)}, bf16[2,256,128]{2,1,0:T(8,128)(2,1)S(1)}, u32[]{:S(2)}, u32[]{:S(2)}) collective-permute-start(bf16[2,256,128]{2,1,0:T(8,128)(2,1)S(1)} %get-tuple-element.15.refs_3_.refs_1_), channel_id=1, source_target_pairs={{16,0},{32,16},{48,32},{64,48},{80,64},{96,80},{112,96},{128,112},... | collective-permute-start | bytes 393224 | tf_op jit(solution)/shard_map/ppermute | solution.py:224
  24.2 10.6 %collective-permute-start.11 = (bf16[2,256,128]{2,1,0:T(8,128)(2,1)S(1)}, bf16[2,256,128]{2,1,0:T(8,128)(2,1)S(1)}, u32[]{:S(2)}, u32[]{:S(2)}) collective-permute-start(bf16[2,256,128]{2,1,0:T(8,128)(2,1)S(1)} %sweep.3.refs_1_.refs_3_), channel_id=1, source_target_pairs={{0,1},{1,2},{2,3},{3,4},{4,5},{5,6},{6,7},{7,8},{8,9},{9,10},{10,1... | collective-permute-start | bytes 393224 | tf_op jit(solution)/shard_map/ppermute | solution.py:229
  27.2 10.5 %collective-permute-start.10 = (bf16[2,256,128]{2,1,0:T(8,128)(2,1)S(1)}, bf16[2,256,128]{2,1,0:T(8,128)(2,1)S(1)}, u32[]{:S(2)}, u32[]{:S(2)}) collective-permute-start(bf16[2,256,128]{2,1,0:T(8,128)(2,1)S(1)} %sweep.3.refs_1_.refs_3_), channel_id=1, source_target_pairs={{1,0},{2,1},{3,2},{4,3},{5,4},{6,5},{7,6},{8,7},{9,8},{10,9},{11,1... | collective-permute-start | bytes 393224 | tf_op jit(solution)/shard_map/ppermute | solution.py:224
  30.6 7.1 %collective-permute-start.9 = (bf16[2,256,128]{2,1,0:T(8,128)(2,1)S(1)}, bf16[2,256,128]{2,1,0:T(8,128)(2,1)S(1)}, u32[]{:S(2)}, u32[]{:S(2)}) collective-permute-start(bf16[2,256,128]{2,1,0:T(8,128)(2,1)S(1)} %sweep.2.refs_2_.refs_1_), channel_id=1, source_target_pairs={{0,16},{16,32},{32,48},{48,64},{64,80},{80,96},{96,112},{112,128},... | collective-permute-start | bytes 393224 | tf_op jit(solution)/shard_map/ppermute | solution.py:229
  32.0 8.0 %collective-permute-start.6 = (bf16[2,256,128]{2,1,0:T(8,128)(2,1)S(1)}, bf16[2,256,128]{2,1,0:T(8,128)(2,1)S(1)}, u32[]{:S(2)}, u32[]{:S(2)}) collective-permute-start(bf16[2,256,128]{2,1,0:T(8,128)(2,1)S(1)} %sweep.3.refs_1_.refs_3_), channel_id=1, source_target_pairs={{16,0},{32,16},{48,32},{64,48},{80,64},{96,80},{112,96},{128,112},... | collective-permute-start | bytes 393224 | tf_op jit(solution)/shard_map/ppermute | solution.py:224
  32.0 12.3 %collective-permute-start.8 = (bf16[2,256,128]{2,1,0:T(8,128)(2,1)S(1)}, bf16[2,256,128]{2,1,0:T(8,128)(2,1)S(1)}, u32[]{:S(2)}, u32[]{:S(2)}) collective-permute-start(bf16[2,256,128]{2,1,0:T(8,128)(2,1)S(1)} %sweep.2.refs_2_.refs_1_), channel_id=1, source_target_pairs={{0,1},{1,2},{2,3},{3,4},{4,5},{5,6},{6,7},{7,8},{8,9},{9,10},{10,1... | collective-permute-start | bytes 393224 | tf_op jit(solution)/shard_map/ppermute | solution.py:229
  34.8 9.5 %collective-permute-start.7 = (bf16[2,256,128]{2,1,0:T(8,128)(2,1)S(1)}, bf16[2,256,128]{2,1,0:T(8,128)(2,1)S(1)}, u32[]{:S(2)}, u32[]{:S(2)}) collective-permute-start(bf16[2,256,128]{2,1,0:T(8,128)(2,1)S(1)} %sweep.2.refs_2_.refs_1_), channel_id=1, source_target_pairs={{1,0},{2,1},{3,2},{4,3},{5,4},{6,5},{7,6},{8,7},{9,8},{10,9},{11,1... | collective-permute-start | bytes 393224 | tf_op jit(solution)/shard_map/ppermute | solution.py:224

commit v4 on v3

--- a/solution.py
+++ b/solution.py
@@ -51,6 +51,7 @@
     copies = Copies(sems)
     agg_in = copies.start(agg, agg_s)
     nbr_in = copies.start(nbr, nbr_s)
+    dinv_in = copies.start(dinv, dinv_v)
     loads = {}
     for t in range(nt):
         for s in range(ns):
@@ -62,17 +63,18 @@
                     copies.start(basis.at[t, s, part], basis_v.at[t, s, part]),
                     copies.start(fine.at[t, s, :, part], fine_v.at[t, s, :, part]),
                 )
-    dinv_in = copies.start(dinv, dinv_v)
     agg_in.wait()
     nbr_in.wait()
+    lane = lax.axis_index("lat")
     hops_in = []
     for t in range(nt):
         for c in range(ns):
             spatial = nbr_s.shape[1]
             site = (agg_s[0, 0] & -2) + c
-            upward = (nbr_s[0, site] == lax.rem(site + 2, spatial)).astype(jnp.int32)
-            hops_in.append(copies.start(hops.at[t, c, 1 - upward], hops_v[t].at[c, 0]))
-            hops_in.append(copies.start(hops.at[t, c, upward], hops_v[t].at[c, 1]))
+            down_first = (nbr_s[0, site] != lax.rem(site + 2, spatial)).astype(jnp.int32)
+            even = down_first ^ (((site >> 1) + lane) & 1)
+            hops_in.append(copies.start(hops.at[t, c, even], hops_v[t].at[c, 0]))
+            hops_in.append(copies.start(hops.at[t, c, 1 - even], hops_v[t].at[c, 1]))
             rest = pl.ds(2, 6)
             hops_in.append(copies.start(hops.at[t, c, rest], hops_v[t].at[c, rest]))
     for t in range(nt):
@@ -128,11 +130,11 @@
     return out[:nt], out[nt : 2 * nt], out[2 * nt], out[2 * nt + 1], out[2 * nt + 2 :]
 
 
-def next_iterate(c, rhs, e, later, earlier, up, dn, hops, dinv):
+def next_iterate(c, rhs, e, later, earlier, even, odd, hops, dinv):
     ns, _, nc = e.shape
     own, other = e[c], e[ns - 1 - c]
     stacked = jnp.concatenate(
-        [up[c], dn[c], own, own, other, other, later[c], earlier[c]], axis=1
+        [even[c], odd[c], own, own, other, other, later[c], earlier[c]], axis=1
     )
     hop = dot(stacked, hops[c].reshape(8 * nc, nc))
     difference = (rhs[c].astype(F32) - hop).astype(BF16)
@@ -229,11 +231,18 @@
     return lax.ppermute(x, axis, [(i, (i + 1) % count) for i in range(count)])
 
 
+def swap_sites(x, offset):
+    axes = ("lat", "src")
+    nt, count = (lax.axis_size(a) for a in axes)
+    step = lambda l, s: (s + 1 - 2 * ((l + s + offset) % 2)) % count
+    pairs = [(l * count + s, l * count + step(l, s)) for l in range(nt) for s in range(count)]
+    return lax.ppermute(x, axes, pairs)
+
+
 def halos(e):
-    first, last = e[0], e[-1]
-    beyond = from_next(first, "lat")
-    before = from_previous(last, "lat")
-    spatial = [(from_next(x, "src"), from_previous(x, "src")) for x in e]
+    spatial = [(swap_sites(x, 0), swap_sites(x, 1)) for x in e]
+    beyond = from_next(e[0], "lat")
+    before = from_previous(e[-1], "lat")
     later = [*e[1:], beyond]
     earlier = [before, *e[:-1]]
     return [(e[t], later[t], earlier[t], *spatial[t]) for t in range(len(e))]

time: 46.8 us -> 45.8 us (0.979)
  the two profiles are of different devices: /device:TPU:3 before, /device:TPU:32 now
where the time goes in v4:
time: 45.8 us; the launch traced here: 45.6 us
  starting transfers between devices  29 us (63%)
  Pallas kernels  9.88 us (22%)
  waiting for transfers between devices  6.67 us (15%)
    ppermute x8, starting transfers between devices, swap_sites(): return lax.ppermute(x, axes, pairs)  19.4 us
    ppermute x2, starting transfers between devices, from_next(): return lax.ppermute(x, axis, [((i + 1) % count, i) for i in range(count)])  8.17 us
    ppermute x8, waiting for transfers between devices, swap_sites(): return lax.ppermute(x, axes, pairs)  6.25 us
    pallas_call x2, Pallas kernels, prolong(): pl.pallas_call(functools.partial(prolong_kernel, t), in_specs=in_specs, o...  4.68 us
    pallas_call x1, Pallas kernels, restrict(): pl.pallas_call(restrict_kernel, in_specs=[HBM] * 6, out_specs=[VMEM] * le...  3.89 us
    ppermute x2, starting transfers between devices, from_previous(): return lax.ppermute(x, axis, [(i, (i + 1) % count) for i in range(count)])  1.48 us
    pallas_call x2, Pallas kernels, sweep(): pl.pallas_call(functools.partial(sweep_kernel, t), in_specs=[VMEM] * 8, o...  1.31 us
  transfers between devices with their start and end apart: 12, of which 5 were waited for; matrix products, arithmetic and copies ran while one was open for 0% of the time, Pallas kernels for 8%

profile of v4, /device:TPU:32, one launch (start us, length us, event | category | flops | bytes accessed | tf_op | source)
XLA Modules:
  0.0 45.6 jit_solution(10237895800806437695)
XLA Ops:
  0.0 3.9 %restrict.1 = (bf16[2,256,128]{2,1,0:T(8,128)(2,1)S(1)}, bf16[2,256,128]{2,1,0:T(8,128)(2,1)S(1)}, bf16[2,256,128]{2,1,0:T(8,128)(2,1)S(1)}, bf16[2,256,128]{2,1...) custom-call(s32[2,2]{1,0:T(2,128)} %refs_9_.3, ...), custom_call_target="tpu_custom_call" | custom-call | flops 570425344 | bytes 7471104 | tf_op jit(solution)/shard_map/restrict/pallas_call | solution.py:111
  3.9 0.1 collective-permute-start.3
  4.0 7.9 %collective-permute-start.5 = (bf16[2,256,128]{2,1,0:T(8,128)(2,1)S(1)}, bf16[2,256,128]{2,1,0:T(8,128)(2,1)S(1)}, u32[]{:S(2)}, u32[]{:S(2)}) collective-permute-start(bf16[2,256,128]{2,1,0:T(8,128)(2,1)S(1)} %get-tuple-element.15.refs_3_.refs_1_), channel_id=1, source_target_pairs={{0,15},{1,2},{2,1},{3,4},{4,3},{5,6},{6,5},{7,8},{8,7},{9,10},{10,... | collective-permute-start | bytes 393224 | tf_op jit(solution)/shard_map/ppermute | solution.py:239
  11.9 0.0 collective-permute-start.4
  11.9 2.0 %collective-permute-start.2 = (bf16[2,256,128]{2,1,0:T(8,128)(2,1)S(1)}, bf16[2,256,128]{2,1,0:T(8,128)(2,1)S(1)}, u32[]{:S(2)}, u32[]{:S(2)}) collective-permute-start(bf16[2,256,128]{2,1,0:T(8,128)(2,1)S(1)} %get-tuple-element.14.refs_1_.refs_2_), channel_id=1, source_target_pairs={{0,15},{1,2},{2,1},{3,4},{4,3},{5,6},{6,5},{7,8},{8,7},{9,10},{10,... | collective-permute-start | bytes 393224 | tf_op jit(solution)/shard_map/ppermute | solution.py:239
  13.9 0.9 %collective-permute-start.1 = (bf16[2,256,128]{2,1,0:T(8,128)(2,1)S(1)}, bf16[2,256,128]{2,1,0:T(8,128)(2,1)S(1)}, u32[]{:S(2)}, u32[]{:S(2)}) collective-permute-start(bf16[2,256,128]{2,1,0:T(8,128)(2,1)S(1)} %get-tuple-element.14.refs_1_.refs_2_), channel_id=1, source_target_pairs={{0,1},{1,0},{2,3},{3,2},{4,5},{5,4},{6,7},{7,6},{8,9},{9,8},{10,11... | collective-permute-start | bytes 393224 | tf_op jit(solution)/shard_map/ppermute | solution.py:239
  14.9 0.0 collective-permute-done.3.refs_3_
  14.9 2.9 %collective-permute-start = (bf16[2,256,128]{2,1,0:T(8,128)(2,1)S(1)}, bf16[2,256,128]{2,1,0:T(8,128)(2,1)S(1)}, u32[]{:S(2)}, u32[]{:S(2)}) collective-permute-start(bf16[2,256,128]{2,1,0:T(8,128)(2,1)S(1)} %get-tuple-element.15.refs_3_.refs_1_), channel_id=1, source_target_pairs={{16,0},{32,16},{48,32},{64,48},{80,64},{96,80},{112,96},{128,112},... | collective-permute-start | bytes 393224 | tf_op jit(solution)/shard_map/ppermute | solution.py:226
  17.8 0.8 %collective-permute-done.5.refs_5_ = bf16[2,256,128]{2,1,0:T(8,128)(2,1)S(1)} collective-permute-done((bf16[2,256,128]{2,1,0:T(8,128)(2,1)S(1)}, bf16[2,256,128]{2,1,0:T(8,128)(2,1)S(1)}, u32[]{:S(2)}, u32[]{:S(2)}) %collective-permute-start.5) | collective-permute-done | bytes 131104 | tf_op jit(solution)/shard_map/ppermute | solution.py:239
  18.5 0.6 %collective-permute-done.4.refs_4_ = bf16[2,256,128]{2,1,0:T(8,128)(2,1)S(1)} collective-permute-done((bf16[2,256,128]{2,1,0:T(8,128)(2,1)S(1)}, bf16[2,256,128]{2,1,0:T(8,128)(2,1)S(1)}, u32[]{:S(2)}, u32[]{:S(2)}) %collective-permute-start.4) | collective-permute-done | bytes 131104 | tf_op jit(solution)/shard_map/ppermute | solution.py:239
  19.2 0.7 %sweep.3.refs_1_.refs_3_ = bf16[2,256,128]{2,1,0:T(8,128)(2,1)S(1)} custom-call(bf16[2,256,128]{2,1,0:T(8,128)(2,1)S(1)} %get-tuple-element.18.refs_0_, bf16[2,256,128]{2,1,0:T(8,128)(2,1)S(1)} %get-tuple-element.15.refs_3_.refs_1_, bf16[2,256,128]{2,1,0:T(8,128)(2,1)S(1)} %get-tuple-element.14.refs_1_.refs_2_, ...), custom_call_target="tpu_custom_call" | custom-call | flops 150994944 | bytes 1507328 | tf_op jit(solution)/shard_map/sweep/pallas_call | solution.py:153
  19.8 3.5 %collective-permute-start.11 = (bf16[2,256,128]{2,1,0:T(8,128)(2,1)S(1)}, bf16[2,256,128]{2,1,0:T(8,128)(2,1)S(1)}, u32[]{:S(2)}, u32[]{:S(2)}) collective-permute-start(bf16[2,256,128]{2,1,0:T(8,128)(2,1)S(1)} %sweep.3.refs_1_.refs_3_), channel_id=1, source_target_pairs={{0,15},{1,2},{2,1},{3,4},{4,3},{5,6},{6,5},{7,8},{8,7},{9,10},{10,... | collective-permute-start | bytes 393224 | tf_op jit(solution)/shard_map/ppermute | solution.py:239
  23.3 0.5 %collective-permute-start.10 = (bf16[2,256,128]{2,1,0:T(8,128)(2,1)S(1)}, bf16[2,256,128]{2,1,0:T(8,128)(2,1)S(1)}, u32[]{:S(2)}, u32[]{:S(2)}) collective-permute-start(bf16[2,256,128]{2,1,0:T(8,128)(2,1)S(1)} %sweep.3.refs_1_.refs_3_), channel_id=1, source_target_pairs={{0,1},{1,0},{2,3},{3,2},{4,5},{5,4},{6,7},{7,6},{8,9},{9,8},{10,11... | collective-permute-start | bytes 393224 | tf_op jit(solution)/shard_map/ppermute | solution.py:239
  23.8 0.0 collective-permute-done.2.refs_5_
  23.9 1.0 %collective-permute-done.1.refs_4_ = bf16[2,256,128]{2,1,0:T(8,128)(2,1)S(1)} collective-permute-done((bf16[2,256,128]{2,1,0:T(8,128)(2,1)S(1)}, bf16[2,256,128]{2,1,0:T(8,128)(2,1)S(1)}, u32[]{:S(2)}, u32[]{:S(2)}) %collective-permute-start.1) | collective-permute-done | bytes 131104 | tf_op jit(solution)/shard_map/ppermute | solution.py:239
  24.8 0.4 collective-permute-done.refs_2_
  25.3 0.7 %sweep.2.refs_2_.refs_1_ = bf16[2,256,128]{2,1,0:T(8,128)(2,1)S(1)} custom-call(bf16[2,256,128]{2,1,0:T(8,128)(2,1)S(1)} %get-tuple-element.13.refs_0_, bf16[2,256,128]{2,1,0:T(8,128)(2,1)S(1)} %get-tuple-element.14.refs_1_.refs_2_, bf16[2,256,128]{2,1,0:T(8,128)(2,1)S(1)} %collective-permute-done.refs_2_, ...), custom_call_target="tpu_custom_call" | custom-call | flops 150994944 | bytes 1507328 | tf_op jit(solution)/shard_map/sweep/pallas_call | solution.py:153
  25.9 1.4 %collective-permute-start.9 = (bf16[2,256,128]{2,1,0:T(8,128)(2,1)S(1)}, bf16[2,256,128]{2,1,0:T(8,128)(2,1)S(1)}, u32[]{:S(2)}, u32[]{:S(2)}) collective-permute-start(bf16[2,256,128]{2,1,0:T(8,128)(2,1)S(1)} %sweep.2.refs_2_.refs_1_), channel_id=1, source_target_pairs={{0,16},{16,32},{32,48},{48,64},{64,80},{80,96},{96,112},{112,128},... | collective-permute-start | bytes 393224 | tf_op jit(solution)/shard_map/ppermute | solution.py:231
  27.3 5.3 %collective-permute-start.6 = (bf16[2,256,128]{2,1,0:T(8,128)(2,1)S(1)}, bf16[2,256,128]{2,1,0:T(8,128)(2,1)S(1)}, u32[]{:S(2)}, u32[]{:S(2)}) collective-permute-start(bf16[2,256,128]{2,1,0:T(8,128)(2,1)S(1)} %sweep.3.refs_1_.refs_3_), channel_id=1, source_target_pairs={{16,0},{32,16},{48,32},{64,48},{80,64},{96,80},{112,96},{128,112},... | collective-permute-start | bytes 393224 | tf_op jit(solution)/shard_map/ppermute | solution.py:226
  32.6 1.9 %collective-permute-start.8 = (bf16[2,256,128]{2,1,0:T(8,128)(2,1)S(1)}, bf16[2,256,128]{2,1,0:T(8,128)(2,1)S(1)}, u32[]{:S(2)}, u32[]{:S(2)}) collective-permute-start(bf16[2,256,128]{2,1,0:T(8,128)(2,1)S(1)} %sweep.2.refs_2_.refs_1_), channel_id=1, source_target_pairs={{0,15},{1,2},{2,1},{3,4},{4,3},{5,6},{6,5},{7,8},{8,7},{9,10},{10,... | collective-permute-start | bytes 393224 | tf_op jit(solution)/shard_map/ppermute | solution.py:239
  34.5 0.0 collective-permute-done.11.refs_5_
  34.5 2.6 %collective-permute-start.7 = (bf16[2,256,128]{2,1,0:T(8,128)(2,1)S(1)}, bf16[2,256,128]{2,1,0:T(8,128)(2,1)S(1)}, u32[]{:S(2)}, u32[]{:S(2)}) collective-permute-start(bf16[2,256,128]{2,1,0:T(8,128)(2,1)S(1)} %sweep.2.refs_2_.refs_1_), channel_id=1, source_target_pairs={{0,1},{1,0},{2,3},{3,2},{4,5},{5,4},{6,7},{7,6},{8,9},{9,8},{10,11... | collective-permute-start | bytes 393224 | tf_op jit(solution)/shard_map/ppermute | solution.py:239
  37.1 0.0 collective-permute-done.10.refs_4_
  37.1 0.0 collective-permute-done.9.refs_3_
  37.1 2.3 %prolong.2.refs_10_ = bf16[2,2,256,2048]{3,2,1,0:T(8,128)(2,1)} custom-call(bf16[2,256,128]{2,1,0:T(8,128)(2,1)S(1)} %get-tuple-element.18.refs_0_, bf16[2,256,128]{2,1,0:T(8,128)(2,1)S(1)} %sweep.3.refs_1_.refs_3_, bf16[2,256,128]{2,1,0:T(8,128)(2,1)S(1)} %sweep.2.refs_2_.refs_1_, bf16[2,256,128]{2,1,0:T(8,128)(2,1)S(1)} %collective-permute-done.9.refs_3_, ...), custom_call_target="tpu_custom_call" | custom-call | flops 419430400 | bytes 4521984 | tf_op jit(solution)/shard_map/prolong/pallas_call | solution.py:202
  39.4 0.0 collective-permute-done.6.refs_2_
  39.4 3.9 %collective-permute-done.8.refs_5_ = bf16[2,256,128]{2,1,0:T(8,128)(2,1)S(1)} collective-permute-done((bf16[2,256,128]{2,1,0:T(8,128)(2,1)S(1)}, bf16[2,256,128]{2,1,0:T(8,128)(2,1)S(1)}, u32[]{:S(2)}, u32[]{:S(2)}) %collective-permute-start.8) | collective-permute-done | bytes 131104 | tf_op jit(solution)/shard_map/ppermute | solution.py:239
  43.3 0.0 collective-permute-done.7.refs_4_
  43.3 2.3 %prolong.3 = bf16[2,2,256,2048]{3,2,1,0:T(8,128)(2,1)} custom-call(bf16[2,256,128]{2,1,0:T(8,128)(2,1)S(1)} %get-tuple-element.13.refs_0_, bf16[2,256,128]{2,1,0:T(8,128)(2,1)S(1)} %sweep.2.refs_2_.refs_1_, bf16[2,256,128]{2,1,0:T(8,128)(2,1)S(1)} %collective-permute-done.6.refs_2_, ...), custom_call_target="tpu_custom_call", output_to_operand_aliasing={{}: (10, {})} | custom-call | flops 419430400 | bytes 4521984 | tf_op jit(solution)/shard_map/prolong/pallas_call | solution.py:202
Async XLA Ops:
  3.9 11.0 %collective-permute-start.3 = (bf16[2,256,128]{2,1,0:T(8,128)(2,1)S(1)}, bf16[2,256,128]{2,1,0:T(8,128)(2,1)S(1)}, u32[]{:S(2)}, u32[]{:S(2)}) collective-permute-start(bf16[2,256,128]{2,1,0:T(8,128)(2,1)S(1)} %get-tuple-element.14.refs_1_.refs_2_), channel_id=1, source_target_pairs={{0,16},{16,32},{32,48},{48,64},{64,80},{80,96},{96,112},{112,128},... | collective-permute-start | bytes 393224 | tf_op jit(solution)/shard_map/ppermute | solution.py:231
  4.0 14.6 %collective-permute-start.5 = (bf16[2,256,128]{2,1,0:T(8,128)(2,1)S(1)}, bf16[2,256,128]{2,1,0:T(8,128)(2,1)S(1)}, u32[]{:S(2)}, u32[]{:S(2)}) collective-permute-start(bf16[2,256,128]{2,1,0:T(8,128)(2,1)S(1)} %get-tuple-element.15.refs_3_.refs_1_), channel_id=1, source_target_pairs={{0,15},{1,2},{2,1},{3,4},{4,3},{5,6},{6,5},{7,8},{8,7},{9,10},{10,... | collective-permute-start | bytes 393224 | tf_op jit(solution)/shard_map/ppermute | solution.py:239
  11.9 7.2 %collective-permute-start.4 = (bf16[2,256,128]{2,1,0:T(8,128)(2,1)S(1)}, bf16[2,256,128]{2,1,0:T(8,128)(2,1)S(1)}, u32[]{:S(2)}, u32[]{:S(2)}) collective-permute-start(bf16[2,256,128]{2,1,0:T(8,128)(2,1)S(1)} %get-tuple-element.15.refs_3_.refs_1_), channel_id=1, source_target_pairs={{0,1},{1,0},{2,3},{3,2},{4,5},{5,4},{6,7},{7,6},{8,9},{9,8},{10,11... | collective-permute-start | bytes 393224 | tf_op jit(solution)/shard_map/ppermute | solution.py:239
  11.9 11.9 %collective-permute-start.2 = (bf16[2,256,128]{2,1,0:T(8,128)(2,1)S(1)}, bf16[2,256,128]{2,1,0:T(8,128)(2,1)S(1)}, u32[]{:S(2)}, u32[]{:S(2)}) collective-permute-start(bf16[2,256,128]{2,1,0:T(8,128)(2,1)S(1)} %get-tuple-element.14.refs_1_.refs_2_), channel_id=1, source_target_pairs={{0,15},{1,2},{2,1},{3,4},{4,3},{5,6},{6,5},{7,8},{8,7},{9,10},{10,... | collective-permute-start | bytes 393224 | tf_op jit(solution)/shard_map/ppermute | solution.py:239
  13.9 10.9 %collective-permute-start.1 = (bf16[2,256,128]{2,1,0:T(8,128)(2,1)S(1)}, bf16[2,256,128]{2,1,0:T(8,128)(2,1)S(1)}, u32[]{:S(2)}, u32[]{:S(2)}) collective-permute-start(bf16[2,256,128]{2,1,0:T(8,128)(2,1)S(1)} %get-tuple-element.14.refs_1_.refs_2_), channel_id=1, source_target_pairs={{0,1},{1,0},{2,3},{3,2},{4,5},{5,4},{6,7},{7,6},{8,9},{9,8},{10,11... | collective-permute-start | bytes 393224 | tf_op jit(solution)/shard_map/ppermute | solution.py:239
  14.9 10.4 %collective-permute-start = (bf16[2,256,128]{2,1,0:T(8,128)(2,1)S(1)}, bf16[2,256,128]{2,1,0:T(8,128)(2,1)S(1)}, u32[]{:S(2)}, u32[]{:S(2)}) collective-permute-start(bf16[2,256,128]{2,1,0:T(8,128)(2,1)S(1)} %get-tuple-element.15.refs_3_.refs_1_), channel_id=1, source_target_pairs={{16,0},{32,16},{48,32},{64,48},{80,64},{96,80},{112,96},{128,112},... | collective-permute-start | bytes 393224 | tf_op jit(solution)/shard_map/ppermute | solution.py:226
  19.8 14.7 %collective-permute-start.11 = (bf16[2,256,128]{2,1,0:T(8,128)(2,1)S(1)}, bf16[2,256,128]{2,1,0:T(8,128)(2,1)S(1)}, u32[]{:S(2)}, u32[]{:S(2)}) collective-permute-start(bf16[2,256,128]{2,1,0:T(8,128)(2,1)S(1)} %sweep.3.refs_1_.refs_3_), channel_id=1, source_target_pairs={{0,15},{1,2},{2,1},{3,4},{4,3},{5,6},{6,5},{7,8},{8,7},{9,10},{10,... | collective-permute-start | bytes 393224 | tf_op jit(solution)/shard_map/ppermute | solution.py:239
  23.3 13.8 %collective-permute-start.10 = (bf16[2,256,128]{2,1,0:T(8,128)(2,1)S(1)}, bf16[2,256,128]{2,1,0:T(8,128)(2,1)S(1)}, u32[]{:S(2)}, u32[]{:S(2)}) collective-permute-start(bf16[2,256,128]{2,1,0:T(8,128)(2,1)S(1)} %sweep.3.refs_1_.refs_3_), channel_id=1, source_target_pairs={{0,1},{1,0},{2,3},{3,2},{4,5},{5,4},{6,7},{7,6},{8,9},{9,8},{10,11... | collective-permute-start | bytes 393224 | tf_op jit(solution)/shard_map/ppermute | solution.py:239
  25.9 11.2 %collective-permute-start.9 = (bf16[2,256,128]{2,1,0:T(8,128)(2,1)S(1)}, bf16[2,256,128]{2,1,0:T(8,128)(2,1)S(1)}, u32[]{:S(2)}, u32[]{:S(2)}) collective-permute-start(bf16[2,256,128]{2,1,0:T(8,128)(2,1)S(1)} %sweep.2.refs_2_.refs_1_), channel_id=1, source_target_pairs={{0,16},{16,32},{32,48},{48,64},{64,80},{80,96},{96,112},{112,128},... | collective-permute-start | bytes 393224 | tf_op jit(solution)/shard_map/ppermute | solution.py:231
  27.3 12.1 %collective-permute-start.6 = (bf16[2,256,128]{2,1,0:T(8,128)(2,1)S(1)}, bf16[2,256,128]{2,1,0:T(8,128)(2,1)S(1)}, u32[]{:S(2)}, u32[]{:S(2)}) collective-permute-start(bf16[2,256,128]{2,1,0:T(8,128)(2,1)S(1)} %sweep.3.refs_1_.refs_3_), channel_id=1, source_target_pairs={{16,0},{32,16},{48,32},{64,48},{80,64},{96,80},{112,96},{128,112},... | collective-permute-start | bytes 393224 | tf_op jit(solution)/shard_map/ppermute | solution.py:226
  32.6 10.7 %collective-permute-start.8 = (bf16[2,256,128]{2,1,0:T(8,128)(2,1)S(1)}, bf16[2,256,128]{2,1,0:T(8,128)(2,1)S(1)}, u32[]{:S(2)}, u32[]{:S(2)}) collective-permute-start(bf16[2,256,128]{2,1,0:T(8,128)(2,1)S(1)} %sweep.2.refs_2_.refs_1_), channel_id=1, source_target_pairs={{0,15},{1,2},{2,1},{3,4},{4,3},{5,6},{6,5},{7,8},{8,7},{9,10},{10,... | collective-permute-start | bytes 393224 | tf_op jit(solution)/shard_map/ppermute | solution.py:239
  34.5 8.8 %collective-permute-start.7 = (bf16[2,256,128]{2,1,0:T(8,128)(2,1)S(1)}, bf16[2,256,128]{2,1,0:T(8,128)(2,1)S(1)}, u32[]{:S(2)}, u32[]{:S(2)}) collective-permute-start(bf16[2,256,128]{2,1,0:T(8,128)(2,1)S(1)} %sweep.2.refs_2_.refs_1_), channel_id=1, source_target_pairs={{0,1},{1,0},{2,3},{3,2},{4,5},{5,4},{6,7},{7,6},{8,9},{9,8},{10,11... | collective-permute-start | bytes 393224 | tf_op jit(solution)/shard_map/ppermute | solution.py:239

commit v5 on v4

--- a/solution.py
+++ b/solution.py
@@ -66,6 +66,7 @@
     agg_in.wait()
     nbr_in.wait()
     lane = lax.axis_index("lat")
+    lane = lane + (lane < 2).astype(jnp.int32)
     hops_in = []
     for t in range(nt):
         for c in range(ns):
@@ -142,19 +143,22 @@
 
 
 def sweep_kernel(t, *refs):
-    hops, dinv, out = refs[6:]
+    hops, dinv = refs[6:8]
+    if len(refs) == 11:
+        refs[10][...] = refs[8][...]
+    out = refs[8 + (len(refs) == 11)]
     for c in range(out.shape[0]):
         out[c] = next_iterate(c, *refs[:6], hops, dinv.at[t])
 
 
-def sweep(t, coarse, hops, dinv):
+def sweep(t, coarse, hops, dinv, edge):
     shape = coarse[0].shape
     ns, n, nc = shape
     return pl.pallas_call(
         functools.partial(sweep_kernel, t),
-        in_specs=[VMEM] * 8,
-        out_specs=VMEM,
-        out_shape=pltpu.VMEM(shape, BF16),
+        in_specs=[VMEM] * (8 + len(edge)),
+        out_specs=[VMEM] * (1 + len(edge)),
+        out_shape=[pltpu.VMEM(shape, BF16)] * (1 + len(edge)),
         compiler_params=PARAMS,
         cost_estimate=pl.CostEstimate(
             flops=2 * ns * n * nc * 9 * nc,
@@ -162,7 +166,7 @@
             transcendentals=0,
         ),
         name="sweep",
-    )(*map(in_vmem, (*coarse, hops, dinv)))
+    )(*map(in_vmem, (*coarse, hops, dinv, *edge)))
 
 
 def prolong_kernel(t, *refs):
@@ -234,15 +238,15 @@
 def swap_sites(x, offset):
     axes = ("lat", "src")
     nt, count = (lax.axis_size(a) for a in axes)
-    step = lambda l, s: (s + 1 - 2 * ((l + s + offset) % 2)) % count
+    step = lambda l, s: (s + 1 - 2 * (((l + (l < 2)) + s + offset) % 2)) % count
     pairs = [(l * count + s, l * count + step(l, s)) for l in range(nt) for s in range(count)]
     return lax.ppermute(x, axes, pairs)
 
 
-def halos(e):
+def halos(e, first, last):
     spatial = [(swap_sites(x, 0), swap_sites(x, 1)) for x in e]
-    beyond = from_next(e[0], "lat")
-    before = from_previous(e[-1], "lat")
+    beyond = from_next(first, "lat")
+    before = from_previous(last, "lat")
     later = [*e[1:], beyond]
     earlier = [before, *e[:-1]]
     return [(e[t], later[t], earlier[t], *spatial[t]) for t in range(len(e))]
@@ -251,9 +255,13 @@
 def body(fine, basis, dinv, hops, nbr, agg):
     slices = range(fine.shape[0])
     rhs, e, basis, dinv, hops = restrict(agg, nbr.T, fine, basis, dinv, hops)
-    around = halos(e)
-    e = [sweep(t, (rhs[t], *around[t]), hops[t], dinv) for t in slices]
-    around = halos(e)
+    around = halos(e, e[0], e[-1])
+    e = []
+    for t in slices:
+        edge = (e[0],) if t == slices[-1] else ()
+        value, *edge = sweep(t, (rhs[t], *around[t]), hops[t], dinv, edge)
+        e.append(value)
+    around = halos(e, edge[0], e[-1])
     out = None
     for t in slices:
         out = prolong(t, fine.shape, agg, (rhs[t], *around[t]), hops[t], dinv, basis, out)

time: 45.8 us -> 45 us (0.983)
  starting transfers between devices: 29 us -> 22.4 us
  waiting for transfers between devices: 6.67 us -> 12.3 us
    ppermute x8, starting transfers between devices: 19.4 us -> 13.4 us  [swap_sites(): return lax.ppermute(x, axes, pairs)]
    ppermute x8, waiting for transfers between devices: 6.25 us -> 10.6 us  [swap_sites(): return lax.ppermute(x, axes, pairs)]
    ppermute x2, starting transfers between devices: 8.17 us -> 6.33 us  [from_next(): return lax.ppermute(x, axis, [((i + 1) % count, i) for i in range(count)])]
    ppermute x2, waiting for transfers between devices: 0.42 us -> 1.67 us  [from_next(): return lax.ppermute(x, axis, [((i + 1) % count, i) for i in range(count)])]
    ppermute x2, starting transfers between devices: 1.48 us -> 2.64 us  [from_previous(): return lax.ppermute(x, axis, [(i, (i + 1) % count) for i in range(count)])]
where the time goes in v5:
time: 45 us; the launch traced here: 44.6 us
  starting transfers between devices  22.4 us (50%)
  waiting for transfers between devices  12.3 us (27%)
  Pallas kernels  9.89 us (22%)
    ppermute x8, starting transfers between devices, swap_sites(): return lax.ppermute(x, axes, pairs)  13.4 us
    ppermute x8, waiting for transfers between devices, swap_sites(): return lax.ppermute(x, axes, pairs)  10.6 us
    ppermute x2, starting transfers between devices, from_next(): return lax.ppermute(x, axis, [((i + 1) % count, i) for i in range(count)])  6.33 us
    pallas_call x2, Pallas kernels, prolong(): pl.pallas_call(functools.partial(prolong_kernel, t), in_specs=in_specs, o...  4.67 us
    pallas_call x1, Pallas kernels, restrict(): pl.pallas_call(restrict_kernel, in_specs=[HBM] * 6, out_specs=[VMEM] * le...  3.89 us
    ppermute x2, starting transfers between devices, from_previous(): return lax.ppermute(x, axis, [(i, (i + 1) % count) for i in range(count)])  2.64 us
    ppermute x2, waiting for transfers between devices, from_next(): return lax.ppermute(x, axis, [((i + 1) % count, i) for i in range(count)])  1.67 us
    pallas_call x2, Pallas kernels, sweep(): pl.pallas_call(functools.partial(sweep_kernel, t), in_specs=[VMEM] * (8 +...  1.32 us
  transfers between devices with their start and end apart: 12, of which 5 were waited for; matrix products, arithmetic and copies ran while one was open for 0% of the time, Pallas kernels for 8%

profile of v5, /device:TPU:32, one launch (start us, length us, event | category | flops | bytes accessed | tf_op | source)
XLA Modules:
  0.0 44.6 jit_solution(5031055140081191826)
XLA Ops:
  0.0 3.9 %restrict.1 = (bf16[2,256,128]{2,1,0:T(8,128)(2,1)S(1)}, bf16[2,256,128]{2,1,0:T(8,128)(2,1)S(1)}, bf16[2,256,128]{2,1,0:T(8,128)(2,1)S(1)}, bf16[2,256,128]{2,1...) custom-call(s32[2,2]{1,0:T(2,128)} %refs_9_.3, ...), custom_call_target="tpu_custom_call" | custom-call | flops 570425344 | bytes 7471104 | tf_op jit(solution)/shard_map/restrict/pallas_call | solution.py:112
  3.9 0.1 collective-permute-start.3
  4.0 7.9 %collective-permute-start.5 = (bf16[2,256,128]{2,1,0:T(8,128)(2,1)S(1)}, bf16[2,256,128]{2,1,0:T(8,128)(2,1)S(1)}, u32[]{:S(2)}, u32[]{:S(2)}) collective-permute-start(bf16[2,256,128]{2,1,0:T(8,128)(2,1)S(1)} %get-tuple-element.17.refs_1_.refs_3_), channel_id=1, source_target_pairs={{0,1},{1,0},{2,3},{3,2},{4,5},{5,4},{6,7},{7,6},{8,9},{9,8},{10,11... | collective-permute-start | bytes 393224 | tf_op jit(solution)/shard_map/ppermute | solution.py:243
  11.9 0.0 collective-permute-start.4
  11.9 2.0 %collective-permute-start.2 = (bf16[2,256,128]{2,1,0:T(8,128)(2,1)S(1)}, bf16[2,256,128]{2,1,0:T(8,128)(2,1)S(1)}, u32[]{:S(2)}, u32[]{:S(2)}) collective-permute-start(bf16[2,256,128]{2,1,0:T(8,128)(2,1)S(1)} %get-tuple-element.16.refs_2_.refs_1_), channel_id=1, source_target_pairs={{0,1},{1,0},{2,3},{3,2},{4,5},{5,4},{6,7},{7,6},{8,9},{9,8},{10,11... | collective-permute-start | bytes 393224 | tf_op jit(solution)/shard_map/ppermute | solution.py:243
  13.9 0.9 %collective-permute-start.1 = (bf16[2,256,128]{2,1,0:T(8,128)(2,1)S(1)}, bf16[2,256,128]{2,1,0:T(8,128)(2,1)S(1)}, u32[]{:S(2)}, u32[]{:S(2)}) collective-permute-start(bf16[2,256,128]{2,1,0:T(8,128)(2,1)S(1)} %get-tuple-element.16.refs_2_.refs_1_), channel_id=1, source_target_pairs={{0,15},{1,2},{2,1},{3,4},{4,3},{5,6},{6,5},{7,8},{8,7},{9,10},{10,... | collective-permute-start | bytes 393224 | tf_op jit(solution)/shard_map/ppermute | solution.py:243
  14.9 0.0 collective-permute-done.3.refs_3_
  14.9 2.9 %collective-permute-start = (bf16[2,256,128]{2,1,0:T(8,128)(2,1)S(1)}, bf16[2,256,128]{2,1,0:T(8,128)(2,1)S(1)}, u32[]{:S(2)}, u32[]{:S(2)}) collective-permute-start(bf16[2,256,128]{2,1,0:T(8,128)(2,1)S(1)} %get-tuple-element.17.refs_1_.refs_3_), channel_id=1, source_target_pairs={{16,0},{32,16},{48,32},{64,48},{80,64},{96,80},{112,96},{128,112},... | collective-permute-start | bytes 393224 | tf_op jit(solution)/shard_map/ppermute | solution.py:230
  17.8 0.0 collective-permute-done.5.refs_5_
  17.8 5.7 %collective-permute-done.4.refs_4_ = bf16[2,256,128]{2,1,0:T(8,128)(2,1)S(1)} collective-permute-done((bf16[2,256,128]{2,1,0:T(8,128)(2,1)S(1)}, bf16[2,256,128]{2,1,0:T(8,128)(2,1)S(1)}, u32[]{:S(2)}, u32[]{:S(2)}) %collective-permute-start.4) | collective-permute-done | bytes 131104 | tf_op jit(solution)/shard_map/ppermute | solution.py:243
  23.5 0.7 %sweep.2.refs_8_.refs_1_.refs_3_ = bf16[2,256,128]{2,1,0:T(8,128)(2,1)S(1)} custom-call(bf16[2,256,128]{2,1,0:T(8,128)(2,1)S(1)} %get-tuple-element.20.refs_0_, bf16[2,256,128]{2,1,0:T(8,128)(2,1)S(1)} %get-tuple-element.17.refs_1_.refs_3_, bf16[2,256,128]{2,1,0:T(8,128)(2,1)S(1)} %get-tuple-element.16.refs_2_.refs_1_, ...), custom_call_target="tpu_custom_call" | custom-call | flops 150994944 | bytes 1507328 | tf_op jit(solution)/shard_map/sweep/pallas_call | solution.py:157
  24.1 0.1 collective-permute-start.11
  24.2 0.1 collective-permute-start.10
  24.3 0.0 collective-permute-done.2.refs_5_
  24.3 2.0 %collective-permute-done.1.refs_4_ = bf16[2,256,128]{2,1,0:T(8,128)(2,1)S(1)} collective-permute-done((bf16[2,256,128]{2,1,0:T(8,128)(2,1)S(1)}, bf16[2,256,128]{2,1,0:T(8,128)(2,1)S(1)}, u32[]{:S(2)}, u32[]{:S(2)}) %collective-permute-start.1) | collective-permute-done | bytes 131104 | tf_op jit(solution)/shard_map/ppermute | solution.py:243
  26.4 0.0 collective-permute-done.refs_2_
  26.4 0.7 %sweep.3 = (bf16[2,256,128]{2,1,0:T(8,128)(2,1)S(1)}, bf16[2,256,128]{2,1,0:T(8,128)(2,1)S(1)}) custom-call(bf16[2,256,128]{2,1,0:T(8,128)(2,1)S(1)} %get-tuple-element.15.refs_0_, bf16[2,256,128]{2,1,0:T(8,128)(2,1)S(1)} %get-tuple-element.16.refs_2_.refs_1_, bf16[2,256,128]{2,1,0:T(8,128)(2,1)S(1)} %collective-permute-done.refs_2_, ...), custom_call_target="tpu_custom_call" | custom-call | flops 150994944 | bytes 1507328 | tf_op jit(solution)/shard_map/sweep/pallas_call | solution.py:157
  27.0 2.6 %collective-permute-start.9 = (bf16[2,256,128]{2,1,0:T(8,128)(2,1)S(1)}, bf16[2,256,128]{2,1,0:T(8,128)(2,1)S(1)}, u32[]{:S(2)}, u32[]{:S(2)}) collective-permute-start(bf16[2,256,128]{2,1,0:T(8,128)(2,1)S(1)} %get-tuple-element.22.refs_2_.refs_1_), channel_id=1, source_target_pairs={{0,16},{16,32},{32,48},{48,64},{64,80},{80,96},{96,112},{112,128},... | collective-permute-start | bytes 393224 | tf_op jit(solution)/shard_map/ppermute | solution.py:235
  29.6 2.0 %collective-permute-start.8 = (bf16[2,256,128]{2,1,0:T(8,128)(2,1)S(1)}, bf16[2,256,128]{2,1,0:T(8,128)(2,1)S(1)}, u32[]{:S(2)}, u32[]{:S(2)}) collective-permute-start(bf16[2,256,128]{2,1,0:T(8,128)(2,1)S(1)} %get-tuple-element.22.refs_2_.refs_1_), channel_id=1, source_target_pairs={{0,1},{1,0},{2,3},{3,2},{4,5},{5,4},{6,7},{7,6},{8,9},{9,8},{10,11... | collective-permute-start | bytes 393224 | tf_op jit(solution)/shard_map/ppermute | solution.py:243
  31.6 3.4 %collective-permute-start.6 = (bf16[2,256,128]{2,1,0:T(8,128)(2,1)S(1)}, bf16[2,256,128]{2,1,0:T(8,128)(2,1)S(1)}, u32[]{:S(2)}, u32[]{:S(2)}) collective-permute-start(bf16[2,256,128]{2,1,0:T(8,128)(2,1)S(1)} %get-tuple-element.23), channel_id=1, source_target_pairs={{16,0},{32,16},{48,32},{64,48},{80,64},{96,80},{112,96},{128,112},... | collective-permute-start | bytes 393224 | tf_op jit(solution)/shard_map/ppermute | solution.py:230
  35.0 0.0 collective-permute-done.11.refs_5_
  35.0 0.4 collective-permute-start.7
  35.4 0.0 collective-permute-done.10.refs_4_
  35.4 0.0 collective-permute-done.9.refs_3_
  35.4 2.3 %prolong.2.refs_10_ = bf16[2,2,256,2048]{3,2,1,0:T(8,128)(2,1)} custom-call(bf16[2,256,128]{2,1,0:T(8,128)(2,1)S(1)} %get-tuple-element.20.refs_0_, bf16[2,256,128]{2,1,0:T(8,128)(2,1)S(1)} %sweep.2.refs_8_.refs_1_.refs_3_, bf16[2,256,128]{2,1,0:T(8,128)(2,1)S(1)} %get-tuple-element.22.refs_2_.refs_1_, ...), custom_call_target="tpu_custom_call" | custom-call | flops 419430400 | bytes 4521984 | tf_op jit(solution)/shard_map/prolong/pallas_call | solution.py:206
  37.7 1.7 %collective-permute-done.6.refs_2_ = bf16[2,256,128]{2,1,0:T(8,128)(2,1)S(1)} collective-permute-done((bf16[2,256,128]{2,1,0:T(8,128)(2,1)S(1)}, bf16[2,256,128]{2,1,0:T(8,128)(2,1)S(1)}, u32[]{:S(2)}, u32[]{:S(2)}) %collective-permute-start.6) | collective-permute-done | bytes 131104 | tf_op jit(solution)/shard_map/ppermute | solution.py:230
  39.4 0.6 %collective-permute-done.8.refs_5_ = bf16[2,256,128]{2,1,0:T(8,128)(2,1)S(1)} collective-permute-done((bf16[2,256,128]{2,1,0:T(8,128)(2,1)S(1)}, bf16[2,256,128]{2,1,0:T(8,128)(2,1)S(1)}, u32[]{:S(2)}, u32[]{:S(2)}) %collective-permute-start.8) | collective-permute-done | bytes 131104 | tf_op jit(solution)/shard_map/ppermute | solution.py:243
  40.0 2.3 %collective-permute-done.7.refs_4_ = bf16[2,256,128]{2,1,0:T(8,128)(2,1)S(1)} collective-permute-done((bf16[2,256,128]{2,1,0:T(8,128)(2,1)S(1)}, bf16[2,256,128]{2,1,0:T(8,128)(2,1)S(1)}, u32[]{:S(2)}, u32[]{:S(2)}) %collective-permute-start.7) | collective-permute-done | bytes 131104 | tf_op jit(solution)/shard_map/ppermute | solution.py:243
  42.3 2.3 %prolong.3 = bf16[2,2,256,2048]{3,2,1,0:T(8,128)(2,1)} custom-call(bf16[2,256,128]{2,1,0:T(8,128)(2,1)S(1)} %get-tuple-element.15.refs_0_, bf16[2,256,128]{2,1,0:T(8,128)(2,1)S(1)} %get-tuple-element.22.refs_2_.refs_1_, bf16[2,256,128]{2,1,0:T(8,128)(2,1)S(1)} %collective-permute-done.6.refs_2_, ...), custom_call_target="tpu_custom_call", output_to_operand_aliasing={{}: (10, {})} | custom-call | flops 419430400 | bytes 4521984 | tf_op jit(solution)/shard_map/prolong/pallas_call | solution.py:206
Async XLA Ops:
  3.9 11.0 %collective-permute-start.3 = (bf16[2,256,128]{2,1,0:T(8,128)(2,1)S(1)}, bf16[2,256,128]{2,1,0:T(8,128)(2,1)S(1)}, u32[]{:S(2)}, u32[]{:S(2)}) collective-permute-start(bf16[2,256,128]{2,1,0:T(8,128)(2,1)S(1)} %get-tuple-element.16.refs_2_.refs_1_), channel_id=1, source_target_pairs={{0,16},{16,32},{32,48},{48,64},{64,80},{80,96},{96,112},{112,128},... | collective-permute-start | bytes 393224 | tf_op jit(solution)/shard_map/ppermute | solution.py:235
  4.0 13.8 %collective-permute-start.5 = (bf16[2,256,128]{2,1,0:T(8,128)(2,1)S(1)}, bf16[2,256,128]{2,1,0:T(8,128)(2,1)S(1)}, u32[]{:S(2)}, u32[]{:S(2)}) collective-permute-start(bf16[2,256,128]{2,1,0:T(8,128)(2,1)S(1)} %get-tuple-element.17.refs_1_.refs_3_), channel_id=1, source_target_pairs={{0,1},{1,0},{2,3},{3,2},{4,5},{5,4},{6,7},{7,6},{8,9},{9,8},{10,11... | collective-permute-start | bytes 393224 | tf_op jit(solution)/shard_map/ppermute | solution.py:243
  11.9 11.5 %collective-permute-start.4 = (bf16[2,256,128]{2,1,0:T(8,128)(2,1)S(1)}, bf16[2,256,128]{2,1,0:T(8,128)(2,1)S(1)}, u32[]{:S(2)}, u32[]{:S(2)}) collective-permute-start(bf16[2,256,128]{2,1,0:T(8,128)(2,1)S(1)} %get-tuple-element.17.refs_1_.refs_3_), channel_id=1, source_target_pairs={{0,15},{1,2},{2,1},{3,4},{4,3},{5,6},{6,5},{7,8},{8,7},{9,10},{10,... | collective-permute-start | bytes 393224 | tf_op jit(solution)/shard_map/ppermute | solution.py:243
  11.9 12.4 %collective-permute-start.2 = (bf16[2,256,128]{2,1,0:T(8,128)(2,1)S(1)}, bf16[2,256,128]{2,1,0:T(8,128)(2,1)S(1)}, u32[]{:S(2)}, u32[]{:S(2)}) collective-permute-start(bf16[2,256,128]{2,1,0:T(8,128)(2,1)S(1)} %get-tuple-element.16.refs_2_.refs_1_), channel_id=1, source_target_pairs={{0,1},{1,0},{2,3},{3,2},{4,5},{5,4},{6,7},{7,6},{8,9},{9,8},{10,11... | collective-permute-start | bytes 393224 | tf_op jit(solution)/shard_map/ppermute | solution.py:243
  13.9 12.4 %collective-permute-start.1 = (bf16[2,256,128]{2,1,0:T(8,128)(2,1)S(1)}, bf16[2,256,128]{2,1,0:T(8,128)(2,1)S(1)}, u32[]{:S(2)}, u32[]{:S(2)}) collective-permute-start(bf16[2,256,128]{2,1,0:T(8,128)(2,1)S(1)} %get-tuple-element.16.refs_2_.refs_1_), channel_id=1, source_target_pairs={{0,15},{1,2},{2,1},{3,4},{4,3},{5,6},{6,5},{7,8},{8,7},{9,10},{10,... | collective-permute-start | bytes 393224 | tf_op jit(solution)/shard_map/ppermute | solution.py:243
  14.9 11.5 %collective-permute-start = (bf16[2,256,128]{2,1,0:T(8,128)(2,1)S(1)}, bf16[2,256,128]{2,1,0:T(8,128)(2,1)S(1)}, u32[]{:S(2)}, u32[]{:S(2)}) collective-permute-start(bf16[2,256,128]{2,1,0:T(8,128)(2,1)S(1)} %get-tuple-element.17.refs_1_.refs_3_), channel_id=1, source_target_pairs={{16,0},{32,16},{48,32},{64,48},{80,64},{96,80},{112,96},{128,112},... | collective-permute-start | bytes 393224 | tf_op jit(solution)/shard_map/ppermute | solution.py:230
  24.1 10.9 %collective-permute-start.11 = (bf16[2,256,128]{2,1,0:T(8,128)(2,1)S(1)}, bf16[2,256,128]{2,1,0:T(8,128)(2,1)S(1)}, u32[]{:S(2)}, u32[]{:S(2)}) collective-permute-start(bf16[2,256,128]{2,1,0:T(8,128)(2,1)S(1)} %sweep.2.refs_8_.refs_1_.refs_3_), channel_id=1, source_target_pairs={{0,1},{1,0},{2,3},{3,2},{4,5},{5,4},{6,7},{7,6},{8,9},{9,8},{10,11... | collective-permute-start | bytes 393224 | tf_op jit(solution)/shard_map/ppermute | solution.py:243
  24.2 11.2 %collective-permute-start.10 = (bf16[2,256,128]{2,1,0:T(8,128)(2,1)S(1)}, bf16[2,256,128]{2,1,0:T(8,128)(2,1)S(1)}, u32[]{:S(2)}, u32[]{:S(2)}) collective-permute-start(bf16[2,256,128]{2,1,0:T(8,128)(2,1)S(1)} %sweep.2.refs_8_.refs_1_.refs_3_), channel_id=1, source_target_pairs={{0,15},{1,2},{2,1},{3,4},{4,3},{5,6},{6,5},{7,8},{8,7},{9,10},{10,... | collective-permute-start | bytes 393224 | tf_op jit(solution)/shard_map/ppermute | solution.py:243
  27.0 8.3 %collective-permute-start.9 = (bf16[2,256,128]{2,1,0:T(8,128)(2,1)S(1)}, bf16[2,256,128]{2,1,0:T(8,128)(2,1)S(1)}, u32[]{:S(2)}, u32[]{:S(2)}) collective-permute-start(bf16[2,256,128]{2,1,0:T(8,128)(2,1)S(1)} %get-tuple-element.22.refs_2_.refs_1_), channel_id=1, source_target_pairs={{0,16},{16,32},{32,48},{48,64},{64,80},{80,96},{96,112},{112,128},... | collective-permute-start | bytes 393224 | tf_op jit(solution)/shard_map/ppermute | solution.py:235
  29.6 10.4 %collective-permute-start.8 = (bf16[2,256,128]{2,1,0:T(8,128)(2,1)S(1)}, bf16[2,256,128]{2,1,0:T(8,128)(2,1)S(1)}, u32[]{:S(2)}, u32[]{:S(2)}) collective-permute-start(bf16[2,256,128]{2,1,0:T(8,128)(2,1)S(1)} %get-tuple-element.22.refs_2_.refs_1_), channel_id=1, source_target_pairs={{0,1},{1,0},{2,3},{3,2},{4,5},{5,4},{6,7},{7,6},{8,9},{9,8},{10,11... | collective-permute-start | bytes 393224 | tf_op jit(solution)/shard_map/ppermute | solution.py:243
  31.6 7.8 %collective-permute-start.6 = (bf16[2,256,128]{2,1,0:T(8,128)(2,1)S(1)}, bf16[2,256,128]{2,1,0:T(8,128)(2,1)S(1)}, u32[]{:S(2)}, u32[]{:S(2)}) collective-permute-start(bf16[2,256,128]{2,1,0:T(8,128)(2,1)S(1)} %get-tuple-element.23), channel_id=1, source_target_pairs={{16,0},{32,16},{48,32},{64,48},{80,64},{96,80},{112,96},{128,112},... | collective-permute-start | bytes 393224 | tf_op jit(solution)/shard_map/ppermute | solution.py:230
  35.0 7.3 %collective-permute-start.7 = (bf16[2,256,128]{2,1,0:T(8,128)(2,1)S(1)}, bf16[2,256,128]{2,1,0:T(8,128)(2,1)S(1)}, u32[]{:S(2)}, u32[]{:S(2)}) collective-permute-start(bf16[2,256,128]{2,1,0:T(8,128)(2,1)S(1)} %get-tuple-element.22.refs_2_.refs_1_), channel_id=1, source_target_pairs={{0,15},{1,2},{2,1},{3,4},{4,3},{5,6},{6,5},{7,8},{8,7},{9,10},{10,... | collective-permute-start | bytes 393224 | tf_op jit(solution)/shard_map/ppermute | solution.py:243

commit v6 on v5

--- a/solution.py
+++ b/solution.py
@@ -176,18 +176,20 @@
     width = nf // PIECES
     copies = Copies(sems)
     agg_in = copies.start(agg, agg_s)
+    outs = []
     for c in range(ns):
-        value_v[c] = next_iterate(c, *refs[:6], hops, dinv.at[t])
-    agg_in.wait()
-    outs = []
-    for s in range(ns):
-        value = value_v[agg_s[t, s] & 1]
+        value = next_iterate(c, *refs[:6], hops, dinv.at[t])
+        if c == 0:
+            value_v[c] = value
+            agg_in.wait()
+            value = value_v[c]
+        s = (agg_s[t, 0] & 1) ^ c
         for p in range(PIECES):
             part = pl.ds(p * width, width)
-            out_v[s, :, part] = lax.dot_general(
+            out_v[c, :, part] = lax.dot_general(
                 value, basis[t, s, part], (((1,), (1,)), ((), ())), preferred_element_type=F32
             ).astype(BF16)
-            outs.append(copies.start(out_v.at[s, :, part], out.at[t, s, :, part]))
+            outs.append(copies.start(out_v.at[c, :, part], out.at[t, s, :, part]))
     for wait in outs:
         wait.wait()
 

time: 45 us -> 45.3 us (level)
  Pallas kernels: 9.89 us -> 10.4 us
    pallas_call x2, Pallas kernels: 4.67 us -> 5.23 us  [prolong(): pl.pallas_call(functools.partial(prolong_kernel, t), in_specs=in_specs, o...]
  transfers between devices with their start and end apart: 12 -> 12, of which waited for: 5 -> 5; matrix products, arithmetic and copies ran while one was open for 0% -> 0% of each run, Pallas kernels for 8% -> 9%
where the time goes in v6:
time: 45.3 us; the launch traced here: 44.9 us
  starting transfers between devices  22.4 us (49%)
  waiting for transfers between devices  12 us (26%)
  Pallas kernels  10.4 us (23%)
    ppermute x8, starting transfers between devices, swap_sites(): return lax.ppermute(x, axes, pairs)  13.4 us
    ppermute x8, waiting for transfers between devices, swap_sites(): return lax.ppermute(x, axes, pairs)  10.6 us
    ppermute x2, starting transfers between devices, from_next(): return lax.ppermute(x, axis, [((i + 1) % count, i) for i in range(count)])  6.33 us
    pallas_call x2, Pallas kernels, prolong(): pl.pallas_call(functools.partial(prolong_kernel, t), in_specs=in_specs, o...  5.23 us
    pallas_call x1, Pallas kernels, restrict(): pl.pallas_call(restrict_kernel, in_specs=[HBM] * 6, out_specs=[VMEM] * le...  3.89 us
    ppermute x2, starting transfers between devices, from_previous(): return lax.ppermute(x, axis, [(i, (i + 1) % count) for i in range(count)])  2.64 us
    ppermute x2, waiting for transfers between devices, from_next(): return lax.ppermute(x, axis, [((i + 1) % count, i) for i in range(count)])  1.4 us
    pallas_call x2, Pallas kernels, sweep(): pl.pallas_call(functools.partial(sweep_kernel, t), in_specs=[VMEM] * (8 +...  1.32 us
  transfers between devices with their start and end apart: 12, of which 5 were waited for; matrix products, arithmetic and copies ran while one was open for 0% of the time, Pallas kernels for 9%

profile of v6, /device:TPU:32, one launch (start us, length us, event | category | flops | bytes accessed | tf_op | source)
XLA Modules:
  0.0 44.9 jit_solution(13610300168314692106)
XLA Ops:
  0.0 3.9 %restrict.1 = (bf16[2,256,128]{2,1,0:T(8,128)(2,1)S(1)}, bf16[2,256,128]{2,1,0:T(8,128)(2,1)S(1)}, bf16[2,256,128]{2,1,0:T(8,128)(2,1)S(1)}, bf16[2,256,128]{2,1...) custom-call(s32[2,2]{1,0:T(2,128)} %refs_9_.3, ...), custom_call_target="tpu_custom_call" | custom-call | flops 570425344 | bytes 7471104 | tf_op jit(solution)/shard_map/restrict/pallas_call | solution.py:112
  3.9 0.1 collective-permute-start.3
  4.0 7.9 %collective-permute-start.5 = (bf16[2,256,128]{2,1,0:T(8,128)(2,1)S(1)}, bf16[2,256,128]{2,1,0:T(8,128)(2,1)S(1)}, u32[]{:S(2)}, u32[]{:S(2)}) collective-permute-start(bf16[2,256,128]{2,1,0:T(8,128)(2,1)S(1)} %get-tuple-element.17.refs_1_.refs_3_), channel_id=1, source_target_pairs={{0,1},{1,0},{2,3},{3,2},{4,5},{5,4},{6,7},{7,6},{8,9},{9,8},{10,11... | collective-permute-start | bytes 393224 | tf_op jit(solution)/shard_map/ppermute | solution.py:245
  11.9 0.0 collective-permute-start.4
  11.9 2.0 %collective-permute-start.2 = (bf16[2,256,128]{2,1,0:T(8,128)(2,1)S(1)}, bf16[2,256,128]{2,1,0:T(8,128)(2,1)S(1)}, u32[]{:S(2)}, u32[]{:S(2)}) collective-permute-start(bf16[2,256,128]{2,1,0:T(8,128)(2,1)S(1)} %get-tuple-element.16.refs_2_.refs_1_), channel_id=1, source_target_pairs={{0,1},{1,0},{2,3},{3,2},{4,5},{5,4},{6,7},{7,6},{8,9},{9,8},{10,11... | collective-permute-start | bytes 393224 | tf_op jit(solution)/shard_map/ppermute | solution.py:245
  13.9 0.9 %collective-permute-start.1 = (bf16[2,256,128]{2,1,0:T(8,128)(2,1)S(1)}, bf16[2,256,128]{2,1,0:T(8,128)(2,1)S(1)}, u32[]{:S(2)}, u32[]{:S(2)}) collective-permute-start(bf16[2,256,128]{2,1,0:T(8,128)(2,1)S(1)} %get-tuple-element.16.refs_2_.refs_1_), channel_id=1, source_target_pairs={{0,15},{1,2},{2,1},{3,4},{4,3},{5,6},{6,5},{7,8},{8,7},{9,10},{10,... | collective-permute-start | bytes 393224 | tf_op jit(solution)/shard_map/ppermute | solution.py:245
  14.9 0.0 collective-permute-done.3.refs_3_
  14.9 2.9 %collective-permute-start = (bf16[2,256,128]{2,1,0:T(8,128)(2,1)S(1)}, bf16[2,256,128]{2,1,0:T(8,128)(2,1)S(1)}, u32[]{:S(2)}, u32[]{:S(2)}) collective-permute-start(bf16[2,256,128]{2,1,0:T(8,128)(2,1)S(1)} %get-tuple-element.17.refs_1_.refs_3_), channel_id=1, source_target_pairs={{16,0},{32,16},{48,32},{64,48},{80,64},{96,80},{112,96},{128,112},... | collective-permute-start | bytes 393224 | tf_op jit(solution)/shard_map/ppermute | solution.py:232
  17.8 0.0 collective-permute-done.5.refs_5_
  17.8 5.7 %collective-permute-done.4.refs_4_ = bf16[2,256,128]{2,1,0:T(8,128)(2,1)S(1)} collective-permute-done((bf16[2,256,128]{2,1,0:T(8,128)(2,1)S(1)}, bf16[2,256,128]{2,1,0:T(8,128)(2,1)S(1)}, u32[]{:S(2)}, u32[]{:S(2)}) %collective-permute-start.4) | collective-permute-done | bytes 131104 | tf_op jit(solution)/shard_map/ppermute | solution.py:245
  23.5 0.7 %sweep.2.refs_8_.refs_1_.refs_3_ = bf16[2,256,128]{2,1,0:T(8,128)(2,1)S(1)} custom-call(bf16[2,256,128]{2,1,0:T(8,128)(2,1)S(1)} %get-tuple-element.20.refs_0_, bf16[2,256,128]{2,1,0:T(8,128)(2,1)S(1)} %get-tuple-element.17.refs_1_.refs_3_, bf16[2,256,128]{2,1,0:T(8,128)(2,1)S(1)} %get-tuple-element.16.refs_2_.refs_1_, ...), custom_call_target="tpu_custom_call" | custom-call | flops 150994944 | bytes 1507328 | tf_op jit(solution)/shard_map/sweep/pallas_call | solution.py:157
  24.1 0.1 collective-permute-start.11
  24.2 0.1 collective-permute-start.10
  24.3 0.0 collective-permute-done.2.refs_5_
  24.3 2.0 %collective-permute-done.1.refs_4_ = bf16[2,256,128]{2,1,0:T(8,128)(2,1)S(1)} collective-permute-done((bf16[2,256,128]{2,1,0:T(8,128)(2,1)S(1)}, bf16[2,256,128]{2,1,0:T(8,128)(2,1)S(1)}, u32[]{:S(2)}, u32[]{:S(2)}) %collective-permute-start.1) | collective-permute-done | bytes 131104 | tf_op jit(solution)/shard_map/ppermute | solution.py:245
  26.4 0.0 collective-permute-done.refs_2_
  26.4 0.7 %sweep.3 = (bf16[2,256,128]{2,1,0:T(8,128)(2,1)S(1)}, bf16[2,256,128]{2,1,0:T(8,128)(2,1)S(1)}) custom-call(bf16[2,256,128]{2,1,0:T(8,128)(2,1)S(1)} %get-tuple-element.15.refs_0_, bf16[2,256,128]{2,1,0:T(8,128)(2,1)S(1)} %get-tuple-element.16.refs_2_.refs_1_, bf16[2,256,128]{2,1,0:T(8,128)(2,1)S(1)} %collective-permute-done.refs_2_, ...), custom_call_target="tpu_custom_call" | custom-call | flops 150994944 | bytes 1507328 | tf_op jit(solution)/shard_map/sweep/pallas_call | solution.py:157
  27.0 2.6 %collective-permute-start.9 = (bf16[2,256,128]{2,1,0:T(8,128)(2,1)S(1)}, bf16[2,256,128]{2,1,0:T(8,128)(2,1)S(1)}, u32[]{:S(2)}, u32[]{:S(2)}) collective-permute-start(bf16[2,256,128]{2,1,0:T(8,128)(2,1)S(1)} %get-tuple-element.22.refs_2_.refs_1_), channel_id=1, source_target_pairs={{0,16},{16,32},{32,48},{48,64},{64,80},{80,96},{96,112},{112,128},... | collective-permute-start | bytes 393224 | tf_op jit(solution)/shard_map/ppermute | solution.py:237
  29.6 2.0 %collective-permute-start.8 = (bf16[2,256,128]{2,1,0:T(8,128)(2,1)S(1)}, bf16[2,256,128]{2,1,0:T(8,128)(2,1)S(1)}, u32[]{:S(2)}, u32[]{:S(2)}) collective-permute-start(bf16[2,256,128]{2,1,0:T(8,128)(2,1)S(1)} %get-tuple-element.22.refs_2_.refs_1_), channel_id=1, source_target_pairs={{0,1},{1,0},{2,3},{3,2},{4,5},{5,4},{6,7},{7,6},{8,9},{9,8},{10,11... | collective-permute-start | bytes 393224 | tf_op jit(solution)/shard_map/ppermute | solution.py:245
  31.6 3.4 %collective-permute-start.6 = (bf16[2,256,128]{2,1,0:T(8,128)(2,1)S(1)}, bf16[2,256,128]{2,1,0:T(8,128)(2,1)S(1)}, u32[]{:S(2)}, u32[]{:S(2)}) collective-permute-start(bf16[2,256,128]{2,1,0:T(8,128)(2,1)S(1)} %get-tuple-element.23), channel_id=1, source_target_pairs={{16,0},{32,16},{48,32},{64,48},{80,64},{96,80},{112,96},{128,112},... | collective-permute-start | bytes 393224 | tf_op jit(solution)/shard_map/ppermute | solution.py:232
  35.0 0.0 collective-permute-done.11.refs_5_
  35.0 0.4 collective-permute-start.7
  35.4 0.0 collective-permute-done.10.refs_4_
  35.4 0.0 collective-permute-done.9.refs_3_
  35.4 2.6 %prolong.2.refs_10_ = bf16[2,2,256,2048]{3,2,1,0:T(8,128)(2,1)} custom-call(bf16[2,256,128]{2,1,0:T(8,128)(2,1)S(1)} %get-tuple-element.20.refs_0_, bf16[2,256,128]{2,1,0:T(8,128)(2,1)S(1)} %sweep.2.refs_8_.refs_1_.refs_3_, bf16[2,256,128]{2,1,0:T(8,128)(2,1)S(1)} %get-tuple-element.22.refs_2_.refs_1_, ...), custom_call_target="tpu_custom_call" | custom-call | flops 419430400 | bytes 4521984 | tf_op jit(solution)/shard_map/prolong/pallas_call | solution.py:208
  38.0 1.4 %collective-permute-done.6.refs_2_ = bf16[2,256,128]{2,1,0:T(8,128)(2,1)S(1)} collective-permute-done((bf16[2,256,128]{2,1,0:T(8,128)(2,1)S(1)}, bf16[2,256,128]{2,1,0:T(8,128)(2,1)S(1)}, u32[]{:S(2)}, u32[]{:S(2)}) %collective-permute-start.6) | collective-permute-done | bytes 131104 | tf_op jit(solution)/shard_map/ppermute | solution.py:232
  39.4 0.6 %collective-permute-done.8.refs_5_ = bf16[2,256,128]{2,1,0:T(8,128)(2,1)S(1)} collective-permute-done((bf16[2,256,128]{2,1,0:T(8,128)(2,1)S(1)}, bf16[2,256,128]{2,1,0:T(8,128)(2,1)S(1)}, u32[]{:S(2)}, u32[]{:S(2)}) %collective-permute-start.8) | collective-permute-done | bytes 131104 | tf_op jit(solution)/shard_map/ppermute | solution.py:245
  40.0 2.3 %collective-permute-done.7.refs_4_ = bf16[2,256,128]{2,1,0:T(8,128)(2,1)S(1)} collective-permute-done((bf16[2,256,128]{2,1,0:T(8,128)(2,1)S(1)}, bf16[2,256,128]{2,1,0:T(8,128)(2,1)S(1)}, u32[]{:S(2)}, u32[]{:S(2)}) %collective-permute-start.7) | collective-permute-done | bytes 131104 | tf_op jit(solution)/shard_map/ppermute | solution.py:245
  42.3 2.6 %prolong.3 = bf16[2,2,256,2048]{3,2,1,0:T(8,128)(2,1)} custom-call(bf16[2,256,128]{2,1,0:T(8,128)(2,1)S(1)} %get-tuple-element.15.refs_0_, bf16[2,256,128]{2,1,0:T(8,128)(2,1)S(1)} %get-tuple-element.22.refs_2_.refs_1_, bf16[2,256,128]{2,1,0:T(8,128)(2,1)S(1)} %collective-permute-done.6.refs_2_, ...), custom_call_target="tpu_custom_call", output_to_operand_aliasing={{}: (10, {})} | custom-call | flops 419430400 | bytes 4521984 | tf_op jit(solution)/shard_map/prolong/pallas_call | solution.py:208
Async XLA Ops:
  3.9 11.0 %collective-permute-start.3 = (bf16[2,256,128]{2,1,0:T(8,128)(2,1)S(1)}, bf16[2,256,128]{2,1,0:T(8,128)(2,1)S(1)}, u32[]{:S(2)}, u32[]{:S(2)}) collective-permute-start(bf16[2,256,128]{2,1,0:T(8,128)(2,1)S(1)} %get-tuple-element.16.refs_2_.refs_1_), channel_id=1, source_target_pairs={{0,16},{16,32},{32,48},{48,64},{64,80},{80,96},{96,112},{112,128},... | collective-permute-start | bytes 393224 | tf_op jit(solution)/shard_map/ppermute | solution.py:237
  4.0 13.8 %collective-permute-start.5 = (bf16[2,256,128]{2,1,0:T(8,128)(2,1)S(1)}, bf16[2,256,128]{2,1,0:T(8,128)(2,1)S(1)}, u32[]{:S(2)}, u32[]{:S(2)}) collective-permute-start(bf16[2,256,128]{2,1,0:T(8,128)(2,1)S(1)} %get-tuple-element.17.refs_1_.refs_3_), channel_id=1, source_target_pairs={{0,1},{1,0},{2,3},{3,2},{4,5},{5,4},{6,7},{7,6},{8,9},{9,8},{10,11... | collective-permute-start | bytes 393224 | tf_op jit(solution)/shard_map/ppermute | solution.py:245
  11.9 11.5 %collective-permute-start.4 = (bf16[2,256,128]{2,1,0:T(8,128)(2,1)S(1)}, bf16[2,256,128]{2,1,0:T(8,128)(2,1)S(1)}, u32[]{:S(2)}, u32[]{:S(2)}) collective-permute-start(bf16[2,256,128]{2,1,0:T(8,128)(2,1)S(1)} %get-tuple-element.17.refs_1_.refs_3_), channel_id=1, source_target_pairs={{0,15},{1,2},{2,1},{3,4},{4,3},{5,6},{6,5},{7,8},{8,7},{9,10},{10,... | collective-permute-start | bytes 393224 | tf_op jit(solution)/shard_map/ppermute | solution.py:245
  11.9 12.4 %collective-permute-start.2 = (bf16[2,256,128]{2,1,0:T(8,128)(2,1)S(1)}, bf16[2,256,128]{2,1,0:T(8,128)(2,1)S(1)}, u32[]{:S(2)}, u32[]{:S(2)}) collective-permute-start(bf16[2,256,128]{2,1,0:T(8,128)(2,1)S(1)} %get-tuple-element.16.refs_2_.refs_1_), channel_id=1, source_target_pairs={{0,1},{1,0},{2,3},{3,2},{4,5},{5,4},{6,7},{7,6},{8,9},{9,8},{10,11... | collective-permute-start | bytes 393224 | tf_op jit(solution)/shard_map/ppermute | solution.py:245
  13.9 12.4 %collective-permute-start.1 = (bf16[2,256,128]{2,1,0:T(8,128)(2,1)S(1)}, bf16[2,256,128]{2,1,0:T(8,128)(2,1)S(1)}, u32[]{:S(2)}, u32[]{:S(2)}) collective-permute-start(bf16[2,256,128]{2,1,0:T(8,128)(2,1)S(1)} %get-tuple-element.16.refs_2_.refs_1_), channel_id=1, source_target_pairs={{0,15},{1,2},{2,1},{3,4},{4,3},{5,6},{6,5},{7,8},{8,7},{9,10},{10,... | collective-permute-start | bytes 393224 | tf_op jit(solution)/shard_map/ppermute | solution.py:245
  14.9 11.5 %collective-permute-start = (bf16[2,256,128]{2,1,0:T(8,128)(2,1)S(1)}, bf16[2,256,128]{2,1,0:T(8,128)(2,1)S(1)}, u32[]{:S(2)}, u32[]{:S(2)}) collective-permute-start(bf16[2,256,128]{2,1,0:T(8,128)(2,1)S(1)} %get-tuple-element.17.refs_1_.refs_3_), channel_id=1, source_target_pairs={{16,0},{32,16},{48,32},{64,48},{80,64},{96,80},{112,96},{128,112},... | collective-permute-start | bytes 393224 | tf_op jit(solution)/shard_map/ppermute | solution.py:232
  24.1 10.9 %collective-permute-start.11 = (bf16[2,256,128]{2,1,0:T(8,128)(2,1)S(1)}, bf16[2,256,128]{2,1,0:T(8,128)(2,1)S(1)}, u32[]{:S(2)}, u32[]{:S(2)}) collective-permute-start(bf16[2,256,128]{2,1,0:T(8,128)(2,1)S(1)} %sweep.2.refs_8_.refs_1_.refs_3_), channel_id=1, source_target_pairs={{0,1},{1,0},{2,3},{3,2},{4,5},{5,4},{6,7},{7,6},{8,9},{9,8},{10,11... | collective-permute-start | bytes 393224 | tf_op jit(solution)/shard_map/ppermute | solution.py:245
  24.2 11.2 %collective-permute-start.10 = (bf16[2,256,128]{2,1,0:T(8,128)(2,1)S(1)}, bf16[2,256,128]{2,1,0:T(8,128)(2,1)S(1)}, u32[]{:S(2)}, u32[]{:S(2)}) collective-permute-start(bf16[2,256,128]{2,1,0:T(8,128)(2,1)S(1)} %sweep.2.refs_8_.refs_1_.refs_3_), channel_id=1, source_target_pairs={{0,15},{1,2},{2,1},{3,4},{4,3},{5,6},{6,5},{7,8},{8,7},{9,10},{10,... | collective-permute-start | bytes 393224 | tf_op jit(solution)/shard_map/ppermute | solution.py:245
  27.0 8.3 %collective-permute-start.9 = (bf16[2,256,128]{2,1,0:T(8,128)(2,1)S(1)}, bf16[2,256,128]{2,1,0:T(8,128)(2,1)S(1)}, u32[]{:S(2)}, u32[]{:S(2)}) collective-permute-start(bf16[2,256,128]{2,1,0:T(8,128)(2,1)S(1)} %get-tuple-element.22.refs_2_.refs_1_), channel_id=1, source_target_pairs={{0,16},{16,32},{32,48},{48,64},{64,80},{80,96},{96,112},{112,128},... | collective-permute-start | bytes 393224 | tf_op jit(solution)/shard_map/ppermute | solution.py:237
  29.6 10.4 %collective-permute-start.8 = (bf16[2,256,128]{2,1,0:T(8,128)(2,1)S(1)}, bf16[2,256,128]{2,1,0:T(8,128)(2,1)S(1)}, u32[]{:S(2)}, u32[]{:S(2)}) collective-permute-start(bf16[2,256,128]{2,1,0:T(8,128)(2,1)S(1)} %get-tuple-element.22.refs_2_.refs_1_), channel_id=1, source_target_pairs={{0,1},{1,0},{2,3},{3,2},{4,5},{5,4},{6,7},{7,6},{8,9},{9,8},{10,11... | collective-permute-start | bytes 393224 | tf_op jit(solution)/shard_map/ppermute | solution.py:245
  31.6 7.8 %collective-permute-start.6 = (bf16[2,256,128]{2,1,0:T(8,128)(2,1)S(1)}, bf16[2,256,128]{2,1,0:T(8,128)(2,1)S(1)}, u32[]{:S(2)}, u32[]{:S(2)}) collective-permute-start(bf16[2,256,128]{2,1,0:T(8,128)(2,1)S(1)} %get-tuple-element.23), channel_id=1, source_target_pairs={{16,0},{32,16},{48,32},{64,48},{80,64},{96,80},{112,96},{128,112},... | collective-permute-start | bytes 393224 | tf_op jit(solution)/shard_map/ppermute | solution.py:232
  35.0 7.3 %collective-permute-start.7 = (bf16[2,256,128]{2,1,0:T(8,128)(2,1)S(1)}, bf16[2,256,128]{2,1,0:T(8,128)(2,1)S(1)}, u32[]{:S(2)}, u32[]{:S(2)}) collective-permute-start(bf16[2,256,128]{2,1,0:T(8,128)(2,1)S(1)} %get-tuple-element.22.refs_2_.refs_1_), channel_id=1, source_target_pairs={{0,15},{1,2},{2,1},{3,4},{4,3},{5,6},{6,5},{7,8},{8,7},{9,10},{10,... | collective-permute-start | bytes 393224 | tf_op jit(solution)/shard_map/ppermute | solution.py:245
